TPU v7x, 128 devices: a whole 4x4x4 slice. The times are simulated.
128 devices in a mesh: row: 4 (over z), col: 32 (over x, y, core).
Axes of the slice: x: 4, y: 4, z: 4, core: 2. Of those that a mesh axis runs over, the one named last changes fastest.
Arguments:
- embeddings: bfloat16 [65536, 256], P(('row', 'col')), may hold values from -6 to 6
- partition_source: int32 [65536], P(('row', 'col')), may hold values from 0 to 65535, as said below
- hash_target: int32 [65536], P(('row', 'col')), may hold values from 0 to 65535, as said below
- tile_values: bfloat16 [12288, 128, 128], P(('row', 'col')), may hold values from -0.109375 to 0.109375
- tile_row: int32 [12288], P(('row', 'col')), may hold values from 0 to 3
- tile_owner: int32 [12288, 1], P(('row', 'col')), may hold values from 0 to 31; in each aligned block of 96 rows (0 to 95, 96 to 191, ...) at most 4 rows name the same one
- tile_sub: int32 [12288], P(('row', 'col')), may hold values from 0 to 3
- tile_count: int32 [128], P(('row', 'col')), may hold values from 1 to 96, as said below
- cotangent: bfloat16 [65536, 256], P(('row', 'col')), may hold values from -6 to 6
Outputs:
- propagated: bfloat16 [65536, 256], P(('row', 'col'))
- embed_grad: bfloat16 [65536, 256], P(('row', 'col'))
Inputs may be any that keep to these rules, and one draw needn't show every extreme that they name: `partition_source`: A permutation of the nodes; for every two devices, exactly 4 of the first device's hash rows are named at the second device's partition rows. `hash_target`: the inverse of partition_source. `tile_count`: some device uses all 96 slots in every draw. `tile_owner`: among the 96 slots of one device no value is named by more than 4 slots.
All inputs are finite; a program needn't handle non-finite values.
Results may differ from a plain program's by a relative error of at most 0.017.
Values may be sent and summed in bfloat16 or wider, within the bound.
No kernel may reach another device: no remote copies, remote signals or barrier semaphores. Data moves between devices by JAX's collectives and lax.ppermute only.
A program may use at most 192 MiB of HBM per device.

v0:
```python
import jax
import jax.numpy as jnp
from jax import lax
from jax.sharding import PartitionSpec as P

PRECISE = lax.Precision.HIGHEST


def reshuffle(payload, row_count, col_count):
    peer_rows = payload.shape[0] // (row_count * col_count)
    direct = payload.reshape(row_count * col_count, peer_rows, payload.shape[1])
    moved = lax.all_to_all(direct, ("row", "col"), split_axis=0, concat_axis=0, tiled=True)
    return moved.reshape(payload.shape)


def spread(features, tile_values, tile_row, columns, live_slots):
    tile_size = tile_values.shape[1]
    feat_width = features.shape[1]
    blocks_dev = features.shape[0] // tile_size
    group_rows = lax.all_gather(features, "col", axis=0, tiled=True)
    chosen = group_rows.reshape(-1, tile_size, feat_width)[columns]
    products = jnp.einsum("sij,sjw->siw", tile_values, chosen, preferred_element_type=jnp.float32)
    selector = (tile_row[None, :] == jnp.arange(blocks_dev)[:, None]).astype(
        jnp.float32
    ) * live_slots[None, :]
    summed = jnp.einsum("bs,siw->biw", selector, products, precision=PRECISE)
    return summed.reshape(features.shape[0], feat_width)


def transpose_partials(gradient, tile_values, tile_row, columns, live_slots, col_count):
    tile_size = tile_values.shape[1]
    feat_width = gradient.shape[1]
    blocks_dev = gradient.shape[0] // tile_size
    chosen = gradient.reshape(blocks_dev, tile_size, feat_width)[tile_row]
    products = jnp.einsum("sij,siw->sjw", tile_values, chosen, preferred_element_type=jnp.float32)
    products = products * live_slots[:, None, None]
    partial_sum = jax.ops.segment_sum(products, columns, num_segments=blocks_dev * col_count)
    return lax.psum_scatter(
        partial_sum.reshape(-1, feat_width).astype(jnp.bfloat16),
        "col",
        scatter_dimension=0,
        tiled=True,
    ).astype(jnp.float32)


def shards(
    embeddings,
    partition_source,
    hash_target,
    tile_values,
    tile_row,
    tile_owner,
    tile_sub,
    tile_count,
    cotangent,
):
    row_count = lax.axis_size("row")
    col_count = lax.axis_size("col")
    nodes_dev = embeddings.shape[0]
    tile_size = tile_values.shape[1]
    blocks_dev = nodes_dev // tile_size
    slot_total = tile_values.shape[0]
    live_slots = (jnp.arange(slot_total) < tile_count[0]).astype(jnp.float32)
    owners = tile_owner[:, 0]
    columns = owners * blocks_dev + tile_sub
    send_order = jnp.argsort(hash_target)
    arrive_order = jnp.argsort(partition_source // nodes_dev, stable=True)
    incoming = reshuffle(embeddings[send_order], row_count, col_count)
    initial = incoming[jnp.argsort(arrive_order)]
    layer_one = spread(initial, tile_values, tile_row, columns, live_slots).astype(jnp.bfloat16)
    layer_one = lax.optimization_barrier(layer_one)
    layer_two = spread(layer_one, tile_values, tile_row, columns, live_slots)
    propagated = (
        (initial.astype(jnp.float32) + layer_one.astype(jnp.float32) + layer_two) / 3.0
    ).astype(jnp.bfloat16)

    def transposed(gradient):
        return transpose_partials(gradient, tile_values, tile_row, columns, live_slots, col_count)

    back_one = transposed(cotangent)
    middle = ((cotangent.astype(jnp.float32) + back_one) / 3.0).astype(jnp.bfloat16)
    back_zero = transposed(middle)
    grad_part = (cotangent.astype(jnp.float32) / 3.0 + back_zero).astype(jnp.bfloat16)
    returned = reshuffle(grad_part[arrive_order], row_count, col_count)
    embed_grad = returned[jnp.argsort(send_order)]
    return (propagated, embed_grad)


def solution(mesh):
    return jax.shard_map(
        shards,
        mesh=mesh,
        in_specs=(
            P(("row", "col"), None),
            P(("row", "col")),
            P(("row", "col")),
            P(("row", "col"), None, None),
            P(("row", "col")),
            P(("row", "col"), None),
            P(("row", "col")),
            P(("row", "col")),
            P(("row", "col"), None),
        ),
        out_specs=(P(("row", "col"), None), P(("row", "col"), None)),
        check_vma=False,
    )
```

profile of v0, /device:TPU:1, one launch (start us, length us, event | category | flops | bytes accessed | tf_op | source)
XLA Modules:
  0.0 455.3 jit_solution(14534381849056537183)
XLA Ops:
  8.8 6.8 %gather_fusion.4 = bf16[96,128,256]{2,1,0:T(8,128)(2,1)} fusion(bf16[4,128,256]{2,1,0:T(8,128)(2,1)} %bitcast.43, s32[1024]{0:T(1024)S(1)} %pad_clamp_fusion.2), kind=kCustom, calls=%fused_computation.4 | custom fusion | bytes 12583296 | tf_op jit(solution)/shard_map/gather | solution.py:34
  15.6 9.9 %multiply_bitcast_fusion.1 = f32[96,128,256]{1,2,0:T(8,128)} fusion(f32[96]{0:T(128)S(1)} %compare_convert_fusion, bf16[96,128,256]{2,1,0:T(8,128)(2,1)} %gather_fusion.4, bf16[96,128,128]{2,1,0:T(8,128)(2,1)S(1)} %copy-done), kind=kOutput, calls=%fused_computation.15 | convolution fusion | flops 808452096 | bytes 22020480 | tf_op jit(solution)/shard_map/sij,siw->sjw/dot_general | solution.py:35
  25.6 12.6 %copy.16 = f32[96,128,256]{2,1,0:T(8,128)} copy(f32[96,128,256]{1,2,0:T(8,128)} %multiply_bitcast_fusion.1) | data formatting | bytes 25165824 | tf_op jit(solution)/shard_map/mul | solution.py:36
  38.2 7.8 %broadcast.54.clone = f32[128,128,256]{2,1,0:T(8,128)} broadcast(f32[]{:T(128)} %constant.28.clone.1), dimensions={} | broadcast | bytes 16777220 | tf_op jit(solution)/shard_map/broadcast.7
  46.0 29.3 %scatter_fusion = f32[128,128,256]{2,1,0:T(8,128)} fusion(f32[128,128,256]{2,1,0:T(8,128)} %broadcast.54.clone, s32[96]{0:T(128)S(1)} %get-tuple-element.11, f32[96,128,256]{2,1,0:T(8,128)} %copy.16), kind=kCustom, calls=%fused_computation.8 | custom fusion | flops 3145728 | bytes 37749120 | tf_op jit(solution)/shard_map/scatter-add | solution.py:37
  75.3 9.0 %convert_element_type.63 = bf16[128,128,256]{2,1,0:T(8,128)(2,1)} convert(f32[128,128,256]{2,1,0:T(8,128)} %scatter_fusion) | non-fusion elementwise | flops 4194304 | bytes 25165824 | tf_op jit(solution)/shard_map/convert_element_type | solution.py:39
  85.0 3.8 sort.62
  88.8 3.2 gather_fusion
  93.7 11.8 %all-to-all-start = ((bf16[128,4,256]{2,1,0:T(4,128)(2,1)}), bf16[128,4,256]{2,1,0:T(4,128)(2,1)}, u32[]{:S(2)}, u32[]{:S(2)}) async-start(bf16[128,4,256]{2,1,0:T(4,128)(2,1)} %reshape.50), calls=%async_computation | async-start | bytes 524288 | tf_op jit(solution)/shard_map/all_to_all | solution.py:12
  105.6 3.8 sort.63
  109.3 3.8 sort.64
  117.9 3.2 gather_fusion.1
  121.4 57.1 %reduce-scatter.3.cloned.1.call-done = bf16[512,256]{1,0:T(8,128)(2,1)} async-done(((bf16[16384,256]{1,0:T(8,128)(2,1)}), bf16[512,256]{1,0:T(8,128)(2,1)}) %reduce-scatter.3.cloned.1.call-update) | async-done | bytes 262160 | tf_op jit(solution)/shard_map/reduce_scatter | solution.py:38
  180.2 6.8 %gather_fusion.5 = bf16[96,128,256]{2,1,0:T(8,128)(2,1)} fusion(bf16[4,128,256]{2,1,0:T(8,128)(2,1)} %bitcast.44, s32[1024]{0:T(1024)S(1)} %pad_clamp_fusion.2), kind=kCustom, calls=%fused_computation.5 | custom fusion | bytes 12583296 | tf_op jit(solution)/shard_map/gather | solution.py:34
  187.0 9.9 %multiply_bitcast_fusion = f32[96,128,256]{1,2,0:T(8,128)} fusion(f32[96]{0:T(128)S(1)} %compare_convert_fusion, bf16[96,128,256]{2,1,0:T(8,128)(2,1)} %gather_fusion.5, bf16[96,128,128]{2,1,0:T(8,128)(2,1)S(1)} %copy-done), kind=kOutput, calls=%fused_computation.14 | convolution fusion | flops 808452096 | bytes 22020480 | tf_op jit(solution)/shard_map/sij,siw->sjw/dot_general | solution.py:35
  197.0 12.6 %copy.18 = f32[96,128,256]{2,1,0:T(8,128)} copy(f32[96,128,256]{1,2,0:T(8,128)} %multiply_bitcast_fusion) | data formatting | bytes 25165824 | tf_op jit(solution)/shard_map/mul | solution.py:36
  209.6 8.3 %broadcast.54 = f32[128,128,256]{2,1,0:T(8,128)} broadcast(f32[]{:T(128)} %constant.28.clone.1), dimensions={} | broadcast | bytes 16777220 | tf_op jit(solution)/shard_map/broadcast.7
  217.9 30.0 %scatter_fusion.1 = f32[128,128,256]{2,1,0:T(8,128)} fusion(f32[128,128,256]{2,1,0:T(8,128)} %broadcast.54, s32[96]{0:T(128)S(1)} %get-tuple-element.11, f32[96,128,256]{2,1,0:T(8,128)} %copy.18), kind=kCustom, calls=%fused_computation.9 | custom fusion | flops 3145728 | bytes 37749120 | tf_op jit(solution)/shard_map/scatter-add | solution.py:37
  247.9 9.0 %convert_element_type.67 = bf16[128,128,256]{2,1,0:T(8,128)(2,1)} convert(f32[128,128,256]{2,1,0:T(8,128)} %scatter_fusion.1) | non-fusion elementwise | flops 4194304 | bytes 25165824 | tf_op jit(solution)/shard_map/convert_element_type | solution.py:39
  257.2 9.5 %gather_fusion.2 = bf16[96,128,256]{2,1,0:T(8,128)(2,1)} fusion(bf16[128,128,256]{2,1,0:T(8,128)(2,1)} %bitcast.48, s32[1024]{0:T(1024)S(1)} %pad_clamp_fusion.3), kind=kCustom, calls=%fused_computation.2 | custom fusion | bytes 12583296 | tf_op jit(solution)/shard_map/gather | solution.py:21
  266.6 9.8 %fusion.27 = f32[96,256,128]{2,1,0:T(8,128)} fusion(bf16[96,128,256]{2,1,0:T(8,128)(2,1)} %gather_fusion.2, bf16[96,128,128]{2,1,0:T(8,128)(2,1)S(1)} %copy-done), kind=kOutput, calls=%fused_computation.60 | convolution fusion | flops 805306368 | bytes 22020096 | tf_op jit(solution)/shard_map/sij,sjw->siw/dot_general | solution.py:22
  276.4 13.1 %copy.19 = f32[96,256,128]{1,0,2:T(8,128)} copy(f32[96,256,128]{2,1,0:T(8,128)} %fusion.27) | data formatting | bytes 25165824 | tf_op jit(solution)/shard_map/sij,sjw->siw/dot_general | solution.py:22
  289.5 9.2 %fusion.4 = bf16[4,128,256]{2,0,1:T(4,128)(2,1)S(1)} fusion(f32[96,256,128]{1,0,2:T(8,128)} %copy.19, f32[96]{0:T(128)S(1)} %compare_convert_fusion, s32[96]{0:T(128)S(1)} %copy-done.6), kind=kOutput, calls=%fused_computation.16 | convolution fusion | flops 151126784 | bytes 12845824 | tf_op jit(solution)/shard_map/bs,siw->biw/dot_general | solution.py:26
  299.5 3.8 sort.65
  303.3 45.5 %reduce-scatter.5.cloned.1.call-done = bf16[512,256]{1,0:T(8,128)(2,1)} async-done(((bf16[16384,256]{1,0:T(8,128)(2,1)}), bf16[512,256]{1,0:T(8,128)(2,1)}) %reduce-scatter.5.cloned.1.call-update) | async-done | bytes 262160 | tf_op jit(solution)/shard_map/reduce_scatter | solution.py:38
  353.8 9.8 %all-to-all-start.1 = ((bf16[128,4,256]{2,1,0:T(4,128)(2,1)}), bf16[128,4,256]{2,1,0:T(4,128)(2,1)}, u32[]{:S(2)}, u32[]{:S(2)}) async-start(bf16[128,4,256]{2,1,0:T(4,128)(2,1)} %reshape.57), calls=%async_computation.3 | async-start | bytes 524288 | tf_op jit(solution)/shard_map/all_to_all | solution.py:12
  363.7 12.3 %all-to-all-done.1 = bf16[128,4,256]{2,1,0:T(4,128)(2,1)} async-done(((bf16[128,4,256]{2,1,0:T(4,128)(2,1)}), bf16[128,4,256]{2,1,0:T(4,128)(2,1)}, u32[]{:S(2)}, u32[]{:S(2)}) %all-to-all-start.1) | async-done | bytes 262176 | tf_op jit(solution)/shard_map/all_to_all | solution.py:12
  379.6 28.1 %all-gather.4.cloned.1.call-done = bf16[16384,256]{1,0:T(8,128)(2,1)} async-done(((bf16[512,256]{1,0:T(8,128)(2,1)}), bf16[16384,256]{1,0:T(8,128)(2,1)}) %all-gather.4.cloned.1.call-update) | async-done | bytes 8388624 | tf_op jit(solution)/shard_map/all_gather | solution.py:20
  407.7 9.3 %gather_fusion.3 = bf16[96,128,256]{2,1,0:T(8,128)(2,1)} fusion(bf16[128,128,256]{2,1,0:T(8,128)(2,1)} %bitcast.47, s32[1024]{0:T(1024)S(1)} %pad_clamp_fusion.3), kind=kCustom, calls=%fused_computation.3 | custom fusion | bytes 12583296 | tf_op jit(solution)/shard_map/gather | solution.py:21
  417.0 9.2 %fusion.28 = f32[96,256,128]{2,1,0:T(8,128)} fusion(bf16[96,128,256]{2,1,0:T(8,128)(2,1)} %gather_fusion.3, bf16[96,128,128]{2,1,0:T(8,128)(2,1)S(1)} %copy-done), kind=kOutput, calls=%fused_computation.61 | convolution fusion | flops 805306368 | bytes 22020096 | tf_op jit(solution)/shard_map/sij,sjw->siw/dot_general | solution.py:22
  426.2 12.6 %copy.20 = f32[96,256,128]{1,0,2:T(8,128)} copy(f32[96,256,128]{2,1,0:T(8,128)} %fusion.28) | data formatting | bytes 25165824 | tf_op jit(solution)/shard_map/sij,sjw->siw/dot_general | solution.py:22
  438.9 8.9 %fusion = f32[4,128,256]{2,0,1:T(4,128)S(1)} fusion(f32[96,256,128]{1,0,2:T(8,128)} %copy.20, f32[96]{0:T(128)S(1)} %compare_convert_fusion, s32[96]{0:T(128)S(1)} %copy-done.6), kind=kOutput, calls=%fused_computation.10 | convolution fusion | flops 150995712 | bytes 13107968 | tf_op jit(solution)/shard_map/bs,siw->biw/dot_general | solution.py:26
  (57 shorter events, 20.7 us)
Async XLA Ops:
  7.2 8.5 %copy-start = (bf16[96,128,128]{2,1,0:T(8,128)(2,1)S(1)}, bf16[96,128,128]{2,1,0:T(8,128)(2,1)}, u32[]{:S(2)}) copy-start(bf16[96,128,128]{2,1,0:T(8,128)(2,1)} %param.12) | copy-start | bytes 9437188
  7.2 171.3 %reduce-scatter.3.cloned.1.call-start = ((), (), s32[]{:S(2)}) async-start(), calls=%async_computation.5 | async-start | bytes 8650752 | tf_op jit(solution)/shard_map/reduce_scatter | solution.py:38
  25.6 12.6 %copy-start.7 = (s32[96]{0:T(128)S(1)}, s32[96]{0:T(128)}, u32[]{:S(2)}) copy-start(s32[96]{0:T(128)} %param.15) | copy-start | bytes 1156
  25.6 12.6 %copy-start.8 = (s32[96,1]{0,1:T(1,128)S(1)}, s32[96,1]{0,1:T(1,128)}, u32[]{:S(2)}) copy-start(s32[96,1]{0,1:T(1,128)} %param.14) | copy-start | bytes 1156
  84.3 0.7 copy-start.4
  84.3 21.2 %copy-start.5 = (s32[512]{0:T(512)S(1)}, s32[512]{0:T(512)}, u32[]{:S(2)}) copy-start(s32[512]{0:T(512)} %param.10) | copy-start | bytes 6148
  84.3 94.1 %copy-start.1 = (bf16[512,256]{1,0:T(8,128)(2,1)S(1)}, bf16[512,256]{1,0:T(8,128)(2,1)}, u32[]{:S(2)}) copy-start(bf16[512,256]{1,0:T(8,128)(2,1)} %param.17) | copy-start | bytes 786436
  93.7 22.5 %all-to-all-start = ((bf16[128,4,256]{2,1,0:T(4,128)(2,1)}), bf16[128,4,256]{2,1,0:T(4,128)(2,1)}, u32[]{:S(2)}, u32[]{:S(2)}) async-start(bf16[128,4,256]{2,1,0:T(4,128)(2,1)} %reshape.50), calls=%async_computation | async-start | bytes 524288 | tf_op jit(solution)/shard_map/all_to_all | solution.py:12
  105.5 151.7 %all-gather.6.cloned.1.call-start = ((), (), s32[]{:S(2)}) async-start(), calls=%async_computation.7 | async-start | bytes 8650752 | tf_op jit(solution)/shard_map/all_gather | solution.py:20
  121.1 227.6 %reduce-scatter.5.cloned.1.call-start = ((), (), s32[]{:S(2)}) async-start(), calls=%async_computation.6 | async-start | bytes 8650752 | tf_op jit(solution)/shard_map/reduce_scatter | solution.py:38
  256.9 150.8 %all-gather.4.cloned.1.call-start = ((), (), s32[]{:S(2)}) async-start(), calls=%async_computation.4 | async-start | bytes 8650752 | tf_op jit(solution)/shard_map/all_gather | solution.py:20
  276.4 13.1 %copy-start.6 = (s32[96]{0:T(128)S(1)}, s32[96]{0:T(128)}, u32[]{:S(2)}) copy-start(s32[96]{0:T(128)} %param.13) | copy-start | bytes 1156
  353.8 22.2 %all-to-all-start.1 = ((bf16[128,4,256]{2,1,0:T(4,128)(2,1)}), bf16[128,4,256]{2,1,0:T(4,128)(2,1)}, u32[]{:S(2)}, u32[]{:S(2)}) async-start(bf16[128,4,256]{2,1,0:T(4,128)(2,1)} %reshape.57), calls=%async_computation.3 | async-start | bytes 524288 | tf_op jit(solution)/shard_map/all_to_all | solution.py:12
  438.9 9.1 %copy-start.2 = (bf16[4,128,256]{2,1,0:T(8,128)(2,1)S(1)}, bf16[4,128,256]{2,1,0:T(8,128)(2,1)}, u32[]{:S(2)}) copy-start(bf16[4,128,256]{2,1,0:T(8,128)(2,1)} %copy.13) | copy-start | bytes 786436
  438.9 9.1 %copy-start.3 = (bf16[512,256]{1,0:T(8,128)(2,1)S(1)}, bf16[512,256]{1,0:T(8,128)(2,1)}, u32[]{:S(2)}) copy-start(bf16[512,256]{1,0:T(8,128)(2,1)} %gather_fusion.1) | copy-start | bytes 786436
Sparse Core Ops, SparseCore 0:
  84.5 93.9 reduce-scatter.2
  181.6 54.2 all-gather.5
  257.0 91.7 reduce-scatter.4
  350.9 56.7 all-gather.3
where the time goes:
time: 457 us; the launch traced here: 455 us
  waiting for transfers between devices  146 us (32%)
  local copies, waits for them, and re-layouts  118 us (26%)
  other arithmetic  97.4 us (21%)
  matrix products  57 us (12%)
  starting transfers between devices  22.2 us (5%)
  between operations  14.7 us (3%)
    reduce_scatter x2, waiting for transfers between devices, transpose_partials(): lax.psum_scatter(partial_sum.reshape(-1, feat_width).astype(jnp.bfloat16)...  103 us
    scatter-add x2, other arithmetic, transpose_partials(): jax.ops.segment_sum(products, columns, num_segments=blocks_dev * col_count)  59.3 us
    all_gather x2, waiting for transfers between devices, spread(): group_rows = lax.all_gather(features, 'col', axis=0, tiled=True)  28.1 us
    dot_general x2, local copies, waits for them, and re-layouts, spread(): jnp.einsum('sij,sjw->siw', tile_values, chosen, preferred_element_type=jn...  25.7 us
    mul x2, local copies, waits for them, and re-layouts, transpose_partials(): products = products * live_slots[:, None, None]  25.2 us
    all_to_all x2, starting transfers between devices, reshuffle(): lax.all_to_all(direct, ('row', 'col'), split_axis=0, concat_axis=0, tiled...  21.6 us
    dot_general x2, matrix products, transpose_partials(): jnp.einsum('sij,siw->sjw', tile_values, chosen, preferred_element_type=jn...  19.9 us
    dot_general x2, matrix products, spread(): jnp.einsum('sij,sjw->siw', tile_values, chosen, preferred_element_type=jn...  19 us
  transfers between devices with their start and end apart: 6, of which 5 were waited for; matrix products, arithmetic and copies ran while one was open for 34% of the time, Pallas kernels for 0%

commit v1 on v0

v1 whole, which is shorter than its diff:
```python
import functools

import jax
import jax.numpy as jnp
from jax import lax
from jax.experimental import pallas as pl
from jax.experimental.pallas import tpu as pltpu
from jax.sharding import PartitionSpec as P

SIDE = 4
CORES = 2
TILE = 128
NODES = 512
BLOCKS = NODES // TILE
WIDTH = 256
SLOTS = 96
OWNER_CAP = 4
CAP = SIDE * CORES * OWNER_CAP
CODE_ROWS = 16
COUNT_LANE = 64
PACKED = CAP * TILE + CODE_ROWS
COLUMNS = CORES * SIDE * BLOCKS
TURNED = BLOCKS * WIDTH
BF16 = jnp.bfloat16
F32 = jnp.float32
VMEM_LIMIT = 48 * 1024 * 1024

WHOLE = pl.BlockSpec(memory_space=pltpu.VMEM)
SCALARS = pl.BlockSpec(memory_space=pltpu.SMEM)


def params(limit=VMEM_LIMIT):
    return pltpu.CompilerParams(vmem_limit_bytes=limit)


def struct(shape, dtype):
    return jax.ShapeDtypeStruct(shape, dtype)


def cost(flops, nbytes):
    return pl.CostEstimate(flops=int(flops), bytes_accessed=int(nbytes), transcendentals=0)


def move(array, axis, step):
    pairs = []
    for x in range(SIDE):
        for y in range(SIDE):
            for c in range(CORES):
                to_x = (x + step) % SIDE if axis == "x" else x
                to_y = (y + step) % SIDE if axis == "y" else y
                to_c = (c + step) % CORES if axis == "c" else c
                pairs.append(((x * SIDE + y) * CORES + c, (to_x * SIDE + to_y) * CORES + to_c))
    return lax.ppermute(array, "col", pairs)


def reshuffle(payload):
    devices = lax.axis_size("row") * lax.axis_size("col")
    direct = payload.reshape(devices, NODES // devices, WIDTH)
    moved = lax.all_to_all(direct, ("row", "col"), split_axis=0, concat_axis=0, tiled=True)
    return moved.reshape(payload.shape)


def ordering(key_row, key_col):
    below = (key_col[...] < key_row[...]).astype(jnp.int32)
    rank = jnp.sum(below, axis=0, keepdims=True)
    spot = lax.broadcasted_iota(jnp.int32, (NODES, NODES), 0)
    return (spot == rank).astype(F32).astype(BF16)


def order_kernel(key_row, key_col, data, out):
    select = ordering(key_row, key_col)
    out[...] = jnp.dot(select, data[...], preferred_element_type=F32).astype(BF16)


def order_turned_kernel(key_row, key_col, data, out):
    select = ordering(key_row, key_col)
    total = jnp.zeros((NODES, WIDTH), F32)
    for b in range(BLOCKS):
        part = select[:, b * TILE : (b + 1) * TILE]
        block = data[b * WIDTH : (b + 1) * WIDTH, :]
        total += lax.dot_general(part, block, (((1,), (1,)), ((), ())), preferred_element_type=F32)
    out[...] = total.astype(BF16)


def restore_kernel(key_row, key_col, data, out):
    below = (key_row[...] < key_col[...]).astype(jnp.int32)
    rank = jnp.sum(below, axis=1, keepdims=True)
    spot = lax.broadcasted_iota(jnp.int32, (NODES, NODES), 1)
    select = (spot == rank).astype(F32).astype(BF16)
    out[...] = jnp.dot(select, data[...], preferred_element_type=F32).astype(BF16)


def permute_call(kernel, key, data):
    return pl.pallas_call(
        kernel,
        out_shape=struct((NODES, WIDTH), BF16),
        in_specs=[WHOLE] * 3,
        out_specs=WHOLE,
        compiler_params=params(),
        cost_estimate=cost(2 * NODES * NODES * WIDTH, 4 * NODES * WIDTH),
    )(key.reshape(1, NODES), key.reshape(NODES, 1), data)


def bucket_kernel(target, code, tiles, *refs):
    outs, (listed, counts) = refs[:SIDE], refs[SIDE:]
    for d in range(SIDE + 1):
        counts[d] = 0

    def note(s, carry):
        d = target[s]
        n = counts[d]
        listed[d * SLOTS + n] = s
        counts[d] = n + 1
        return carry

    lax.fori_loop(0, SLOTS, note, 0)
    lane = lax.broadcasted_iota(jnp.int32, (CODE_ROWS, TILE), 1)
    for d in range(SIDE):
        used = counts[d]

        def place(n, codes, d=d):
            s = listed[d * SLOTS + n]
            outs[d][pl.ds(pl.multiple_of(n * TILE, TILE), TILE), :] = tiles[s]
            return jnp.where(lane == n, code[s], codes)

        def clear(n, carry, d=d):
            outs[d][pl.ds(pl.multiple_of(n * TILE, TILE), TILE), :] = jnp.zeros((TILE, TILE), BF16)
            return carry

        codes = lax.fori_loop(0, used, place, jnp.zeros((CODE_ROWS, TILE), jnp.int32))
        lax.fori_loop(used, CAP, clear, 0)
        codes = jnp.where(lane == COUNT_LANE, used, codes)
        outs[d][CAP * TILE :, :] = codes.astype(F32).astype(BF16)


def bucket(tiles, target, code):
    return pl.pallas_call(
        bucket_kernel,
        out_shape=[struct((PACKED, TILE), BF16)] * SIDE,
        in_specs=[SCALARS, SCALARS, WHOLE],
        out_specs=[WHOLE] * SIDE,
        scratch_shapes=[
            pltpu.SMEM(((SIDE + 1) * SLOTS,), jnp.int32),
            pltpu.SMEM((SIDE + 1,), jnp.int32),
        ],
        compiler_params=params(),
        cost_estimate=cost(1e6, 7e6),
    )(target, code, tiles)


def slot_steps(codes):
    most = codes[COUNT_LANE]
    for k in range(1, SIDE):
        most = jnp.maximum(most, codes[k * TILE + COUNT_LANE])
    return (most + 1) // 2


def forward_kernel(codes, *refs):
    tiles, refs = refs[:SIDE], refs[SIDE:]
    shards, refs = refs[: CORES * SIDE], refs[CORES * SIDE :]
    outs, (features, *totals) = refs[:SIDE], refs[SIDE:]
    for j in range(CORES * SIDE):
        features[j * NODES : (j + 1) * NODES, :] = shards[j][...]
    for k in range(SIDE):
        totals[k][...] = jnp.zeros((NODES, WIDTH), F32)

    def step(i, carry):
        for u in range(2):
            n = i * 2 + u
            for k in range(SIDE):
                code = codes[k * TILE + n]
                row = pl.multiple_of((code // COLUMNS) * TILE, TILE)
                column = pl.multiple_of((code % COLUMNS) * TILE, TILE)
                tile = tiles[k][pl.ds(pl.multiple_of(n * TILE, TILE), TILE), :]
                block = features[pl.ds(column, TILE), :]
                totals[k][pl.ds(row, TILE), :] += jnp.dot(tile, block, preferred_element_type=F32)
        return carry

    lax.fori_loop(0, slot_steps(codes), step, 0)
    for k in range(SIDE):
        outs[k][...] = totals[k][...].astype(outs[k].dtype)


def forward_product(packs, codes, shards):
    shape = (NODES, WIDTH)
    return pl.pallas_call(
        forward_kernel,
        out_shape=[struct(shape, F32)] + [struct(shape, BF16)] * (SIDE - 1),
        in_specs=[SCALARS] + [WHOLE] * (SIDE + CORES * SIDE),
        out_specs=[WHOLE] * SIDE,
        scratch_shapes=[pltpu.VMEM((CORES * SIDE * NODES, WIDTH), BF16)]
        + [pltpu.VMEM(shape, F32)] * SIDE,
        compiler_params=params(),
        cost_estimate=cost(1e9, 16e6),
    )(codes, *packs, *shards)


def backward_kernel(codes, *refs):
    tiles, refs = refs[:SIDE], refs[SIDE:]
    shards, refs = refs[:SIDE], refs[SIDE:]
    outs, (totals,) = refs[: CORES * SIDE], refs[CORES * SIDE :]
    totals[...] = jnp.zeros(totals.shape, F32)

    def step(i, carry):
        for u in range(2):
            n = i * 2 + u
            for k in range(SIDE):
                code = codes[k * TILE + n]
                row = pl.multiple_of((code // COLUMNS) * WIDTH, WIDTH)
                column = pl.multiple_of((code % COLUMNS) * WIDTH, WIDTH)
                tile = tiles[k][pl.ds(pl.multiple_of(n * TILE, TILE), TILE), :]
                block = shards[k][pl.ds(row, WIDTH), :]
                totals[pl.ds(column, WIDTH), :] += jnp.dot(block, tile, preferred_element_type=F32)
        return carry

    lax.fori_loop(0, slot_steps(codes), step, 0)
    for j in range(CORES * SIDE):
        outs[j][...] = totals[j * TURNED : (j + 1) * TURNED, :].astype(outs[j].dtype)


def backward_product(packs, codes, shards):
    shape = (TURNED, TILE)
    return pl.pallas_call(
        backward_kernel,
        out_shape=[struct(shape, F32)] * SIDE + [struct(shape, BF16)] * SIDE,
        in_specs=[SCALARS] + [WHOLE] * (2 * SIDE),
        out_specs=[WHOLE] * (CORES * SIDE),
        scratch_shapes=[pltpu.VMEM((CORES * SIDE * TURNED, TILE), F32)],
        compiler_params=params(),
        cost_estimate=cost(1e9, 16e6),
    )(codes, *packs, *shards)


ORDER = (2, 1, 3)


def gather_line(array, axis):
    got = {d: move(array, axis, d) for d in ORDER}
    return [array] + [got[d] for d in range(1, SIDE)]


def gather_forward(features):
    line = gather_line(features, "x")
    return line + [move(shard, "c", 1) for shard in line]


def scatter_forward(terms):
    total = terms[0]
    got = {k: move(terms[k], "y", -k) for k in ORDER}
    for k in ORDER:
        total = total + got[k].astype(F32)
    return total


def scatter_backward(terms):
    near, far = terms[:SIDE], terms[SIDE:]
    got = {}
    for j in ORDER:
        both = near[j] + move(far[j], "c", 1).astype(F32)
        got[j] = move(both.astype(BF16), "x", -j)
    total = near[0] + move(far[0], "c", 1).astype(F32)
    for j in ORDER:
        total = total + got[j].astype(F32)
    return total


def shards(
    embeddings,
    partition_source,
    hash_target,
    tile_values,
    tile_row,
    tile_owner,
    tile_sub,
    tile_count,
    cotangent,
):
    index = lax.axis_index("col")
    core = index % CORES
    own_y = (index // CORES) % SIDE
    own_x = index // (CORES * SIDE)

    owner = tile_owner[:, 0]
    live = jnp.arange(SLOTS, dtype=jnp.int32) < tile_count[0]
    back_x = (own_x - owner // (CORES * SIDE)) % SIDE
    far_y = (owner // CORES - own_y) % SIDE
    side = (owner + core) % CORES
    column = (side * SIDE + back_x) * BLOCKS + tile_sub
    target = jnp.where(live, far_y, SIDE)
    packs = bucket(tile_values, target, tile_row * COLUMNS + column)
    moved = {d: move(packs[d], "y", d) for d in ORDER}
    packs = [packs[0]] + [moved[d] for d in range(1, SIDE)]
    codes = jnp.concatenate([pack[CAP * TILE] for pack in packs]).astype(jnp.int32)

    part_key = (partition_source // NODES) * NODES + jnp.arange(NODES, dtype=jnp.int32)
    incoming = reshuffle(permute_call(order_kernel, hash_target, embeddings))
    initial = permute_call(restore_kernel, part_key, incoming)

    def spread(features):
        return scatter_forward(forward_product(packs, codes, gather_forward(features)))

    def collect(gradient):
        return scatter_backward(backward_product(packs, codes, gather_line(gradient, "y")))

    turned = cotangent.reshape(BLOCKS, TILE, WIDTH).transpose(0, 2, 1).reshape(TURNED, TILE)
    back_one = collect(turned)
    layer_one = spread(initial).astype(BF16)
    middle = ((turned.astype(F32) + back_one) / 3.0).astype(BF16)
    back_zero = collect(middle)
    layer_two = spread(layer_one)
    grad_part = (turned.astype(F32) / 3.0 + back_zero).astype(BF16)
    returned = reshuffle(permute_call(order_turned_kernel, part_key, grad_part))
    embed_grad = permute_call(restore_kernel, hash_target, returned)
    propagated = ((initial.astype(F32) + layer_one.astype(F32) + layer_two) / 3.0).astype(BF16)
    return propagated, embed_grad


def solution(mesh):
    both = ("row", "col")
    return jax.shard_map(
        shards,
        mesh=mesh,
        in_specs=(
            P(both, None),
            P(both),
            P(both),
            P(both, None, None),
            P(both),
            P(both, None),
            P(both),
            P(both),
            P(both, None),
        ),
        out_specs=(P(both, None), P(both, None)),
        check_vma=False,
    )
```

time: 457 us -> 201 us (0.44)
  local copies, waits for them, and re-layouts: 118 us -> 7.44 us
  other arithmetic: 97.4 us -> 3.83 us
  waiting for transfers between devices: 146 us -> 83.8 us
  matrix products: 57 us -> 0 us
  starting transfers between devices: 22.2 us -> 74.9 us
  Pallas kernels: 0 us -> 28 us
  between operations: 14.7 us -> 1.7 us
    reduce_scatter x2 -> x0, waiting for transfers between devices: 103 us -> none  [transpose_partials(): lax.psum_scatter(partial_sum.reshape(-1, feat_width).astype(jnp.bfloat16)...]
    ppermute x0 -> x43, waiting for transfers between devices: none -> 73.7 us  [move(): return lax.ppermute(array, 'col', pairs)]
    scatter-add x2 -> x0, other arithmetic: 59.3 us -> none  [transpose_partials(): jax.ops.segment_sum(products, columns, num_segments=blocks_dev * col_count)]
    dot_general x6 -> x0, matrix products: 57 us -> none  [the longest x2 19.9 us: transpose_partials(): jnp.einsum('sij,siw->sjw', tile_values, chosen, preferred_element_type=jn...]
    ppermute x0 -> x43, starting transfers between devices: none -> 53.8 us  [move(): return lax.ppermute(array, 'col', pairs)]
    gather x8 -> x0, local copies, waits for them, and re-layouts: 44 us -> none  [the longest x2 18.8 us: spread(): chosen = group_rows.reshape(-1, tile_size, feat_width)[columns]]
    all_gather x2 -> x0, waiting for transfers between devices: 28.1 us -> none  [spread(): group_rows = lax.all_gather(features, 'col', axis=0, tiled=True)]
    pallas_call x0 -> x9, Pallas kernels: none -> 28 us  [the longest x2 10 us: backward_product(): pl.pallas_call(backward_kernel, out_shape=[struct(shape, F32)] * SIDE + [...]
  transfers between devices with their start and end apart: 6 -> 45, of which waited for: 5 -> 16; matrix products, arithmetic and copies ran while one was open for 34% -> 4% of each run, Pallas kernels for 0% -> 10%
where the time goes in v1:
time: 201 us; the launch traced here: 200 us
  waiting for transfers between devices  83.8 us (42%)
  starting transfers between devices  74.9 us (37%)
  Pallas kernels  28 us (14%)
  local copies, waits for them, and re-layouts  7.44 us (4%)
  other arithmetic  3.83 us (2%)
    ppermute x43, waiting for transfers between devices, move(): return lax.ppermute(array, 'col', pairs)  73.7 us
    ppermute x43, starting transfers between devices, move(): return lax.ppermute(array, 'col', pairs)  53.8 us
    all_to_all x2, starting transfers between devices, reshuffle(): lax.all_to_all(direct, ('row', 'col'), split_axis=0, concat_axis=0, tiled...  21.1 us
    all_to_all x2, waiting for transfers between devices, reshuffle(): lax.all_to_all(direct, ('row', 'col'), split_axis=0, concat_axis=0, tiled...  10.1 us
    pallas_call x2, Pallas kernels, backward_product(): pl.pallas_call(backward_kernel, out_shape=[struct(shape, F32)] * SIDE + [...  10 us
    pallas_call x2, Pallas kernels, forward_product(): pl.pallas_call(forward_kernel, out_shape=[struct(shape, F32)] + [struct(s...  8.86 us
    pallas_call x1, Pallas kernels, bucket(): pl.pallas_call(bucket_kernel, out_shape=[struct((PACKED, TILE), BF16)] *...  5.8 us
  transfers between devices with their start and end apart: 45, of which 16 were waited for; matrix products, arithmetic and copies ran while one was open for 4% of the time, Pallas kernels for 10%

profile of v1, /device:TPU:1, one launch (start us, length us, event | category | flops | bytes accessed | tf_op | source)
XLA Modules:
  0.0 199.6 jit_solution(9090153172090851492)
XLA Ops:
  2.1 5.8 %shard_map.106 = (bf16[4112,128]{1,0:T(8,128)(2,1)S(1)}, bf16[4112,128]{1,0:T(8,128)(2,1)}, bf16[4112,128]{1,0:T(8,128)(2,1)}, bf16[4112,128]{1,0:T(8,128)(2,1)}) custom-call(s32[96]{0:T(128)S(1)} %get-tuple-element.59.target, s32[96]{0:T(128)S(1)} %get-tuple-element.58.code, bf16[96,128,128]{2,1,0:T(8,128)(2,1)} %tiles.1), custom_call_target="tpu_custom_call" | custom-call | flops 1000000 | bytes 7000000 | tf_op jit(solution)/shard_map/pallas_call | solution.py:137
  7.9 3.6 %collective-permute-start.2 = (bf16[4112,128]{1,0:T(8,128)(2,1)}, bf16[4112,128]{1,0:T(8,128)(2,1)}, u32[]{:S(2)}, u32[]{:S(2)}) collective-permute-start(bf16[4112,128]{1,0:T(8,128)(2,1)} %get-tuple-element.33), channel_id=1, source_target_pairs={{0,6},{1,7},{2,0},{3,1},{4,2},{5,3},{6,4},{7,5},{8,14},{9,15},{10,... | collective-permute-start | bytes 3158024 | tf_op jit(solution)/shard_map/ppermute | solution.py:53
  12.6 1.7 collective-permute-start.23
  17.2 11.1 %all-to-all-start = ((bf16[128,4,256]{2,1,0:T(4,128)(2,1)}), bf16[128,4,256]{2,1,0:T(4,128)(2,1)}, u32[]{:S(2)}, u32[]{:S(2)}) async-start(bf16[128,4,256]{2,1,0:T(4,128)(2,1)} %reshape.42), calls=%async_computation | async-start | bytes 524288 | tf_op jit(solution)/shard_map/all_to_all | solution.py:59
  28.4 35.8 %collective-permute-done.2.refs_3_ = bf16[4112,128]{1,0:T(8,128)(2,1)} collective-permute-done((bf16[4112,128]{1,0:T(8,128)(2,1)}, bf16[4112,128]{1,0:T(8,128)(2,1)}, u32[]{:S(2)}, u32[]{:S(2)}) %collective-permute-start.2) | collective-permute-done | bytes 1052704 | tf_op jit(solution)/shard_map/ppermute | solution.py:53
  64.1 3.6 %collective-permute-start.25 = (bf16[1024,128]{1,0:T(8,128)(2,1)S(1)}, bf16[1024,128]{1,0:T(8,128)(2,1)S(1)}, u32[]{:S(2)}, u32[]{:S(2)}) collective-permute-start(bf16[1024,128]{1,0:T(8,128)(2,1)S(1)} %bitcast.44), channel_id=1, source_target_pairs={{0,6},{1,7},{2,0},{3,1},{4,2},{5,3},{6,4},{7,5},{8,14},{9,15},{10,... | collective-permute-start | bytes 786440 | tf_op jit(solution)/shard_map/ppermute | solution.py:53
  69.8 3.3 %collective-permute-done.24.refs_6_ = bf16[1024,128]{1,0:T(8,128)(2,1)} collective-permute-done((bf16[1024,128]{1,0:T(8,128)(2,1)S(1)}, bf16[1024,128]{1,0:T(8,128)(2,1)}, u32[]{:S(2)}, u32[]{:S(2)}) %collective-permute-start.24) | collective-permute-done | bytes 262176 | tf_op jit(solution)/shard_map/ppermute | solution.py:53
  73.2 5.4 %shard_map.109 = (f32[1024,128]{1,0:T(8,128)S(1)}, f32[1024,128]{1,0:T(8,128)S(1)}, f32[1024,128]{1,0:T(8,128)S(1)}, f32[1024,128]{1,0:T(8,128)S(1)}, bf16[1024,...) custom-call(s32[512]{0:T(512)S(1)} %maximum_convert_fusion.codes, ...), custom_call_target="tpu_custom_call" | custom-call | flops 1000000000 | bytes 16000000 | tf_op jit(solution)/shard_map/pallas_call | solution.py:223
  81.5 1.8 collective-permute-start.27
  86.2 3.2 %collective-permute-start.3 = (bf16[512,256]{1,0:T(8,128)(2,1)S(1)}, bf16[512,256]{1,0:T(8,128)(2,1)S(1)}, u32[]{:S(2)}, u32[]{:S(2)}) collective-permute-start(bf16[512,256]{1,0:T(8,128)(2,1)S(1)} %shard_map.105.refs_4_), channel_id=1, source_target_pairs={{0,8},{1,9},{2,10},{3,11},{4,12},{5,13},{6,14},{7,15},{8,16},{9,17... | collective-permute-start | bytes 786440 | tf_op jit(solution)/shard_map/ppermute | solution.py:53
  89.4 2.6 %collective-permute-start.4 = (bf16[512,256]{1,0:T(8,128)(2,1)S(1)}, bf16[512,256]{1,0:T(8,128)(2,1)S(1)}, u32[]{:S(2)}, u32[]{:S(2)}) collective-permute-start(bf16[512,256]{1,0:T(8,128)(2,1)S(1)} %shard_map.105.refs_4_), channel_id=1, source_target_pairs={{0,16},{1,17},{2,18},{3,19},{4,20},{5,21},{6,22},{7,23},{8,24},{9,... | collective-permute-start | bytes 786440 | tf_op jit(solution)/shard_map/ppermute | solution.py:53
  95.4 2.1 %collective-permute-done.3.refs_5_ = bf16[512,256]{1,0:T(8,128)(2,1)S(1)} collective-permute-done((bf16[512,256]{1,0:T(8,128)(2,1)S(1)}, bf16[512,256]{1,0:T(8,128)(2,1)S(1)}, u32[]{:S(2)}, u32[]{:S(2)}) %collective-permute-start.3) | collective-permute-done | bytes 262176 | tf_op jit(solution)/shard_map/ppermute | solution.py:53
  98.7 5.3 %collective-permute-done.4.refs_6_ = bf16[512,256]{1,0:T(8,128)(2,1)S(1)} collective-permute-done((bf16[512,256]{1,0:T(8,128)(2,1)S(1)}, bf16[512,256]{1,0:T(8,128)(2,1)S(1)}, u32[]{:S(2)}, u32[]{:S(2)}) %collective-permute-start.4) | collective-permute-done | bytes 262176 | tf_op jit(solution)/shard_map/ppermute | solution.py:53
  105.4 4.3 %collective-permute-done.28 = bf16[1024,128]{1,0:T(8,128)(2,1)S(1)} collective-permute-done((bf16[1024,128]{1,0:T(8,128)(2,1)S(1)}, bf16[1024,128]{1,0:T(8,128)(2,1)S(1)}, u32[]{:S(2)}, u32[]{:S(2)}) %collective-permute-start.28) | collective-permute-done | bytes 262176 | tf_op jit(solution)/shard_map/ppermute | solution.py:53
  110.9 4.0 %collective-permute-done.30 = bf16[1024,128]{1,0:T(8,128)(2,1)S(1)} collective-permute-done((bf16[1024,128]{1,0:T(8,128)(2,1)S(1)}, bf16[1024,128]{1,0:T(8,128)(2,1)S(1)}, u32[]{:S(2)}, u32[]{:S(2)}) %collective-permute-start.30) | collective-permute-done | bytes 262176 | tf_op jit(solution)/shard_map/ppermute | solution.py:53
  116.0 2.8 %collective-permute-start.34 = (bf16[1024,128]{1,0:T(8,128)(2,1)S(1)}, bf16[1024,128]{1,0:T(8,128)(2,1)S(1)}, u32[]{:S(2)}, u32[]{:S(2)}) collective-permute-start(bf16[1024,128]{1,0:T(8,128)(2,1)S(1)} %fusion.3.refs_4_), channel_id=1, source_target_pairs={{0,4},{1,5},{2,6},{3,7},{4,0},{5,1},{6,2},{7,3},{8,12},{9,13},{10,... | collective-permute-start | bytes 786440 | tf_op jit(solution)/shard_map/ppermute | solution.py:53
  118.9 4.0 %shard_map.107 = (f32[512,256]{1,0:T(8,128)S(1)}, bf16[512,256]{1,0:T(8,128)(2,1)S(1)}, bf16[512,256]{1,0:T(8,128)(2,1)S(1)}, bf16[512,256]{1,0:T(8,128)(2,1)S(1)}) custom-call(s32[512]{0:T(512)S(1)} %maximum_convert_fusion.codes, bf16[4112,128]{1,0:T(8,128)(2,1)S(1)} %get-tuple-element.30.refs_0_, bf16[4112,128]{1,0:T(8,128)(2,1)S(1)} %copy-done.1, ...), custom_call_target="tpu_custom_call" | custom-call | flops 1000000000 | bytes 16000000 | tf_op jit(solution)/shard_map/pallas_call | solution.py:186
  123.0 2.2 %collective-permute-start.10 = (bf16[512,256]{1,0:T(8,128)(2,1)S(1)}, bf16[512,256]{1,0:T(8,128)(2,1)S(1)}, u32[]{:S(2)}, u32[]{:S(2)}) collective-permute-start(bf16[512,256]{1,0:T(8,128)(2,1)S(1)} %get-tuple-element.35), channel_id=1, source_target_pairs={{0,4},{1,5},{2,6},{3,7},{4,0},{5,1},{6,2},{7,3},{8,12},{9,13},{10,... | collective-permute-start | bytes 786440 | tf_op jit(solution)/shard_map/ppermute | solution.py:53
  126.7 3.8 %collective-permute-done.34.refs_6_ = bf16[1024,128]{1,0:T(8,128)(2,1)S(1)} collective-permute-done((bf16[1024,128]{1,0:T(8,128)(2,1)S(1)}, bf16[1024,128]{1,0:T(8,128)(2,1)S(1)}, u32[]{:S(2)}, u32[]{:S(2)}) %collective-permute-start.34) | collective-permute-done | bytes 262176 | tf_op jit(solution)/shard_map/ppermute | solution.py:53
  130.7 4.7 %shard_map.110 = (f32[1024,128]{1,0:T(8,128)S(1)}, f32[1024,128]{1,0:T(8,128)S(1)}, f32[1024,128]{1,0:T(8,128)S(1)}, f32[1024,128]{1,0:T(8,128)S(1)}, bf16[1024,...) custom-call(s32[512]{0:T(512)S(1)} %maximum_convert_fusion.codes, ...), custom_call_target="tpu_custom_call" | custom-call | flops 1000000000 | bytes 16000000 | tf_op jit(solution)/shard_map/pallas_call | solution.py:223
  135.4 2.4 %collective-permute-start.37 = (bf16[1024,128]{1,0:T(8,128)(2,1)S(1)}, bf16[1024,128]{1,0:T(8,128)(2,1)S(1)}, u32[]{:S(2)}, u32[]{:S(2)}) collective-permute-start(bf16[1024,128]{1,0:T(8,128)(2,1)S(1)} %get-tuple-element.53), channel_id=1, source_target_pairs={{0,1},{1,0},{2,3},{3,2},{4,5},{5,4},{6,7},{7,6},{8,9},{9,8},{10,11... | collective-permute-start | bytes 786440 | tf_op jit(solution)/shard_map/ppermute | solution.py:53
  137.8 4.2 %collective-permute-done.11 = bf16[512,256]{1,0:T(8,128)(2,1)S(1)} collective-permute-done((bf16[512,256]{1,0:T(8,128)(2,1)S(1)}, bf16[512,256]{1,0:T(8,128)(2,1)S(1)}, u32[]{:S(2)}, u32[]{:S(2)}) %collective-permute-start.11) | collective-permute-done | bytes 262176 | tf_op jit(solution)/shard_map/ppermute | solution.py:53
  144.1 2.1 %collective-permute-start.14 = (bf16[512,256]{1,0:T(8,128)(2,1)S(1)}, bf16[512,256]{1,0:T(8,128)(2,1)S(1)}, u32[]{:S(2)}, u32[]{:S(2)}) collective-permute-start(bf16[512,256]{1,0:T(8,128)(2,1)S(1)} %add_convert_fusion.6.refs_4_), channel_id=1, source_target_pairs={{0,16},{1,17},{2,18},{3,19},{4,20},{5,21},{6,22},{7,23},{8,24},{9,... | collective-permute-start | bytes 786440 | tf_op jit(solution)/shard_map/ppermute | solution.py:53
  150.7 2.6 %collective-permute-start.16 = (bf16[512,256]{1,0:T(8,128)(2,1)S(1)}, bf16[512,256]{1,0:T(8,128)(2,1)S(1)}, u32[]{:S(2)}, u32[]{:S(2)}) collective-permute-start(bf16[512,256]{1,0:T(8,128)(2,1)S(1)} %add_convert_fusion.6.refs_4_), channel_id=1, source_target_pairs={{0,1},{1,0},{2,3},{3,2},{4,5},{5,4},{6,7},{7,6},{8,9},{9,8},{10,11... | collective-permute-start | bytes 786440 | tf_op jit(solution)/shard_map/ppermute | solution.py:53
  153.3 3.8 %collective-permute-done.14.refs_6_ = bf16[512,256]{1,0:T(8,128)(2,1)S(1)} collective-permute-done((bf16[512,256]{1,0:T(8,128)(2,1)S(1)}, bf16[512,256]{1,0:T(8,128)(2,1)S(1)}, u32[]{:S(2)}, u32[]{:S(2)}) %collective-permute-start.14) | collective-permute-done | bytes 262176 | tf_op jit(solution)/shard_map/ppermute | solution.py:53
  157.2 1.9 collective-permute-start.17
  159.9 2.9 %collective-permute-start.38 = (bf16[1024,128]{1,0:T(8,128)(2,1)S(1)}, bf16[1024,128]{1,0:T(8,128)(2,1)S(1)}, u32[]{:S(2)}, u32[]{:S(2)}) collective-permute-start(bf16[1024,128]{1,0:T(8,128)(2,1)S(1)} %add_convert_fusion.2), channel_id=1, source_target_pairs={{0,16},{1,17},{2,18},{3,19},{4,20},{5,21},{6,22},{7,23},{8,24},{9,... | collective-permute-start | bytes 786440 | tf_op jit(solution)/shard_map/ppermute | solution.py:53
  164.3 4.8 %shard_map.108 = (f32[512,256]{1,0:T(8,128)S(1)}, bf16[512,256]{1,0:T(8,128)(2,1)}, bf16[512,256]{1,0:T(8,128)(2,1)}, bf16[512,256]{1,0:T(8,128)(2,1)}) custom-call(s32[512]{0:T(512)S(1)} %maximum_convert_fusion.codes, bf16[4112,128]{1,0:T(8,128)(2,1)S(1)} %get-tuple-element.30.refs_0_, bf16[4112,128]{1,0:T(8,128)(2,1)S(1)} %copy-done.2, ...), custom_call_target="tpu_custom_call" | custom-call | flops 1000000000 | bytes 16000000 | tf_op jit(solution)/shard_map/pallas_call | solution.py:186
  169.1 2.0 collective-permute-start.21
  171.3 3.5 %collective-permute-done.40 = bf16[1024,128]{1,0:T(8,128)(2,1)S(1)} collective-permute-done((bf16[1024,128]{1,0:T(8,128)(2,1)S(1)}, bf16[1024,128]{1,0:T(8,128)(2,1)S(1)}, u32[]{:S(2)}, u32[]{:S(2)}) %collective-permute-start.40) | collective-permute-done | bytes 262176 | tf_op jit(solution)/shard_map/ppermute | solution.py:53
  177.0 10.0 %all-to-all-start.1 = ((bf16[128,4,256]{2,1,0:T(4,128)(2,1)}), bf16[128,4,256]{2,1,0:T(4,128)(2,1)S(1)}, u32[]{:S(2)}, u32[]{:S(2)}) async-start(bf16[128,4,256]{2,1,0:T(4,128)(2,1)} %reshape.46), calls=%async_computation.1 | async-start | bytes 524288 | tf_op jit(solution)/shard_map/all_to_all | solution.py:59
  188.0 10.1 %all-to-all-done.1 = bf16[128,4,256]{2,1,0:T(4,128)(2,1)S(1)} async-done(((bf16[128,4,256]{2,1,0:T(4,128)(2,1)}), bf16[128,4,256]{2,1,0:T(4,128)(2,1)S(1)}, u32[]{:S(2)}, u32[]{:S(2)}) %all-to-all-start.1) | async-done | bytes 262176 | tf_op jit(solution)/shard_map/all_to_all | solution.py:59
  (123 shorter events, 36.4 us)
Async XLA Ops:
  7.9 56.3 %collective-permute-start.2 = (bf16[4112,128]{1,0:T(8,128)(2,1)}, bf16[4112,128]{1,0:T(8,128)(2,1)}, u32[]{:S(2)}, u32[]{:S(2)}) collective-permute-start(bf16[4112,128]{1,0:T(8,128)(2,1)} %get-tuple-element.33), channel_id=1, source_target_pairs={{0,6},{1,7},{2,0},{3,1},{4,2},{5,3},{6,4},{7,5},{8,14},{9,15},{10,... | collective-permute-start | bytes 3158024 | tf_op jit(solution)/shard_map/ppermute | solution.py:53
  11.5 56.9 %collective-permute-start.1 = (bf16[4112,128]{1,0:T(8,128)(2,1)}, bf16[4112,128]{1,0:T(8,128)(2,1)}, u32[]{:S(2)}, u32[]{:S(2)}) collective-permute-start(bf16[4112,128]{1,0:T(8,128)(2,1)} %get-tuple-element.32), channel_id=1, source_target_pairs={{0,4},{1,5},{2,6},{3,7},{4,0},{5,1},{6,2},{7,3},{8,12},{9,13},{10,... | collective-permute-start | bytes 3158024 | tf_op jit(solution)/shard_map/ppermute | solution.py:53
  11.8 57.3 %collective-permute-start = (bf16[4112,128]{1,0:T(8,128)(2,1)}, bf16[4112,128]{1,0:T(8,128)(2,1)S(1)}, u32[]{:S(2)}, u32[]{:S(2)}) collective-permute-start(bf16[4112,128]{1,0:T(8,128)(2,1)} %get-tuple-element.31), channel_id=1, source_target_pairs={{0,2},{1,3},{2,4},{3,5},{4,6},{5,7},{6,0},{7,1},{8,10},{9,11},{10,... | collective-permute-start | bytes 3158024 | tf_op jit(solution)/shard_map/ppermute | solution.py:53
  12.6 57.2 %collective-permute-start.23 = (bf16[1024,128]{1,0:T(8,128)(2,1)S(1)}, bf16[1024,128]{1,0:T(8,128)(2,1)S(1)}, u32[]{:S(2)}, u32[]{:S(2)}) collective-permute-start(bf16[1024,128]{1,0:T(8,128)(2,1)S(1)} %bitcast.42), channel_id=1, source_target_pairs={{0,2},{1,3},{2,4},{3,5},{4,6},{5,7},{6,0},{7,1},{8,10},{9,11},{10,... | collective-permute-start | bytes 786440 | tf_op jit(solution)/shard_map/ppermute | solution.py:53
  14.4 58.8 %collective-permute-start.24 = (bf16[1024,128]{1,0:T(8,128)(2,1)S(1)}, bf16[1024,128]{1,0:T(8,128)(2,1)}, u32[]{:S(2)}, u32[]{:S(2)}) collective-permute-start(bf16[1024,128]{1,0:T(8,128)(2,1)S(1)} %bitcast.43), channel_id=1, source_target_pairs={{0,4},{1,5},{2,6},{3,7},{4,0},{5,1},{6,2},{7,3},{8,12},{9,13},{10,... | collective-permute-start | bytes 786440 | tf_op jit(solution)/shard_map/ppermute | solution.py:53
  17.2 66.3 %all-to-all-start = ((bf16[128,4,256]{2,1,0:T(4,128)(2,1)}), bf16[128,4,256]{2,1,0:T(4,128)(2,1)}, u32[]{:S(2)}, u32[]{:S(2)}) async-start(bf16[128,4,256]{2,1,0:T(4,128)(2,1)} %reshape.42), calls=%async_computation | async-start | bytes 524288 | tf_op jit(solution)/shard_map/all_to_all | solution.py:59
  81.5 11.2 %collective-permute-start.27 = (bf16[1024,128]{1,0:T(8,128)(2,1)}, bf16[1024,128]{1,0:T(8,128)(2,1)}, u32[]{:S(2)}, u32[]{:S(2)}) collective-permute-start(bf16[1024,128]{1,0:T(8,128)(2,1)} %get-tuple-element.45), channel_id=1, source_target_pairs={{0,1},{1,0},{2,3},{3,2},{4,5},{5,4},{6,7},{7,6},{8,9},{9,8},{10,11... | collective-permute-start | bytes 786440 | tf_op jit(solution)/shard_map/ppermute | solution.py:53
  86.2 11.2 %collective-permute-start.3 = (bf16[512,256]{1,0:T(8,128)(2,1)S(1)}, bf16[512,256]{1,0:T(8,128)(2,1)S(1)}, u32[]{:S(2)}, u32[]{:S(2)}) collective-permute-start(bf16[512,256]{1,0:T(8,128)(2,1)S(1)} %shard_map.105.refs_4_), channel_id=1, source_target_pairs={{0,8},{1,9},{2,10},{3,11},{4,12},{5,13},{6,14},{7,15},{8,16},{9,17... | collective-permute-start | bytes 786440 | tf_op jit(solution)/shard_map/ppermute | solution.py:53
  89.4 14.6 %collective-permute-start.4 = (bf16[512,256]{1,0:T(8,128)(2,1)S(1)}, bf16[512,256]{1,0:T(8,128)(2,1)S(1)}, u32[]{:S(2)}, u32[]{:S(2)}) collective-permute-start(bf16[512,256]{1,0:T(8,128)(2,1)S(1)} %shard_map.105.refs_4_), channel_id=1, source_target_pairs={{0,16},{1,17},{2,18},{3,19},{4,20},{5,21},{6,22},{7,23},{8,24},{9,... | collective-permute-start | bytes 786440 | tf_op jit(solution)/shard_map/ppermute | solution.py:53
  92.0 12.1 %collective-permute-start.5 = (bf16[512,256]{1,0:T(8,128)(2,1)S(1)}, bf16[512,256]{1,0:T(8,128)(2,1)S(1)}, u32[]{:S(2)}, u32[]{:S(2)}) collective-permute-start(bf16[512,256]{1,0:T(8,128)(2,1)S(1)} %shard_map.105.refs_4_), channel_id=1, source_target_pairs={{0,24},{1,25},{2,26},{3,27},{4,28},{5,29},{6,30},{7,31},{8,0},{9,1... | collective-permute-start | bytes 786440 | tf_op jit(solution)/shard_map/ppermute | solution.py:53
  94.9 14.8 %collective-permute-start.28 = (bf16[1024,128]{1,0:T(8,128)(2,1)S(1)}, bf16[1024,128]{1,0:T(8,128)(2,1)S(1)}, u32[]{:S(2)}, u32[]{:S(2)}) collective-permute-start(bf16[1024,128]{1,0:T(8,128)(2,1)S(1)} %add_convert_fusion.5), channel_id=1, source_target_pairs={{0,16},{1,17},{2,18},{3,19},{4,20},{5,21},{6,22},{7,23},{8,24},{9,... | collective-permute-start | bytes 786440 | tf_op jit(solution)/shard_map/ppermute | solution.py:53
  97.5 17.4 %collective-permute-start.30 = (bf16[1024,128]{1,0:T(8,128)(2,1)S(1)}, bf16[1024,128]{1,0:T(8,128)(2,1)S(1)}, u32[]{:S(2)}, u32[]{:S(2)}) collective-permute-start(bf16[1024,128]{1,0:T(8,128)(2,1)S(1)} %add_convert_fusion.4), channel_id=1, source_target_pairs={{0,24},{1,25},{2,26},{3,27},{4,28},{5,29},{6,30},{7,31},{8,0},{9,1... | collective-permute-start | bytes 786440 | tf_op jit(solution)/shard_map/ppermute | solution.py:53
  104.1 11.6 %collective-permute-start.32 = (bf16[1024,128]{1,0:T(8,128)(2,1)S(1)}, bf16[1024,128]{1,0:T(8,128)(2,1)S(1)}, u32[]{:S(2)}, u32[]{:S(2)}) collective-permute-start(bf16[1024,128]{1,0:T(8,128)(2,1)S(1)} %add_convert_fusion.3), channel_id=1, source_target_pairs={{0,8},{1,9},{2,10},{3,11},{4,12},{5,13},{6,14},{7,15},{8,16},{9,17... | collective-permute-start | bytes 786440 | tf_op jit(solution)/shard_map/ppermute | solution.py:53
  104.1 12.0 %collective-permute-start.6 = (bf16[512,256]{1,0:T(8,128)(2,1)S(1)}, bf16[512,256]{1,0:T(8,128)(2,1)S(1)}, u32[]{:S(2)}, u32[]{:S(2)}) collective-permute-start(bf16[512,256]{1,0:T(8,128)(2,1)S(1)} %shard_map.105.refs_4_), channel_id=1, source_target_pairs={{0,1},{1,0},{2,3},{3,2},{4,5},{5,4},{6,7},{7,6},{8,9},{9,8},{10,11... | collective-permute-start | bytes 786440 | tf_op jit(solution)/shard_map/ppermute | solution.py:53
  105.3 13.6 %collective-permute-start.7 = (bf16[512,256]{1,0:T(8,128)(2,1)S(1)}, bf16[512,256]{1,0:T(8,128)(2,1)S(1)}, u32[]{:S(2)}, u32[]{:S(2)}) collective-permute-start(bf16[512,256]{1,0:T(8,128)(2,1)S(1)} %collective-permute-done.3.refs_5_), channel_id=1, source_target_pairs={{0,1},{1,0},{2,3},{3,2},{4,5},{5,4},{6,7},{7,6},{8,9},{9,8},{10,11... | collective-permute-start | bytes 786440 | tf_op jit(solution)/shard_map/ppermute | solution.py:53
  115.9 10.6 %collective-permute-start.33 = (bf16[1024,128]{1,0:T(8,128)(2,1)S(1)}, bf16[1024,128]{1,0:T(8,128)(2,1)S(1)}, u32[]{:S(2)}, u32[]{:S(2)}) collective-permute-start(bf16[1024,128]{1,0:T(8,128)(2,1)S(1)} %fusion.3.refs_4_), channel_id=1, source_target_pairs={{0,2},{1,3},{2,4},{3,5},{4,6},{5,7},{6,0},{7,1},{8,10},{9,11},{10,... | collective-permute-start | bytes 786440 | tf_op jit(solution)/shard_map/ppermute | solution.py:53
  116.0 14.4 %collective-permute-start.34 = (bf16[1024,128]{1,0:T(8,128)(2,1)S(1)}, bf16[1024,128]{1,0:T(8,128)(2,1)S(1)}, u32[]{:S(2)}, u32[]{:S(2)}) collective-permute-start(bf16[1024,128]{1,0:T(8,128)(2,1)S(1)} %fusion.3.refs_4_), channel_id=1, source_target_pairs={{0,4},{1,5},{2,6},{3,7},{4,0},{5,1},{6,2},{7,3},{8,12},{9,13},{10,... | collective-permute-start | bytes 786440 | tf_op jit(solution)/shard_map/ppermute | solution.py:53
  118.9 11.8 %collective-permute-start.35 = (bf16[1024,128]{1,0:T(8,128)(2,1)S(1)}, bf16[1024,128]{1,0:T(8,128)(2,1)S(1)}, u32[]{:S(2)}, u32[]{:S(2)}) collective-permute-start(bf16[1024,128]{1,0:T(8,128)(2,1)S(1)} %fusion.3.refs_4_), channel_id=1, source_target_pairs={{0,6},{1,7},{2,0},{3,1},{4,2},{5,3},{6,4},{7,5},{8,14},{9,15},{10,... | collective-permute-start | bytes 786440 | tf_op jit(solution)/shard_map/ppermute | solution.py:53
  123.0 14.8 %collective-permute-start.10 = (bf16[512,256]{1,0:T(8,128)(2,1)S(1)}, bf16[512,256]{1,0:T(8,128)(2,1)S(1)}, u32[]{:S(2)}, u32[]{:S(2)}) collective-permute-start(bf16[512,256]{1,0:T(8,128)(2,1)S(1)} %get-tuple-element.35), channel_id=1, source_target_pairs={{0,4},{1,5},{2,6},{3,7},{4,0},{5,1},{6,2},{7,3},{8,12},{9,13},{10,... | collective-permute-start | bytes 786440 | tf_op jit(solution)/shard_map/ppermute | solution.py:53
  125.2 16.7 %collective-permute-start.11 = (bf16[512,256]{1,0:T(8,128)(2,1)S(1)}, bf16[512,256]{1,0:T(8,128)(2,1)S(1)}, u32[]{:S(2)}, u32[]{:S(2)}) collective-permute-start(bf16[512,256]{1,0:T(8,128)(2,1)S(1)} %get-tuple-element.36), channel_id=1, source_target_pairs={{0,6},{1,7},{2,0},{3,1},{4,2},{5,3},{6,4},{7,5},{8,14},{9,15},{10,... | collective-permute-start | bytes 786440 | tf_op jit(solution)/shard_map/ppermute | solution.py:53
  126.6 15.9 %collective-permute-start.12 = (bf16[512,256]{1,0:T(8,128)(2,1)S(1)}, bf16[512,256]{1,0:T(8,128)(2,1)S(1)}, u32[]{:S(2)}, u32[]{:S(2)}) collective-permute-start(bf16[512,256]{1,0:T(8,128)(2,1)S(1)} %get-tuple-element.37), channel_id=1, source_target_pairs={{0,2},{1,3},{2,4},{3,5},{4,6},{5,7},{6,0},{7,1},{8,10},{9,11},{10,... | collective-permute-start | bytes 786440 | tf_op jit(solution)/shard_map/ppermute | solution.py:53
  135.4 13.8 %collective-permute-start.37 = (bf16[1024,128]{1,0:T(8,128)(2,1)S(1)}, bf16[1024,128]{1,0:T(8,128)(2,1)S(1)}, u32[]{:S(2)}, u32[]{:S(2)}) collective-permute-start(bf16[1024,128]{1,0:T(8,128)(2,1)S(1)} %get-tuple-element.53), channel_id=1, source_target_pairs={{0,1},{1,0},{2,3},{3,2},{4,5},{5,4},{6,7},{7,6},{8,9},{9,8},{10,11... | collective-permute-start | bytes 786440 | tf_op jit(solution)/shard_map/ppermute | solution.py:53
  144.1 13.1 %collective-permute-start.14 = (bf16[512,256]{1,0:T(8,128)(2,1)S(1)}, bf16[512,256]{1,0:T(8,128)(2,1)S(1)}, u32[]{:S(2)}, u32[]{:S(2)}) collective-permute-start(bf16[512,256]{1,0:T(8,128)(2,1)S(1)} %add_convert_fusion.6.refs_4_), channel_id=1, source_target_pairs={{0,16},{1,17},{2,18},{3,19},{4,20},{5,21},{6,22},{7,23},{8,24},{9,... | collective-permute-start | bytes 786440 | tf_op jit(solution)/shard_map/ppermute | solution.py:53
  146.2 12.9 %collective-permute-start.15 = (bf16[512,256]{1,0:T(8,128)(2,1)S(1)}, bf16[512,256]{1,0:T(8,128)(2,1)S(1)}, u32[]{:S(2)}, u32[]{:S(2)}) collective-permute-start(bf16[512,256]{1,0:T(8,128)(2,1)S(1)} %add_convert_fusion.6.refs_4_), channel_id=1, source_target_pairs={{0,24},{1,25},{2,26},{3,27},{4,28},{5,29},{6,30},{7,31},{8,0},{9,1... | collective-permute-start | bytes 786440 | tf_op jit(solution)/shard_map/ppermute | solution.py:53
  147.9 11.2 %collective-permute-start.39 = (bf16[1024,128]{1,0:T(8,128)(2,1)S(1)}, bf16[1024,128]{1,0:T(8,128)(2,1)S(1)}, u32[]{:S(2)}, u32[]{:S(2)}) collective-permute-start(bf16[1024,128]{1,0:T(8,128)(2,1)S(1)} %get-tuple-element.55), channel_id=1, source_target_pairs={{0,1},{1,0},{2,3},{3,2},{4,5},{5,4},{6,7},{7,6},{8,9},{9,8},{10,11... | collective-permute-start | bytes 786440 | tf_op jit(solution)/shard_map/ppermute | solution.py:53
  159.9 11.2 %collective-permute-start.38 = (bf16[1024,128]{1,0:T(8,128)(2,1)S(1)}, bf16[1024,128]{1,0:T(8,128)(2,1)S(1)}, u32[]{:S(2)}, u32[]{:S(2)}) collective-permute-start(bf16[1024,128]{1,0:T(8,128)(2,1)S(1)} %add_convert_fusion.2), channel_id=1, source_target_pairs={{0,16},{1,17},{2,18},{3,19},{4,20},{5,21},{6,22},{7,23},{8,24},{9,... | collective-permute-start | bytes 786440 | tf_op jit(solution)/shard_map/ppermute | solution.py:53
  162.8 11.9 %collective-permute-start.40 = (bf16[1024,128]{1,0:T(8,128)(2,1)S(1)}, bf16[1024,128]{1,0:T(8,128)(2,1)S(1)}, u32[]{:S(2)}, u32[]{:S(2)}) collective-permute-start(bf16[1024,128]{1,0:T(8,128)(2,1)S(1)} %add_convert_fusion.1), channel_id=1, source_target_pairs={{0,24},{1,25},{2,26},{3,27},{4,28},{5,29},{6,30},{7,31},{8,0},{9,1... | collective-permute-start | bytes 786440 | tf_op jit(solution)/shard_map/ppermute | solution.py:53
  163.5 11.8 %collective-permute-start.42 = (bf16[1024,128]{1,0:T(8,128)(2,1)S(1)}, bf16[1024,128]{1,0:T(8,128)(2,1)S(1)}, u32[]{:S(2)}, u32[]{:S(2)}) collective-permute-start(bf16[1024,128]{1,0:T(8,128)(2,1)S(1)} %add_convert_fusion), channel_id=1, source_target_pairs={{0,8},{1,9},{2,10},{3,11},{4,12},{5,13},{6,14},{7,15},{8,16},{9,17... | collective-permute-start | bytes 786440 | tf_op jit(solution)/shard_map/ppermute | solution.py:53
  169.1 17.9 %collective-permute-start.20 = (bf16[512,256]{1,0:T(8,128)(2,1)}, bf16[512,256]{1,0:T(8,128)(2,1)S(1)}, u32[]{:S(2)}, u32[]{:S(2)}) collective-permute-start(bf16[512,256]{1,0:T(8,128)(2,1)} %get-tuple-element.39), channel_id=1, source_target_pairs={{0,4},{1,5},{2,6},{3,7},{4,0},{5,1},{6,2},{7,3},{8,12},{9,13},{10,... | collective-permute-start | bytes 786440 | tf_op jit(solution)/shard_map/ppermute | solution.py:53
  169.1 17.9 %collective-permute-start.21 = (bf16[512,256]{1,0:T(8,128)(2,1)}, bf16[512,256]{1,0:T(8,128)(2,1)S(1)}, u32[]{:S(2)}, u32[]{:S(2)}) collective-permute-start(bf16[512,256]{1,0:T(8,128)(2,1)} %get-tuple-element.40), channel_id=1, source_target_pairs={{0,6},{1,7},{2,0},{3,1},{4,2},{5,3},{6,4},{7,5},{8,14},{9,15},{10,... | collective-permute-start | bytes 786440 | tf_op jit(solution)/shard_map/ppermute | solution.py:53
  171.1 16.0 %collective-permute-start.22 = (bf16[512,256]{1,0:T(8,128)(2,1)}, bf16[512,256]{1,0:T(8,128)(2,1)S(1)}, u32[]{:S(2)}, u32[]{:S(2)}) collective-permute-start(bf16[512,256]{1,0:T(8,128)(2,1)} %get-tuple-element.41), channel_id=1, source_target_pairs={{0,2},{1,3},{2,4},{3,5},{4,6},{5,7},{6,0},{7,1},{8,10},{9,11},{10,... | collective-permute-start | bytes 786440 | tf_op jit(solution)/shard_map/ppermute | solution.py:53
  177.0 21.1 %all-to-all-start.1 = ((bf16[128,4,256]{2,1,0:T(4,128)(2,1)}), bf16[128,4,256]{2,1,0:T(4,128)(2,1)S(1)}, u32[]{:S(2)}, u32[]{:S(2)}) async-start(bf16[128,4,256]{2,1,0:T(4,128)(2,1)} %reshape.46), calls=%async_computation.1 | async-start | bytes 524288 | tf_op jit(solution)/shard_map/all_to_all | solution.py:59
  (29 other events, 240.8 us)

commit v2 on v1

--- a/solution.py
+++ b/solution.py
@@ -155,80 +155,60 @@
     return (most + 1) // 2
 
 
-def forward_kernel(codes, *refs):
+def product_kernel(codes, *refs):
     tiles, refs = refs[:SIDE], refs[SIDE:]
     shards, refs = refs[: CORES * SIDE], refs[CORES * SIDE :]
-    outs, (features, *totals) = refs[:SIDE], refs[SIDE:]
+    turned, refs = refs[:SIDE], refs[SIDE:]
+    rows_out, refs = refs[:SIDE], refs[SIDE:]
+    columns_out, (features, columns, *rows) = refs[: CORES * SIDE], refs[CORES * SIDE :]
     for j in range(CORES * SIDE):
         features[j * NODES : (j + 1) * NODES, :] = shards[j][...]
+    columns[...] = jnp.zeros(columns.shape, F32)
     for k in range(SIDE):
-        totals[k][...] = jnp.zeros((NODES, WIDTH), F32)
+        rows[k][...] = jnp.zeros((NODES, WIDTH), F32)
 
     def step(i, carry):
         for u in range(2):
             n = i * 2 + u
             for k in range(SIDE):
                 code = codes[k * TILE + n]
-                row = pl.multiple_of((code // COLUMNS) * TILE, TILE)
-                column = pl.multiple_of((code % COLUMNS) * TILE, TILE)
+                row, column = code // COLUMNS, code % COLUMNS
                 tile = tiles[k][pl.ds(pl.multiple_of(n * TILE, TILE), TILE), :]
-                block = features[pl.ds(column, TILE), :]
-                totals[k][pl.ds(row, TILE), :] += jnp.dot(tile, block, preferred_element_type=F32)
+                block = features[pl.ds(pl.multiple_of(column * TILE, TILE), TILE), :]
+                to = pl.ds(pl.multiple_of(row * TILE, TILE), TILE)
+                rows[k][to, :] += jnp.dot(tile, block, preferred_element_type=F32)
+                block = turned[k][pl.ds(pl.multiple_of(row * WIDTH, WIDTH), WIDTH), :]
+                to = pl.ds(pl.multiple_of(column * WIDTH, WIDTH), WIDTH)
+                columns[to, :] += jnp.dot(block, tile, preferred_element_type=F32)
         return carry
 
     lax.fori_loop(0, slot_steps(codes), step, 0)
     for k in range(SIDE):
-        outs[k][...] = totals[k][...].astype(outs[k].dtype)
-
-
-def forward_product(packs, codes, shards):
-    shape = (NODES, WIDTH)
-    return pl.pallas_call(
-        forward_kernel,
-        out_shape=[struct(shape, F32)] + [struct(shape, BF16)] * (SIDE - 1),
-        in_specs=[SCALARS] + [WHOLE] * (SIDE + CORES * SIDE),
-        out_specs=[WHOLE] * SIDE,
-        scratch_shapes=[pltpu.VMEM((CORES * SIDE * NODES, WIDTH), BF16)]
-        + [pltpu.VMEM(shape, F32)] * SIDE,
+        rows_out[k][...] = rows[k][...].astype(rows_out[k].dtype)
+    for j in range(CORES * SIDE):
+        part = columns[j * TURNED : (j + 1) * TURNED, :]
+        columns_out[j][...] = part.astype(columns_out[j].dtype)
+
+
+def products(packs, codes, shards, turned):
+    plain, flipped = (NODES, WIDTH), (TURNED, TILE)
+    outs = pl.pallas_call(
+        product_kernel,
+        out_shape=[struct(plain, F32)]
+        + [struct(plain, BF16)] * (SIDE - 1)
+        + [struct(flipped, F32)] * SIDE
+        + [struct(flipped, BF16)] * SIDE,
+        in_specs=[SCALARS] + [WHOLE] * (2 * SIDE + CORES * SIDE),
+        out_specs=[WHOLE] * (SIDE + CORES * SIDE),
+        scratch_shapes=[
+            pltpu.VMEM((CORES * SIDE * NODES, WIDTH), BF16),
+            pltpu.VMEM((CORES * SIDE * TURNED, TILE), F32),
+        ]
+        + [pltpu.VMEM(plain, F32)] * SIDE,
         compiler_params=params(),
-        cost_estimate=cost(1e9, 16e6),
-    )(codes, *packs, *shards)
-
-
-def backward_kernel(codes, *refs):
-    tiles, refs = refs[:SIDE], refs[SIDE:]
-    shards, refs = refs[:SIDE], refs[SIDE:]
-    outs, (totals,) = refs[: CORES * SIDE], refs[CORES * SIDE :]
-    totals[...] = jnp.zeros(totals.shape, F32)
-
-    def step(i, carry):
-        for u in range(2):
-            n = i * 2 + u
-            for k in range(SIDE):
-                code = codes[k * TILE + n]
-                row = pl.multiple_of((code // COLUMNS) * WIDTH, WIDTH)
-                column = pl.multiple_of((code % COLUMNS) * WIDTH, WIDTH)
-                tile = tiles[k][pl.ds(pl.multiple_of(n * TILE, TILE), TILE), :]
-                block = shards[k][pl.ds(row, WIDTH), :]
-                totals[pl.ds(column, WIDTH), :] += jnp.dot(block, tile, preferred_element_type=F32)
-        return carry
-
-    lax.fori_loop(0, slot_steps(codes), step, 0)
-    for j in range(CORES * SIDE):
-        outs[j][...] = totals[j * TURNED : (j + 1) * TURNED, :].astype(outs[j].dtype)
-
-
-def backward_product(packs, codes, shards):
-    shape = (TURNED, TILE)
-    return pl.pallas_call(
-        backward_kernel,
-        out_shape=[struct(shape, F32)] * SIDE + [struct(shape, BF16)] * SIDE,
-        in_specs=[SCALARS] + [WHOLE] * (2 * SIDE),
-        out_specs=[WHOLE] * (CORES * SIDE),
-        scratch_shapes=[pltpu.VMEM((CORES * SIDE * TURNED, TILE), F32)],
-        compiler_params=params(),
-        cost_estimate=cost(1e9, 16e6),
-    )(codes, *packs, *shards)
+        cost_estimate=cost(3e9, 16e6),
+    )(codes, *packs, *shards, *turned)
+    return outs[:SIDE], outs[SIDE:]
 
 
 ORDER = (2, 1, 3)
@@ -287,7 +267,10 @@
     side = (owner + core) % CORES
     column = (side * SIDE + back_x) * BLOCKS + tile_sub
     target = jnp.where(live, far_y, SIDE)
+    turned = cotangent.reshape(BLOCKS, TILE, WIDTH).transpose(0, 2, 1).reshape(TURNED, TILE)
+    gradients = gather_line(turned, "y")
     packs = bucket(tile_values, target, tile_row * COLUMNS + column)
+    packs, gradients = lax.optimization_barrier((packs, gradients))
     moved = {d: move(packs[d], "y", d) for d in ORDER}
     packs = [packs[0]] + [moved[d] for d in range(1, SIDE)]
     codes = jnp.concatenate([pack[CAP * TILE] for pack in packs]).astype(jnp.int32)
@@ -296,18 +279,14 @@
     incoming = reshuffle(permute_call(order_kernel, hash_target, embeddings))
     initial = permute_call(restore_kernel, part_key, incoming)
 
-    def spread(features):
-        return scatter_forward(forward_product(packs, codes, gather_forward(features)))
-
-    def collect(gradient):
-        return scatter_backward(backward_product(packs, codes, gather_line(gradient, "y")))
-
-    turned = cotangent.reshape(BLOCKS, TILE, WIDTH).transpose(0, 2, 1).reshape(TURNED, TILE)
-    back_one = collect(turned)
-    layer_one = spread(initial).astype(BF16)
+    rows, columns = products(packs, codes, gather_forward(initial), gradients)
+    layer_one = scatter_forward(rows).astype(BF16)
+    back_one = scatter_backward(columns)
     middle = ((turned.astype(F32) + back_one) / 3.0).astype(BF16)
-    back_zero = collect(middle)
-    layer_two = spread(layer_one)
+    gradients = gather_line(middle, "y")
+    rows, columns = products(packs, codes, gather_forward(layer_one), gradients)
+    back_zero = scatter_backward(columns)
+    layer_two = scatter_forward(rows)
     grad_part = (turned.astype(F32) / 3.0 + back_zero).astype(BF16)
     returned = reshuffle(permute_call(order_turned_kernel, part_key, grad_part))
     embed_grad = permute_call(restore_kernel, hash_target, returned)

time: 201 us -> 214 us (1.065)
  waiting for transfers between devices: 83.8 us -> 110 us
  starting transfers between devices: 74.9 us -> 63.2 us
  local copies, waits for them, and re-layouts: 7.44 us -> 5.25 us
    all_to_all x2, waiting for transfers between devices: 10.1 us -> 50.1 us  [reshuffle(): lax.all_to_all(direct, ('row', 'col'), split_axis=0, concat_axis=0, tiled...]
    ppermute x43, waiting for transfers between devices: 73.7 us -> 59.5 us  [move(): return lax.ppermute(array, 'col', pairs)]
    ppermute x43, starting transfers between devices: 53.8 us -> 47.9 us  [move(): return lax.ppermute(array, 'col', pairs)]
    all_to_all x2, starting transfers between devices: 21.1 us -> 15.3 us  [reshuffle(): lax.all_to_all(direct, ('row', 'col'), split_axis=0, concat_axis=0, tiled...]
    unnamed x32 -> x18, local copies, waits for them, and re-layouts: 3.02 us -> 0.17 us
    pallas_call x4 -> x2, Pallas kernels: 18.9 us -> 18.6 us  [products(): pl.pallas_call(product_kernel, out_shape=[struct(plain, F32)] + [struct(p...]
  transfers between devices with their start and end apart: 45 -> 45, of which waited for: 16 -> 19; matrix products, arithmetic and copies ran while one was open for 4% -> 4% of each run, Pallas kernels for 10% -> 4%
where the time goes in v2:
time: 214 us; the launch traced here: 212 us
  waiting for transfers between devices  110 us (51%)
  starting transfers between devices  63.2 us (30%)
  Pallas kernels  27.6 us (13%)
  local copies, waits for them, and re-layouts  5.25 us (2%)
  other arithmetic  4.65 us (2%)
    ppermute x43, waiting for transfers between devices, move(): return lax.ppermute(array, 'col', pairs)  59.5 us
    all_to_all x2, waiting for transfers between devices, reshuffle(): lax.all_to_all(direct, ('row', 'col'), split_axis=0, concat_axis=0, tiled...  50.1 us
    ppermute x43, starting transfers between devices, move(): return lax.ppermute(array, 'col', pairs)  47.9 us
    pallas_call x2, Pallas kernels, products(): pl.pallas_call(product_kernel, out_shape=[struct(plain, F32)] + [struct(p...  18.6 us
    all_to_all x2, starting transfers between devices, reshuffle(): lax.all_to_all(direct, ('row', 'col'), split_axis=0, concat_axis=0, tiled...  15.3 us
    pallas_call x1, Pallas kernels, bucket(): pl.pallas_call(bucket_kernel, out_shape=[struct((PACKED, TILE), BF16)] *...  5.77 us
  transfers between devices with their start and end apart: 45, of which 19 were waited for; matrix products, arithmetic and copies ran while one was open for 4% of the time, Pallas kernels for 4%

profile of v2, /device:TPU:1, one launch (start us, length us, event | category | flops | bytes accessed | tf_op | source)
XLA Modules:
  0.0 211.9 jit_solution(5824909267813347737)
XLA Ops:
  1.8 3.6 %collective-permute-start.2 = (bf16[1024,128]{1,0:T(8,128)(2,1)S(1)}, bf16[1024,128]{1,0:T(8,128)(2,1)S(1)}, u32[]{:S(2)}, u32[]{:S(2)}) collective-permute-start(bf16[1024,128]{1,0:T(8,128)(2,1)S(1)} %bitcast.42), channel_id=1, source_target_pairs={{0,6},{1,7},{2,0},{3,1},{4,2},{5,3},{6,4},{7,5},{8,14},{9,15},{10,... | collective-permute-start | bytes 786440 | tf_op jit(solution)/shard_map/ppermute | solution.py:53
  7.8 5.8 %shard_map.106 = (bf16[4112,128]{1,0:T(8,128)(2,1)S(1)}, bf16[4112,128]{1,0:T(8,128)(2,1)}, bf16[4112,128]{1,0:T(8,128)(2,1)}, bf16[4112,128]{1,0:T(8,128)(2,1)}) custom-call(s32[96]{0:T(128)S(1)} %get-tuple-element.75.target, s32[96]{0:T(128)S(1)} %get-tuple-element.74.code, bf16[96,128,128]{2,1,0:T(8,128)(2,1)} %tiles.1), custom_call_target="tpu_custom_call" | custom-call | flops 1000000 | bytes 7000000 | tf_op jit(solution)/shard_map/pallas_call | solution.py:137
  13.6 2.2 %collective-permute-done.2.refs_15_ = bf16[1024,128]{1,0:T(8,128)(2,1)S(1)} collective-permute-done((bf16[1024,128]{1,0:T(8,128)(2,1)S(1)}, bf16[1024,128]{1,0:T(8,128)(2,1)S(1)}, u32[]{:S(2)}, u32[]{:S(2)}) %collective-permute-start.2) | collective-permute-done | bytes 262176 | tf_op jit(solution)/shard_map/ppermute | solution.py:53
  15.8 4.9 %collective-permute-done.refs_13_ = bf16[1024,128]{1,0:T(8,128)(2,1)S(1)} collective-permute-done((bf16[1024,128]{1,0:T(8,128)(2,1)S(1)}, bf16[1024,128]{1,0:T(8,128)(2,1)S(1)}, u32[]{:S(2)}, u32[]{:S(2)}) %collective-permute-start) | collective-permute-done | bytes 262176 | tf_op jit(solution)/shard_map/ppermute | solution.py:53
  21.2 2.2 %collective-permute-start.5 = (bf16[4112,128]{1,0:T(8,128)(2,1)}, bf16[4112,128]{1,0:T(8,128)(2,1)}, u32[]{:S(2)}, u32[]{:S(2)}) collective-permute-start(bf16[4112,128]{1,0:T(8,128)(2,1)} %get-tuple-element.45), channel_id=1, source_target_pairs={{0,6},{1,7},{2,0},{3,1},{4,2},{5,3},{6,4},{7,5},{8,14},{9,15},{10,... | collective-permute-start | bytes 3158024 | tf_op jit(solution)/shard_map/ppermute | solution.py:53
  24.8 10.8 %all-to-all-start = ((bf16[128,4,256]{2,1,0:T(4,128)(2,1)}), bf16[128,4,256]{2,1,0:T(4,128)(2,1)S(1)}, u32[]{:S(2)}, u32[]{:S(2)}) async-start(bf16[128,4,256]{2,1,0:T(4,128)(2,1)} %reshape.42), calls=%async_computation | async-start | bytes 524288 | tf_op jit(solution)/shard_map/all_to_all | solution.py:59
  35.8 40.9 %all-to-all-done = bf16[128,4,256]{2,1,0:T(4,128)(2,1)S(1)} async-done(((bf16[128,4,256]{2,1,0:T(4,128)(2,1)}), bf16[128,4,256]{2,1,0:T(4,128)(2,1)S(1)}, u32[]{:S(2)}, u32[]{:S(2)}) %all-to-all-start) | async-done | bytes 262176 | tf_op jit(solution)/shard_map/all_to_all | solution.py:59
  77.5 2.5 %collective-permute-start.8 = (bf16[512,256]{1,0:T(8,128)(2,1)S(1)}, bf16[512,256]{1,0:T(8,128)(2,1)S(1)}, u32[]{:S(2)}, u32[]{:S(2)}) collective-permute-start(bf16[512,256]{1,0:T(8,128)(2,1)S(1)} %shard_map.105.refs_4_), channel_id=1, source_target_pairs={{0,24},{1,25},{2,26},{3,27},{4,28},{5,29},{6,30},{7,31},{8,0},{9,1... | collective-permute-start | bytes 786440 | tf_op jit(solution)/shard_map/ppermute | solution.py:53
  81.8 4.2 %collective-permute-done.8.refs_7_ = bf16[512,256]{1,0:T(8,128)(2,1)S(1)} collective-permute-done((bf16[512,256]{1,0:T(8,128)(2,1)S(1)}, bf16[512,256]{1,0:T(8,128)(2,1)S(1)}, u32[]{:S(2)}, u32[]{:S(2)}) %collective-permute-start.8) | collective-permute-done | bytes 262176 | tf_op jit(solution)/shard_map/ppermute | solution.py:53
  86.0 6.2 %collective-permute-start.9 = (bf16[512,256]{1,0:T(8,128)(2,1)S(1)}, bf16[512,256]{1,0:T(8,128)(2,1)S(1)}, u32[]{:S(2)}, u32[]{:S(2)}) collective-permute-start(bf16[512,256]{1,0:T(8,128)(2,1)S(1)} %shard_map.105.refs_4_), channel_id=1, source_target_pairs={{0,1},{1,0},{2,3},{3,2},{4,5},{5,4},{6,7},{7,6},{8,9},{9,8},{10,11... | collective-permute-start | bytes 786440 | tf_op jit(solution)/shard_map/ppermute | solution.py:53
  92.2 3.2 %collective-permute-done.6.refs_5_ = bf16[512,256]{1,0:T(8,128)(2,1)S(1)} collective-permute-done((bf16[512,256]{1,0:T(8,128)(2,1)S(1)}, bf16[512,256]{1,0:T(8,128)(2,1)S(1)}, u32[]{:S(2)}, u32[]{:S(2)}) %collective-permute-start.6) | collective-permute-done | bytes 262176 | tf_op jit(solution)/shard_map/ppermute | solution.py:53
  97.4 9.3 %shard_map.107 = (f32[512,256]{1,0:T(8,128)S(1)}, bf16[512,256]{1,0:T(8,128)(2,1)S(1)}, bf16[512,256]{1,0:T(8,128)(2,1)S(1)}, bf16[512,256]{1,0:T(8,128)(2,1)S(1...) custom-call(s32[512]{0:T(512)S(1)} %maximum_convert_fusion.codes, ...), custom_call_target="tpu_custom_call" | custom-call | flops 3000000000 | bytes 16000000 | tf_op jit(solution)/shard_map/pallas_call | solution.py:195
  107.2 2.5 %collective-permute-start.14 = (bf16[512,256]{1,0:T(8,128)(2,1)S(1)}, bf16[512,256]{1,0:T(8,128)(2,1)S(1)}, u32[]{:S(2)}, u32[]{:S(2)}) collective-permute-start(bf16[512,256]{1,0:T(8,128)(2,1)S(1)} %get-tuple-element.52), channel_id=1, source_target_pairs={{0,6},{1,7},{2,0},{3,1},{4,2},{5,3},{6,4},{7,5},{8,14},{9,15},{10,... | collective-permute-start | bytes 786440 | tf_op jit(solution)/shard_map/ppermute | solution.py:53
  110.7 5.0 %collective-permute-done.13 = bf16[512,256]{1,0:T(8,128)(2,1)S(1)} collective-permute-done((bf16[512,256]{1,0:T(8,128)(2,1)S(1)}, bf16[512,256]{1,0:T(8,128)(2,1)S(1)}, u32[]{:S(2)}, u32[]{:S(2)}) %collective-permute-start.13) | collective-permute-done | bytes 262176 | tf_op jit(solution)/shard_map/ppermute | solution.py:53
  115.7 2.1 collective-permute-start.26
  117.8 3.6 %collective-permute-done.14 = bf16[512,256]{1,0:T(8,128)(2,1)S(1)} collective-permute-done((bf16[512,256]{1,0:T(8,128)(2,1)S(1)}, bf16[512,256]{1,0:T(8,128)(2,1)S(1)}, u32[]{:S(2)}, u32[]{:S(2)}) %collective-permute-start.14) | collective-permute-done | bytes 262176 | tf_op jit(solution)/shard_map/ppermute | solution.py:53
  123.7 3.3 %collective-permute-start.27 = (bf16[1024,128]{1,0:T(8,128)(2,1)S(1)}, bf16[1024,128]{1,0:T(8,128)(2,1)S(1)}, u32[]{:S(2)}, u32[]{:S(2)}) collective-permute-start(bf16[1024,128]{1,0:T(8,128)(2,1)S(1)} %add_convert_fusion.4), channel_id=1, source_target_pairs={{0,24},{1,25},{2,26},{3,27},{4,28},{5,29},{6,30},{7,31},{8,0},{9,1... | collective-permute-start | bytes 786440 | tf_op jit(solution)/shard_map/ppermute | solution.py:53
  128.1 2.7 %collective-permute-done.18.refs_7_ = bf16[512,256]{1,0:T(8,128)(2,1)S(1)} collective-permute-done((bf16[512,256]{1,0:T(8,128)(2,1)S(1)}, bf16[512,256]{1,0:T(8,128)(2,1)S(1)}, u32[]{:S(2)}, u32[]{:S(2)}) %collective-permute-start.18) | collective-permute-done | bytes 262176 | tf_op jit(solution)/shard_map/ppermute | solution.py:53
  132.5 3.9 %collective-permute-start.16 = (bf16[512,256]{1,0:T(8,128)(2,1)S(1)}, bf16[512,256]{1,0:T(8,128)(2,1)S(1)}, u32[]{:S(2)}, u32[]{:S(2)}) collective-permute-start(bf16[512,256]{1,0:T(8,128)(2,1)S(1)} %add_convert_fusion.6.refs_4_), channel_id=1, source_target_pairs={{0,8},{1,9},{2,10},{3,11},{4,12},{5,13},{6,14},{7,15},{8,16},{9,17... | collective-permute-start | bytes 786440 | tf_op jit(solution)/shard_map/ppermute | solution.py:53
  136.4 5.7 %collective-permute-done.27 = bf16[1024,128]{1,0:T(8,128)(2,1)S(1)} collective-permute-done((bf16[1024,128]{1,0:T(8,128)(2,1)S(1)}, bf16[1024,128]{1,0:T(8,128)(2,1)S(1)}, u32[]{:S(2)}, u32[]{:S(2)}) %collective-permute-start.27) | collective-permute-done | bytes 262176 | tf_op jit(solution)/shard_map/ppermute | solution.py:53
  143.5 2.4 %collective-permute-start.32 = (bf16[1024,128]{1,0:T(8,128)(2,1)S(1)}, bf16[1024,128]{1,0:T(8,128)(2,1)S(1)}, u32[]{:S(2)}, u32[]{:S(2)}) collective-permute-start(bf16[1024,128]{1,0:T(8,128)(2,1)S(1)} %fusion.1.refs_12_), channel_id=1, source_target_pairs={{0,6},{1,7},{2,0},{3,1},{4,2},{5,3},{6,4},{7,5},{8,14},{9,15},{10,... | collective-permute-start | bytes 786440 | tf_op jit(solution)/shard_map/ppermute | solution.py:53
  146.2 3.4 %collective-permute-done.16.refs_5_ = bf16[512,256]{1,0:T(8,128)(2,1)S(1)} collective-permute-done((bf16[512,256]{1,0:T(8,128)(2,1)S(1)}, bf16[512,256]{1,0:T(8,128)(2,1)S(1)}, u32[]{:S(2)}, u32[]{:S(2)}) %collective-permute-start.16) | collective-permute-done | bytes 262176 | tf_op jit(solution)/shard_map/ppermute | solution.py:53
  151.2 1.8 collective-permute-start.30
  153.1 6.5 %collective-permute-done.31.refs_14_ = bf16[1024,128]{1,0:T(8,128)(2,1)S(1)} collective-permute-done((bf16[1024,128]{1,0:T(8,128)(2,1)S(1)}, bf16[1024,128]{1,0:T(8,128)(2,1)S(1)}, u32[]{:S(2)}, u32[]{:S(2)}) %collective-permute-start.31) | collective-permute-done | bytes 262176 | tf_op jit(solution)/shard_map/ppermute | solution.py:53
  159.6 5.9 %collective-permute-done.30.refs_13_ = bf16[1024,128]{1,0:T(8,128)(2,1)S(1)} collective-permute-done((bf16[1024,128]{1,0:T(8,128)(2,1)S(1)}, bf16[1024,128]{1,0:T(8,128)(2,1)S(1)}, u32[]{:S(2)}, u32[]{:S(2)}) %collective-permute-start.30) | collective-permute-done | bytes 262176 | tf_op jit(solution)/shard_map/ppermute | solution.py:53
  165.5 9.4 %shard_map.108 = (f32[512,256]{1,0:T(8,128)S(1)}, bf16[512,256]{1,0:T(8,128)(2,1)S(1)}, bf16[512,256]{1,0:T(8,128)(2,1)S(1)}, bf16[512,256]{1,0:T(8,128)(2,1)S(1...) custom-call(s32[512]{0:T(512)S(1)} %maximum_convert_fusion.codes, ...), custom_call_target="tpu_custom_call" | custom-call | flops 3000000000 | bytes 16000000 | tf_op jit(solution)/shard_map/pallas_call | solution.py:195
  182.8 4.0 %collective-permute-done.38 = bf16[1024,128]{1,0:T(8,128)(2,1)S(1)} collective-permute-done((bf16[1024,128]{1,0:T(8,128)(2,1)S(1)}, bf16[1024,128]{1,0:T(8,128)(2,1)S(1)}, u32[]{:S(2)}, u32[]{:S(2)}) %collective-permute-start.38) | collective-permute-done | bytes 262176 | tf_op jit(solution)/shard_map/ppermute | solution.py:53
  186.9 4.5 %collective-permute-done.40 = bf16[1024,128]{1,0:T(8,128)(2,1)S(1)} collective-permute-done((bf16[1024,128]{1,0:T(8,128)(2,1)S(1)}, bf16[1024,128]{1,0:T(8,128)(2,1)S(1)}, u32[]{:S(2)}, u32[]{:S(2)}) %collective-permute-start.40) | collective-permute-done | bytes 262176 | tf_op jit(solution)/shard_map/ppermute | solution.py:53
  191.4 1.6 collective-permute-done.42
  194.7 4.5 %all-to-all-start.1 = ((bf16[128,4,256]{2,1,0:T(4,128)(2,1)}), bf16[128,4,256]{2,1,0:T(4,128)(2,1)S(1)}, u32[]{:S(2)}, u32[]{:S(2)}) async-start(bf16[128,4,256]{2,1,0:T(4,128)(2,1)} %reshape.46), calls=%async_computation.1 | async-start | bytes 524288 | tf_op jit(solution)/shard_map/all_to_all | solution.py:59
  199.3 1.9 multiply_convert_fusion
  201.2 9.2 %all-to-all-done.1 = bf16[128,4,256]{2,1,0:T(4,128)(2,1)S(1)} async-done(((bf16[128,4,256]{2,1,0:T(4,128)(2,1)}), bf16[128,4,256]{2,1,0:T(4,128)(2,1)S(1)}, u32[]{:S(2)}, u32[]{:S(2)}) %all-to-all-start.1) | async-done | bytes 262176 | tf_op jit(solution)/shard_map/all_to_all | solution.py:59
  (107 shorter events, 30.5 us)
Async XLA Ops:
  1.8 14.1 %collective-permute-start.2 = (bf16[1024,128]{1,0:T(8,128)(2,1)S(1)}, bf16[1024,128]{1,0:T(8,128)(2,1)S(1)}, u32[]{:S(2)}, u32[]{:S(2)}) collective-permute-start(bf16[1024,128]{1,0:T(8,128)(2,1)S(1)} %bitcast.42), channel_id=1, source_target_pairs={{0,6},{1,7},{2,0},{3,1},{4,2},{5,3},{6,4},{7,5},{8,14},{9,15},{10,... | collective-permute-start | bytes 786440 | tf_op jit(solution)/shard_map/ppermute | solution.py:53
  5.4 10.5 %collective-permute-start.1 = (bf16[1024,128]{1,0:T(8,128)(2,1)S(1)}, bf16[1024,128]{1,0:T(8,128)(2,1)S(1)}, u32[]{:S(2)}, u32[]{:S(2)}) collective-permute-start(bf16[1024,128]{1,0:T(8,128)(2,1)S(1)} %bitcast.43), channel_id=1, source_target_pairs={{0,4},{1,5},{2,6},{3,7},{4,0},{5,1},{6,2},{7,3},{8,12},{9,13},{10,... | collective-permute-start | bytes 786440 | tf_op jit(solution)/shard_map/ppermute | solution.py:53
  5.7 15.0 %collective-permute-start = (bf16[1024,128]{1,0:T(8,128)(2,1)S(1)}, bf16[1024,128]{1,0:T(8,128)(2,1)S(1)}, u32[]{:S(2)}, u32[]{:S(2)}) collective-permute-start(bf16[1024,128]{1,0:T(8,128)(2,1)S(1)} %bitcast.44), channel_id=1, source_target_pairs={{0,2},{1,3},{2,4},{3,5},{4,6},{5,7},{6,0},{7,1},{8,10},{9,11},{10,... | collective-permute-start | bytes 786440 | tf_op jit(solution)/shard_map/ppermute | solution.py:53
  20.7 59.8 %collective-permute-start.3 = (bf16[4112,128]{1,0:T(8,128)(2,1)}, bf16[4112,128]{1,0:T(8,128)(2,1)}, u32[]{:S(2)}, u32[]{:S(2)}) collective-permute-start(bf16[4112,128]{1,0:T(8,128)(2,1)} %get-tuple-element.43), channel_id=1, source_target_pairs={{0,2},{1,3},{2,4},{3,5},{4,6},{5,7},{6,0},{7,1},{8,10},{9,11},{10,... | collective-permute-start | bytes 3158024 | tf_op jit(solution)/shard_map/ppermute | solution.py:53
  20.7 75.1 %collective-permute-start.4 = (bf16[4112,128]{1,0:T(8,128)(2,1)}, bf16[4112,128]{1,0:T(8,128)(2,1)}, u32[]{:S(2)}, u32[]{:S(2)}) collective-permute-start(bf16[4112,128]{1,0:T(8,128)(2,1)} %get-tuple-element.44), channel_id=1, source_target_pairs={{0,4},{1,5},{2,6},{3,7},{4,0},{5,1},{6,2},{7,3},{8,12},{9,13},{10,... | collective-permute-start | bytes 3158024 | tf_op jit(solution)/shard_map/ppermute | solution.py:53
  21.2 75.3 %collective-permute-start.5 = (bf16[4112,128]{1,0:T(8,128)(2,1)}, bf16[4112,128]{1,0:T(8,128)(2,1)}, u32[]{:S(2)}, u32[]{:S(2)}) collective-permute-start(bf16[4112,128]{1,0:T(8,128)(2,1)} %get-tuple-element.45), channel_id=1, source_target_pairs={{0,6},{1,7},{2,0},{3,1},{4,2},{5,3},{6,4},{7,5},{8,14},{9,15},{10,... | collective-permute-start | bytes 3158024 | tf_op jit(solution)/shard_map/ppermute | solution.py:53
  24.8 51.9 %all-to-all-start = ((bf16[128,4,256]{2,1,0:T(4,128)(2,1)}), bf16[128,4,256]{2,1,0:T(4,128)(2,1)S(1)}, u32[]{:S(2)}, u32[]{:S(2)}) async-start(bf16[128,4,256]{2,1,0:T(4,128)(2,1)} %reshape.42), calls=%async_computation | async-start | bytes 524288 | tf_op jit(solution)/shard_map/all_to_all | solution.py:59
  80.0 12.2 %collective-permute-start.7 = (bf16[512,256]{1,0:T(8,128)(2,1)S(1)}, bf16[512,256]{1,0:T(8,128)(2,1)S(1)}, u32[]{:S(2)}, u32[]{:S(2)}) collective-permute-start(bf16[512,256]{1,0:T(8,128)(2,1)S(1)} %shard_map.105.refs_4_), channel_id=1, source_target_pairs={{0,16},{1,17},{2,18},{3,19},{4,20},{5,21},{6,22},{7,23},{8,24},{9,... | collective-permute-start | bytes 786440 | tf_op jit(solution)/shard_map/ppermute | solution.py:53
  80.5 14.9 %collective-permute-start.6 = (bf16[512,256]{1,0:T(8,128)(2,1)S(1)}, bf16[512,256]{1,0:T(8,128)(2,1)S(1)}, u32[]{:S(2)}, u32[]{:S(2)}) collective-permute-start(bf16[512,256]{1,0:T(8,128)(2,1)S(1)} %shard_map.105.refs_4_), channel_id=1, source_target_pairs={{0,8},{1,9},{2,10},{3,11},{4,12},{5,13},{6,14},{7,15},{8,16},{9,17... | collective-permute-start | bytes 786440 | tf_op jit(solution)/shard_map/ppermute | solution.py:53
  86.0 11.2 %collective-permute-start.9 = (bf16[512,256]{1,0:T(8,128)(2,1)S(1)}, bf16[512,256]{1,0:T(8,128)(2,1)S(1)}, u32[]{:S(2)}, u32[]{:S(2)}) collective-permute-start(bf16[512,256]{1,0:T(8,128)(2,1)S(1)} %shard_map.105.refs_4_), channel_id=1, source_target_pairs={{0,1},{1,0},{2,3},{3,2},{4,5},{5,4},{6,7},{7,6},{8,9},{9,8},{10,11... | collective-permute-start | bytes 786440 | tf_op jit(solution)/shard_map/ppermute | solution.py:53
  106.6 9.0 %collective-permute-start.13 = (bf16[512,256]{1,0:T(8,128)(2,1)S(1)}, bf16[512,256]{1,0:T(8,128)(2,1)S(1)}, u32[]{:S(2)}, u32[]{:S(2)}) collective-permute-start(bf16[512,256]{1,0:T(8,128)(2,1)S(1)} %get-tuple-element.51), channel_id=1, source_target_pairs={{0,4},{1,5},{2,6},{3,7},{4,0},{5,1},{6,2},{7,3},{8,12},{9,13},{10,... | collective-permute-start | bytes 786440 | tf_op jit(solution)/shard_map/ppermute | solution.py:53
  107.2 14.2 %collective-permute-start.14 = (bf16[512,256]{1,0:T(8,128)(2,1)S(1)}, bf16[512,256]{1,0:T(8,128)(2,1)S(1)}, u32[]{:S(2)}, u32[]{:S(2)}) collective-permute-start(bf16[512,256]{1,0:T(8,128)(2,1)S(1)} %get-tuple-element.52), channel_id=1, source_target_pairs={{0,6},{1,7},{2,0},{3,1},{4,2},{5,3},{6,4},{7,5},{8,14},{9,15},{10,... | collective-permute-start | bytes 786440 | tf_op jit(solution)/shard_map/ppermute | solution.py:53
  109.6 13.0 %collective-permute-start.15 = (bf16[512,256]{1,0:T(8,128)(2,1)S(1)}, bf16[512,256]{1,0:T(8,128)(2,1)S(1)}, u32[]{:S(2)}, u32[]{:S(2)}) collective-permute-start(bf16[512,256]{1,0:T(8,128)(2,1)S(1)} %get-tuple-element.53), channel_id=1, source_target_pairs={{0,2},{1,3},{2,4},{3,5},{4,6},{5,7},{6,0},{7,1},{8,10},{9,11},{10,... | collective-permute-start | bytes 786440 | tf_op jit(solution)/shard_map/ppermute | solution.py:53
  109.7 17.5 %collective-permute-start.23 = (bf16[1024,128]{1,0:T(8,128)(2,1)S(1)}, bf16[1024,128]{1,0:T(8,128)(2,1)S(1)}, u32[]{:S(2)}, u32[]{:S(2)}) collective-permute-start(bf16[1024,128]{1,0:T(8,128)(2,1)S(1)} %get-tuple-element.55), channel_id=1, source_target_pairs={{0,1},{1,0},{2,3},{3,2},{4,5},{5,4},{6,7},{7,6},{8,9},{9,8},{10,11... | collective-permute-start | bytes 786440 | tf_op jit(solution)/shard_map/ppermute | solution.py:53
  110.7 12.2 %collective-permute-start.24 = (bf16[1024,128]{1,0:T(8,128)(2,1)S(1)}, bf16[1024,128]{1,0:T(8,128)(2,1)S(1)}, u32[]{:S(2)}, u32[]{:S(2)}) collective-permute-start(bf16[1024,128]{1,0:T(8,128)(2,1)S(1)} %get-tuple-element.57), channel_id=1, source_target_pairs={{0,1},{1,0},{2,3},{3,2},{4,5},{5,4},{6,7},{7,6},{8,9},{9,8},{10,11... | collective-permute-start | bytes 786440 | tf_op jit(solution)/shard_map/ppermute | solution.py:53
  123.0 9.5 %collective-permute-start.25 = (bf16[1024,128]{1,0:T(8,128)(2,1)S(1)}, bf16[1024,128]{1,0:T(8,128)(2,1)S(1)}, u32[]{:S(2)}, u32[]{:S(2)}) collective-permute-start(bf16[1024,128]{1,0:T(8,128)(2,1)S(1)} %add_convert_fusion.5), channel_id=1, source_target_pairs={{0,16},{1,17},{2,18},{3,19},{4,20},{5,21},{6,22},{7,23},{8,24},{9,... | collective-permute-start | bytes 786440 | tf_op jit(solution)/shard_map/ppermute | solution.py:53
  123.7 18.3 %collective-permute-start.27 = (bf16[1024,128]{1,0:T(8,128)(2,1)S(1)}, bf16[1024,128]{1,0:T(8,128)(2,1)S(1)}, u32[]{:S(2)}, u32[]{:S(2)}) collective-permute-start(bf16[1024,128]{1,0:T(8,128)(2,1)S(1)} %add_convert_fusion.4), channel_id=1, source_target_pairs={{0,24},{1,25},{2,26},{3,27},{4,28},{5,29},{6,30},{7,31},{8,0},{9,1... | collective-permute-start | bytes 786440 | tf_op jit(solution)/shard_map/ppermute | solution.py:53
  127.1 16.2 %collective-permute-start.29 = (bf16[1024,128]{1,0:T(8,128)(2,1)S(1)}, bf16[1024,128]{1,0:T(8,128)(2,1)S(1)}, u32[]{:S(2)}, u32[]{:S(2)}) collective-permute-start(bf16[1024,128]{1,0:T(8,128)(2,1)S(1)} %add_convert_fusion.3), channel_id=1, source_target_pairs={{0,8},{1,9},{2,10},{3,11},{4,12},{5,13},{6,14},{7,15},{8,16},{9,17... | collective-permute-start | bytes 786440 | tf_op jit(solution)/shard_map/ppermute | solution.py:53
  127.2 22.9 %collective-permute-start.19 = (bf16[512,256]{1,0:T(8,128)(2,1)S(1)}, bf16[512,256]{1,0:T(8,128)(2,1)S(1)}, u32[]{:S(2)}, u32[]{:S(2)}) collective-permute-start(bf16[512,256]{1,0:T(8,128)(2,1)S(1)} %add_convert_fusion.6.refs_4_), channel_id=1, source_target_pairs={{0,1},{1,0},{2,3},{3,2},{4,5},{5,4},{6,7},{7,6},{8,9},{9,8},{10,11... | collective-permute-start | bytes 786440 | tf_op jit(solution)/shard_map/ppermute | solution.py:53
  130.8 15.1 %collective-permute-start.17 = (bf16[512,256]{1,0:T(8,128)(2,1)S(1)}, bf16[512,256]{1,0:T(8,128)(2,1)S(1)}, u32[]{:S(2)}, u32[]{:S(2)}) collective-permute-start(bf16[512,256]{1,0:T(8,128)(2,1)S(1)} %add_convert_fusion.6.refs_4_), channel_id=1, source_target_pairs={{0,16},{1,17},{2,18},{3,19},{4,20},{5,21},{6,22},{7,23},{8,24},{9,... | collective-permute-start | bytes 786440 | tf_op jit(solution)/shard_map/ppermute | solution.py:53
  132.5 17.2 %collective-permute-start.16 = (bf16[512,256]{1,0:T(8,128)(2,1)S(1)}, bf16[512,256]{1,0:T(8,128)(2,1)S(1)}, u32[]{:S(2)}, u32[]{:S(2)}) collective-permute-start(bf16[512,256]{1,0:T(8,128)(2,1)S(1)} %add_convert_fusion.6.refs_4_), channel_id=1, source_target_pairs={{0,8},{1,9},{2,10},{3,11},{4,12},{5,13},{6,14},{7,15},{8,16},{9,17... | collective-permute-start | bytes 786440 | tf_op jit(solution)/shard_map/ppermute | solution.py:53
  142.1 9.2 %collective-permute-start.22 = (bf16[512,256]{1,0:T(8,128)(2,1)S(1)}, bf16[512,256]{1,0:T(8,128)(2,1)S(1)}, u32[]{:S(2)}, u32[]{:S(2)}) collective-permute-start(bf16[512,256]{1,0:T(8,128)(2,1)S(1)} %collective-permute-done.18.refs_7_), channel_id=1, source_target_pairs={{0,1},{1,0},{2,3},{3,2},{4,5},{5,4},{6,7},{7,6},{8,9},{9,8},{10,11... | collective-permute-start | bytes 786440 | tf_op jit(solution)/shard_map/ppermute | solution.py:53
  143.5 9.6 %collective-permute-start.32 = (bf16[1024,128]{1,0:T(8,128)(2,1)S(1)}, bf16[1024,128]{1,0:T(8,128)(2,1)S(1)}, u32[]{:S(2)}, u32[]{:S(2)}) collective-permute-start(bf16[1024,128]{1,0:T(8,128)(2,1)S(1)} %fusion.1.refs_12_), channel_id=1, source_target_pairs={{0,6},{1,7},{2,0},{3,1},{4,2},{5,3},{6,4},{7,5},{8,14},{9,15},{10,... | collective-permute-start | bytes 786440 | tf_op jit(solution)/shard_map/ppermute | solution.py:53
  150.1 9.5 %collective-permute-start.31 = (bf16[1024,128]{1,0:T(8,128)(2,1)S(1)}, bf16[1024,128]{1,0:T(8,128)(2,1)S(1)}, u32[]{:S(2)}, u32[]{:S(2)}) collective-permute-start(bf16[1024,128]{1,0:T(8,128)(2,1)S(1)} %fusion.1.refs_12_), channel_id=1, source_target_pairs={{0,4},{1,5},{2,6},{3,7},{4,0},{5,1},{6,2},{7,3},{8,12},{9,13},{10,... | collective-permute-start | bytes 786440 | tf_op jit(solution)/shard_map/ppermute | solution.py:53
  151.2 14.3 %collective-permute-start.30 = (bf16[1024,128]{1,0:T(8,128)(2,1)S(1)}, bf16[1024,128]{1,0:T(8,128)(2,1)S(1)}, u32[]{:S(2)}, u32[]{:S(2)}) collective-permute-start(bf16[1024,128]{1,0:T(8,128)(2,1)S(1)} %fusion.1.refs_12_), channel_id=1, source_target_pairs={{0,2},{1,3},{2,4},{3,5},{4,6},{5,7},{6,0},{7,1},{8,10},{9,11},{10,... | collective-permute-start | bytes 786440 | tf_op jit(solution)/shard_map/ppermute | solution.py:53
  177.6 9.1 %collective-permute-start.38 = (bf16[1024,128]{1,0:T(8,128)(2,1)S(1)}, bf16[1024,128]{1,0:T(8,128)(2,1)S(1)}, u32[]{:S(2)}, u32[]{:S(2)}) collective-permute-start(bf16[1024,128]{1,0:T(8,128)(2,1)S(1)} %add_convert_fusion.2), channel_id=1, source_target_pairs={{0,16},{1,17},{2,18},{3,19},{4,20},{5,21},{6,22},{7,23},{8,24},{9,... | collective-permute-start | bytes 786440 | tf_op jit(solution)/shard_map/ppermute | solution.py:53
  178.3 13.1 %collective-permute-start.40 = (bf16[1024,128]{1,0:T(8,128)(2,1)S(1)}, bf16[1024,128]{1,0:T(8,128)(2,1)S(1)}, u32[]{:S(2)}, u32[]{:S(2)}) collective-permute-start(bf16[1024,128]{1,0:T(8,128)(2,1)S(1)} %add_convert_fusion.1), channel_id=1, source_target_pairs={{0,24},{1,25},{2,26},{3,27},{4,28},{5,29},{6,30},{7,31},{8,0},{9,1... | collective-permute-start | bytes 786440 | tf_op jit(solution)/shard_map/ppermute | solution.py:53
  179.8 13.2 %collective-permute-start.42 = (bf16[1024,128]{1,0:T(8,128)(2,1)S(1)}, bf16[1024,128]{1,0:T(8,128)(2,1)S(1)}, u32[]{:S(2)}, u32[]{:S(2)}) collective-permute-start(bf16[1024,128]{1,0:T(8,128)(2,1)S(1)} %add_convert_fusion), channel_id=1, source_target_pairs={{0,8},{1,9},{2,10},{3,11},{4,12},{5,13},{6,14},{7,15},{8,16},{9,17... | collective-permute-start | bytes 786440 | tf_op jit(solution)/shard_map/ppermute | solution.py:53
  179.9 19.3 %collective-permute-start.33 = (bf16[512,256]{1,0:T(8,128)(2,1)S(1)}, bf16[512,256]{1,0:T(8,128)(2,1)S(1)}, u32[]{:S(2)}, u32[]{:S(2)}) collective-permute-start(bf16[512,256]{1,0:T(8,128)(2,1)S(1)} %get-tuple-element.63), channel_id=1, source_target_pairs={{0,4},{1,5},{2,6},{3,7},{4,0},{5,1},{6,2},{7,3},{8,12},{9,13},{10,... | collective-permute-start | bytes 786440 | tf_op jit(solution)/shard_map/ppermute | solution.py:53
  181.4 17.9 %collective-permute-start.34 = (bf16[512,256]{1,0:T(8,128)(2,1)S(1)}, bf16[512,256]{1,0:T(8,128)(2,1)S(1)}, u32[]{:S(2)}, u32[]{:S(2)}) collective-permute-start(bf16[512,256]{1,0:T(8,128)(2,1)S(1)} %get-tuple-element.64), channel_id=1, source_target_pairs={{0,6},{1,7},{2,0},{3,1},{4,2},{5,3},{6,4},{7,5},{8,14},{9,15},{10,... | collective-permute-start | bytes 786440 | tf_op jit(solution)/shard_map/ppermute | solution.py:53
  186.8 12.5 %collective-permute-start.35 = (bf16[512,256]{1,0:T(8,128)(2,1)S(1)}, bf16[512,256]{1,0:T(8,128)(2,1)}, u32[]{:S(2)}, u32[]{:S(2)}) collective-permute-start(bf16[512,256]{1,0:T(8,128)(2,1)S(1)} %get-tuple-element.65), channel_id=1, source_target_pairs={{0,2},{1,3},{2,4},{3,5},{4,6},{5,7},{6,0},{7,1},{8,10},{9,11},{10,... | collective-permute-start | bytes 786440 | tf_op jit(solution)/shard_map/ppermute | solution.py:53
  194.7 15.6 %all-to-all-start.1 = ((bf16[128,4,256]{2,1,0:T(4,128)(2,1)}), bf16[128,4,256]{2,1,0:T(4,128)(2,1)S(1)}, u32[]{:S(2)}, u32[]{:S(2)}) async-start(bf16[128,4,256]{2,1,0:T(4,128)(2,1)} %reshape.46), calls=%async_computation.1 | async-start | bytes 524288 | tf_op jit(solution)/shard_map/all_to_all | solution.py:59
  (22 other events, 206.4 us)

commit v3 on v1

v3 whole, which is shorter than its diff:
```python
import functools

import jax
import jax.numpy as jnp
from jax import lax
from jax.experimental import pallas as pl
from jax.experimental.pallas import tpu as pltpu
from jax.sharding import PartitionSpec as P

SIDE = 4
CORES = 2
TILE = 128
NODES = 512
BLOCKS = NODES // TILE
WIDTH = 256
SLOTS = 96
OWNER_CAP = 4
CAP = SIDE * CORES * OWNER_CAP
CODE_ROWS = 16
COUNT_LANE = 64
PACKED = CAP * TILE + CODE_ROWS
COLUMNS = CORES * SIDE * BLOCKS
TURNED = BLOCKS * WIDTH
PART = NODES // SIDE
SHIPPED = TURNED + PART * WIDTH // TILE
BF16 = jnp.bfloat16
F32 = jnp.float32
VMEM_LIMIT = 24 * 1024 * 1024
VMEM_MOST = 62 * 1024 * 1024

WHOLE = pl.BlockSpec(memory_space=pltpu.VMEM)
FAR = pl.BlockSpec(memory_space=pltpu.HBM)
SCALARS = pl.BlockSpec(memory_space=pltpu.SMEM)


def params(limit=VMEM_LIMIT):
    return pltpu.CompilerParams(vmem_limit_bytes=limit)


def struct(shape, dtype):
    return jax.ShapeDtypeStruct(shape, dtype)


def cost(flops, nbytes):
    return pl.CostEstimate(flops=int(flops), bytes_accessed=int(nbytes), transcendentals=0)


def move(array, axis, step):
    pairs = []
    for x in range(SIDE):
        for y in range(SIDE):
            for c in range(CORES):
                ahead = step * (1 - 2 * c)
                to_x = (x + ahead) % SIDE if axis == "x" else x
                to_y = (y + ahead) % SIDE if axis == "y" else y
                to_c = (c + step) % CORES if axis == "c" else c
                pairs.append(((x * SIDE + y) * CORES + c, (to_x * SIDE + to_y) * CORES + to_c))
    return lax.ppermute(array, "col", pairs)


def reshuffle(payload):
    devices = lax.axis_size("row") * lax.axis_size("col")
    direct = payload.reshape(devices, NODES // devices, WIDTH)
    moved = lax.all_to_all(direct, ("row", "col"), split_axis=0, concat_axis=0, tiled=True)
    return moved.reshape(payload.shape)


def exchange_planes(payload):
    rows, columns = lax.axis_size("row"), lax.axis_size("col")
    groups = [
        [z * columns + (x * SIDE + y) * CORES + c for z in range(rows) for x in range(SIDE) for c in range(CORES)]
        for y in range(SIDE)
    ]
    direct = payload.reshape(len(groups[0]), NODES // len(groups[0]), WIDTH)
    moved = lax.all_to_all(
        direct, ("row", "col"), split_axis=0, concat_axis=0, tiled=True, axis_index_groups=groups
    )
    return moved.reshape(payload.shape)


def ordering(key_row, key_col):
    below = (key_col[...] < key_row[...]).astype(jnp.int32)
    rank = jnp.sum(below, axis=0, keepdims=True)
    spot = lax.broadcasted_iota(jnp.int32, (NODES, NODES), 0)
    return (spot == rank).astype(F32).astype(BF16)


def order_kernel(key_row, key_col, data, out):
    select = ordering(key_row, key_col)
    out[...] = jnp.dot(select, data[...], preferred_element_type=F32).astype(BF16)


def order_turned_kernel(key_row, key_col, data, out):
    select = ordering(key_row, key_col)
    total = jnp.zeros((NODES, WIDTH), F32)
    for b in range(BLOCKS):
        part = select[:, b * TILE : (b + 1) * TILE]
        block = data[b * WIDTH : (b + 1) * WIDTH, :]
        total += lax.dot_general(part, block, (((1,), (1,)), ((), ())), preferred_element_type=F32)
    out[...] = total.astype(BF16)


def restore_kernel(key_row, key_col, data, out):
    below = (key_row[...] < key_col[...]).astype(jnp.int32)
    rank = jnp.sum(below, axis=1, keepdims=True)
    spot = lax.broadcasted_iota(jnp.int32, (NODES, NODES), 1)
    select = (spot == rank).astype(F32).astype(BF16)
    out[...] = jnp.dot(select, data[...], preferred_element_type=F32).astype(BF16)


def ship_kernel(key_row, key_col, data, turned, *outs):
    select = ordering(key_row, key_col)
    ordered = jnp.dot(select, data[...], preferred_element_type=F32).astype(BF16)
    for k in range(SIDE):
        outs[k][:TURNED, :] = turned[...]
        for h in range(WIDTH // TILE):
            rows = slice(TURNED + h * PART, TURNED + (h + 1) * PART)
            outs[k][rows, :] = ordered[k * PART : (k + 1) * PART, h * TILE : (h + 1) * TILE]


def ship(key, data, turned):
    return pl.pallas_call(
        ship_kernel,
        out_shape=[struct((SHIPPED, TILE), BF16)] * SIDE,
        in_specs=[WHOLE] * 4,
        out_specs=[WHOLE] * SIDE,
        compiler_params=params(),
        cost_estimate=cost(2 * NODES * NODES * WIDTH, 8 * NODES * WIDTH),
    )(key.reshape(1, NODES), key.reshape(NODES, 1), data, turned)


def regroup_kernel(pair, *refs):
    shipped, out = refs[:SIDE], refs[SIDE]
    place = lax.broadcasted_iota(jnp.int32, (NODES, NODES), 0)
    held = lax.broadcasted_iota(jnp.int32, (NODES, NODES), 1)
    peer, step, row = (held % PART) // pair, held // PART, held % pair
    select = (place == (peer * SIDE + step) * pair + row).astype(F32).astype(BF16)
    for h in range(WIDTH // TILE):
        rows = slice(TURNED + h * PART, TURNED + (h + 1) * PART)
        data = jnp.concatenate([part[rows, :] for part in shipped], axis=0)
        total = jnp.dot(select, data, preferred_element_type=F32)
        out[:, h * TILE : (h + 1) * TILE] = total.astype(BF16)


def regroup(shipped, devices):
    return pl.pallas_call(
        functools.partial(regroup_kernel, NODES // devices),
        out_shape=struct((NODES, WIDTH), BF16),
        in_specs=[WHOLE] * SIDE,
        out_specs=WHOLE,
        compiler_params=params(),
        cost_estimate=cost(2 * NODES * NODES * WIDTH, 4 * NODES * WIDTH),
    )(*shipped)


def permute_call(kernel, key, data):
    return pl.pallas_call(
        kernel,
        out_shape=struct((NODES, WIDTH), BF16),
        in_specs=[WHOLE] * 3,
        out_specs=WHOLE,
        compiler_params=params(),
        cost_estimate=cost(2 * NODES * NODES * WIDTH, 4 * NODES * WIDTH),
    )(key.reshape(1, NODES), key.reshape(NODES, 1), data)


def bucket_kernel(target, code, source, *refs):
    outs, (tiles, packed, listed, counts, sent) = refs[:SIDE], refs[SIDE:]
    fetched = pltpu.make_async_copy(source, tiles, sent.at[SIDE])
    fetched.start()
    for d in range(SIDE + 1):
        counts[d] = 0

    def note(s, carry):
        d = target[s]
        n = counts[d]
        listed[d * SLOTS + n] = s
        counts[d] = n + 1
        return carry

    lax.fori_loop(0, SLOTS, note, 0)
    fetched.wait()
    lane = lax.broadcasted_iota(jnp.int32, (CODE_ROWS, TILE), 1)
    copies = []
    for d in (1, 3, 2, 0):
        used = counts[d]

        def place(n, codes, d=d):
            s = listed[d * SLOTS + n]
            packed[d, pl.ds(pl.multiple_of(n * TILE, TILE), TILE), :] = tiles[s]
            return jnp.where(lane == n, code[s], codes)

        def clear(n, carry, d=d):
            rows = pl.ds(pl.multiple_of(n * TILE, TILE), TILE)
            packed[d, rows, :] = jnp.zeros((TILE, TILE), BF16)
            return carry

        codes = lax.fori_loop(0, used, place, jnp.zeros((CODE_ROWS, TILE), jnp.int32))
        lax.fori_loop(used, CAP, clear, 0)
        codes = jnp.where(lane == COUNT_LANE, used, codes)
        packed[d, CAP * TILE :, :] = codes.astype(F32).astype(BF16)
        copies.append(pltpu.make_async_copy(packed.at[d], outs[d], sent.at[d]))
        copies[-1].start()
    for copy in copies:
        copy.wait()


def bucket(tiles, target, code):
    return pl.pallas_call(
        bucket_kernel,
        out_shape=[struct((PACKED, TILE), BF16)] * SIDE,
        in_specs=[SCALARS, SCALARS, FAR],
        out_specs=[FAR] * SIDE,
        scratch_shapes=[
            pltpu.VMEM((SLOTS, TILE, TILE), BF16),
            pltpu.VMEM((SIDE, PACKED, TILE), BF16),
            pltpu.SMEM(((SIDE + 1) * SLOTS,), jnp.int32),
            pltpu.SMEM((SIDE + 1,), jnp.int32),
            pltpu.SemaphoreType.DMA((SIDE + 1,)),
        ],
        compiler_params=params(VMEM_MOST),
        cost_estimate=cost(1e6, 7e6),
    )(target, code, tiles)


def slot_steps(codes):
    most = codes[COUNT_LANE]
    for k in range(1, SIDE):
        most = jnp.maximum(most, codes[k * TILE + COUNT_LANE])
    return (most + 1) // 2


def fetch(sources, places, arrived):
    copies = [
        pltpu.make_async_copy(source, place, arrived.at[i])
        for i, (source, place) in enumerate(zip(sources, places, strict=True))
    ]
    for copy in copies:
        copy.start()
    return copies


def forward_kernel(codes, *refs):
    packs, refs = refs[:SIDE], refs[SIDE:]
    shards, refs = refs[: CORES * SIDE], refs[CORES * SIDE :]
    outs, (tiles, features, arrived, *totals) = refs[:SIDE], refs[SIDE:]
    places = [tiles.at[k] for k in range(SIDE)]
    places += [features.at[pl.ds(j * NODES, NODES)] for j in range(CORES * SIDE)]
    copies = fetch([*packs, *shards], places, arrived)
    for k in range(SIDE):
        totals[k][...] = jnp.zeros((NODES, WIDTH), F32)
    for copy in copies:
        copy.wait()

    def step(i, carry):
        for u in range(2):
            n = i * 2 + u
            for k in range(SIDE):
                code = codes[k * TILE + n]
                row = pl.multiple_of((code // COLUMNS) * TILE, TILE)
                column = pl.multiple_of((code % COLUMNS) * TILE, TILE)
                tile = tiles[k, pl.ds(pl.multiple_of(n * TILE, TILE), TILE), :]
                block = features[pl.ds(column, TILE), :]
                totals[k][pl.ds(row, TILE), :] += jnp.dot(tile, block, preferred_element_type=F32)
        return carry

    lax.fori_loop(0, slot_steps(codes), step, 0)
    for k in range(SIDE):
        outs[k][...] = totals[k][...].astype(outs[k].dtype)


def forward_product(packs, codes, shards):
    shape = (NODES, WIDTH)
    inputs = SIDE + CORES * SIDE
    return pl.pallas_call(
        forward_kernel,
        out_shape=[struct(shape, dtype) for dtype in (F32, BF16, BF16, F32)],
        in_specs=[SCALARS] + [FAR] * inputs,
        out_specs=[WHOLE] * SIDE,
        scratch_shapes=[
            pltpu.VMEM((SIDE, PACKED, TILE), BF16),
            pltpu.VMEM((CORES * SIDE * NODES, WIDTH), BF16),
            pltpu.SemaphoreType.DMA((inputs,)),
        ]
        + [pltpu.VMEM(shape, F32)] * SIDE,
        compiler_params=params(),
        cost_estimate=cost(6e9, 1e6),
    )(codes, *packs, *shards)


def backward_kernel(codes, *refs):
    packs, refs = refs[:SIDE], refs[SIDE:]
    shards, refs = refs[:SIDE], refs[SIDE:]
    near, far, tiles, turned, arrived, totals = refs
    places = [tiles.at[k] for k in range(SIDE)] + [turned.at[k] for k in range(SIDE)]
    shards = [shard.at[pl.ds(0, TURNED)] for shard in shards]
    copies = fetch([*packs, *shards], places, arrived)
    totals[...] = jnp.zeros(totals.shape, F32)
    for copy in copies:
        copy.wait()

    def step(i, carry):
        for u in range(2):
            n = i * 2 + u
            for k in range(SIDE):
                code = codes[k * TILE + n]
                row = pl.multiple_of((code // COLUMNS) * WIDTH, WIDTH)
                column = pl.multiple_of((code % COLUMNS) * WIDTH, WIDTH)
                tile = tiles[k, pl.ds(pl.multiple_of(n * TILE, TILE), TILE), :]
                block = turned[k, pl.ds(row, WIDTH), :]
                totals[pl.ds(column, WIDTH), :] += jnp.dot(block, tile, preferred_element_type=F32)
        return carry

    lax.fori_loop(0, slot_steps(codes), step, 0)
    near[...] = totals[: SIDE * TURNED, :]
    far[...] = totals[SIDE * TURNED :, :].astype(BF16)


def backward_product(packs, codes, shards):
    shape = (SIDE * TURNED, TILE)
    return pl.pallas_call(
        backward_kernel,
        out_shape=[struct(shape, F32), struct(shape, BF16)],
        in_specs=[SCALARS] + [FAR] * (2 * SIDE),
        out_specs=[WHOLE] * CORES,
        scratch_shapes=[
            pltpu.VMEM((SIDE, PACKED, TILE), BF16),
            pltpu.VMEM((SIDE, TURNED, TILE), BF16),
            pltpu.SemaphoreType.DMA((2 * SIDE,)),
            pltpu.VMEM((CORES * SIDE * TURNED, TILE), F32),
        ],
        compiler_params=params(),
        cost_estimate=cost(6e9, 1e6),
    )(codes, *packs, *shards)


ORDER = (2, 1, 3)


def gather_line(array, axis):
    got = {d: move(array, axis, d) for d in ORDER}
    return [array] + [got[d] for d in range(1, SIDE)]


def gather_forward(features):
    one, three = move(features, "x", 1), move(features, "x", -1)
    line = [features, one, move(one, "x", 1), three]
    return line, line + [move(shard, "c", 1) for shard in line]


def scatter_forward(rows):
    passed, back = move(rows[2], "y", 1), move(rows[1], "y", -1)
    ahead = move((rows[3] + passed.astype(F32)).astype(BF16), "y", 1)
    return rows[0] + back.astype(F32) + ahead.astype(F32), back


def add_cores(near, far):
    parts = [slice(j * TURNED, (j + 1) * TURNED) for j in range(SIDE)]
    return [near[part] + far[part].astype(F32) for part in parts]


def add_up(own, arrived):
    for term in arrived:
        own = own + term.astype(F32)
    return own


def after(arrays, others):
    return lax.optimization_barrier((arrays, others))[0]


def shards(
    embeddings,
    partition_source,
    hash_target,
    tile_values,
    tile_row,
    tile_owner,
    tile_sub,
    tile_count,
    cotangent,
):
    index = lax.axis_index("col")
    core = index % CORES
    own_y = (index // CORES) % SIDE
    own_x = index // (CORES * SIDE)

    owner = tile_owner[:, 0]
    live = jnp.arange(SLOTS, dtype=jnp.int32) < tile_count[0]
    back_x = ((own_x - owner // (CORES * SIDE)) * (1 - 2 * (owner % CORES))) % SIDE
    far_y = ((owner // CORES - own_y) * (1 - 2 * core)) % SIDE
    side = (owner + core) % CORES
    column = (side * SIDE + back_x) * BLOCKS + tile_sub
    target = jnp.where(live, far_y, SIDE)
    devices = lax.axis_size("row") * lax.axis_size("col")
    turn = 1 - 2 * core

    def by_plane(device):
        return device // (CORES * SIDE) * CORES + device % CORES, device // CORES % SIDE

    plane, line_y = by_plane(hash_target // NODES)
    key = ((line_y - own_y) * turn) % SIDE * (devices // SIDE) + plane
    turned = cotangent.reshape(BLOCKS, TILE, WIDTH).transpose(0, 2, 1).reshape(TURNED, TILE)
    shipped = ship(key * NODES + hash_target % NODES, embeddings, turned)
    packs = bucket(tile_values, after(target, shipped[0]), tile_row * COLUMNS + column)
    shipped = [shipped[0]] + [move(shipped[k], "y", k) for k in range(1, SIDE)]
    moved = {d: move(after(packs[d], shipped[1]), "y", d) for d in (1, 3)}
    moved[2] = move(after(packs[2], shipped), "y", 2)

    incoming = exchange_planes(regroup(shipped, devices))
    plane, line_y = by_plane(partition_source // NODES)
    turn = 1 - 2 * (plane % CORES)
    key = plane * SIDE + ((own_y - line_y) * turn) % SIDE
    place = jnp.arange(NODES, dtype=jnp.int32)
    initial = permute_call(restore_kernel, key * NODES + place, incoming)
    part_key = (partition_source // NODES) * NODES + place
    packs = [packs[0]] + [moved[d] for d in range(1, SIDE)]
    codes = jnp.concatenate([pack[CAP * TILE] for pack in packs]).astype(jnp.int32)
    line, features = gather_forward(initial)

    def both_products(features, gradients, beside):
        near, far = backward_product(packs, codes, gradients)
        far = move(far, "c", 1)
        if beside:
            rows = forward_product(packs, codes, after(features, near))
            near = after(near, rows[0])
        columns = add_cores(near, far)
        got = {j: move(columns[j].astype(BF16), "x", -j) for j in ORDER}
        if beside:
            rows = after(rows, columns)
        else:
            rows = forward_product(packs, codes, after(features, columns))
            columns[0] = after(columns[0], rows[0])
        total, arrived = scatter_forward(rows)
        if beside:
            columns[0] = after(columns[0], arrived)
        return total, add_up(columns[0], got.values())

    packs = after(packs, line)
    layer_one, back_one = both_products(features, shipped, True)
    layer_one = layer_one.astype(BF16)
    middle = ((turned.astype(F32) + back_one) / 3.0).astype(BF16)
    gradients = gather_line(middle, "y")
    line, features = gather_forward(after(layer_one, middle))
    layer_two, back_zero = both_products(features, after(gradients, line), False)
    grad_part = (turned.astype(F32) / 3.0 + back_zero).astype(BF16)
    returned = reshuffle(permute_call(order_turned_kernel, part_key, grad_part))
    embed_grad = permute_call(restore_kernel, hash_target, returned)
    propagated = ((initial.astype(F32) + layer_one.astype(F32) + layer_two) / 3.0).astype(BF16)
    return propagated, embed_grad


def solution(mesh):
    both = ("row", "col")
    return jax.shard_map(
        shards,
        mesh=mesh,
        in_specs=(
            P(both, None),
            P(both),
            P(both),
            P(both, None, None),
            P(both),
            P(both, None),
            P(both),
            P(both),
            P(both, None),
        ),
        out_specs=(P(both, None), P(both, None)),
        check_vma=False,
    )
```

time: 201 us -> 178 us (0.89)
  waiting for transfers between devices: 83.8 us -> 61.9 us
  starting transfers between devices: 74.9 us -> 65.7 us
  Pallas kernels: 28 us -> 34.3 us
  other arithmetic: 3.83 us -> 5.99 us
    ppermute x43 -> x37, waiting for transfers between devices: 73.7 us -> 45 us  [move(): return lax.ppermute(array, 'col', pairs)]
    all_to_all x2 -> x1, starting transfers between devices: 21.1 us -> 8.8 us  [reshuffle(): lax.all_to_all(direct, ('row', 'col'), split_axis=0, concat_axis=0, tiled...]
    all_to_all x0 -> x1, starting transfers between devices: none -> 10.7 us  [exchange_planes(): lax.all_to_all(direct, ('row', 'col'), split_axis=0, concat_axis=0, tiled...]
    all_to_all x0 -> x1, waiting for transfers between devices: none -> 8.75 us  [exchange_planes(): lax.all_to_all(direct, ('row', 'col'), split_axis=0, concat_axis=0, tiled...]
    pallas_call x4 -> x6, Pallas kernels: 18.9 us -> 26.7 us  [the longest x2 12.1 us: backward_product(): pl.pallas_call(backward_kernel, out_shape=[struct(shape, F32), struct(sha...]
    ppermute x43 -> x37, starting transfers between devices: 53.8 us -> 46.2 us  [move(): return lax.ppermute(array, 'col', pairs)]
    add x2 -> x6, other arithmetic: 0.72 us -> 4.48 us  [the longest x4 3.15 us: add_cores(): return [near[part] + far[part].astype(F32) for part in parts]]
    all_to_all x2 -> x1, waiting for transfers between devices: 10.1 us -> 8.14 us  [reshuffle(): lax.all_to_all(direct, ('row', 'col'), split_axis=0, concat_axis=0, tiled...]
  transfers between devices with their start and end apart: 45 -> 39, of which waited for: 16 -> 19; matrix products, arithmetic and copies ran while one was open for 4% -> 3% of each run, Pallas kernels for 10% -> 12%
where the time goes in v3:
time: 178 us; the launch traced here: 177 us
  starting transfers between devices  65.7 us (37%)
  waiting for transfers between devices  61.9 us (35%)
  Pallas kernels  34.3 us (19%)
  local copies, waits for them, and re-layouts  7.82 us (4%)
  other arithmetic  5.99 us (3%)
    ppermute x37, starting transfers between devices, move(): return lax.ppermute(array, 'col', pairs)  46.2 us
    ppermute x37, waiting for transfers between devices, move(): return lax.ppermute(array, 'col', pairs)  45 us
    pallas_call x2, Pallas kernels, backward_product(): pl.pallas_call(backward_kernel, out_shape=[struct(shape, F32), struct(sha...  12.1 us
    pallas_call x2, Pallas kernels, forward_product(): pl.pallas_call(forward_kernel, out_shape=[struct(shape, dtype) for dtype...  12 us
    all_to_all x1, starting transfers between devices, exchange_planes(): lax.all_to_all(direct, ('row', 'col'), split_axis=0, concat_axis=0, tiled...  10.7 us
    all_to_all x1, starting transfers between devices, reshuffle(): lax.all_to_all(direct, ('row', 'col'), split_axis=0, concat_axis=0, tiled...  8.8 us
    all_to_all x1, waiting for transfers between devices, exchange_planes(): lax.all_to_all(direct, ('row', 'col'), split_axis=0, concat_axis=0, tiled...  8.75 us
    all_to_all x1, waiting for transfers between devices, reshuffle(): lax.all_to_all(direct, ('row', 'col'), split_axis=0, concat_axis=0, tiled...  8.14 us
  transfers between devices with their start and end apart: 39, of which 19 were waited for; matrix products, arithmetic and copies ran while one was open for 3% of the time, Pallas kernels for 12%

profile of v3, /device:TPU:1, one launch (start us, length us, event | category | flops | bytes accessed | tf_op | source)
XLA Modules:
  0.0 177.4 jit_solution(8012475633136755228)
XLA Ops:
  4.2 3.6 %collective-permute-start = (bf16[1280,128]{1,0:T(8,128)(2,1)}, bf16[1280,128]{1,0:T(8,128)(2,1)S(1)}, u32[]{:S(2)}, u32[]{:S(2)}) collective-permute-start(bf16[1280,128]{1,0:T(8,128)(2,1)} %get-tuple-element.59), channel_id=1, source_target_pairs={{0,2},{1,7},{2,4},{3,1},{4,6},{5,3},{6,0},{7,5},{8,10},{9,15},{10,... | collective-permute-start | bytes 983048 | tf_op jit(solution)/shard_map/ppermute | solution.py:58
  10.1 4.8 %shard_map.107 = (bf16[4112,128]{1,0:T(8,128)(2,1)}, bf16[4112,128]{1,0:T(8,128)(2,1)}, bf16[4112,128]{1,0:T(8,128)(2,1)}, bf16[4112,128]{1,0:T(8,128)(2,1)}) custom-call(s32[96]{0:T(128)} %get-tuple-element.62.target, s32[96]{0:T(128)} %get-tuple-element.122.code, bf16[96,128,128]{2,1,0:T(8,128)(2,1)} %source.1), custom_call_target="tpu_custom_call" | custom-call | flops 1000000 | bytes 7000000 | tf_op jit(solution)/shard_map/pallas_call | solution.py:209
  14.9 5.8 %collective-permute-done.refs_1_.refs_5_ = bf16[1280,128]{1,0:T(8,128)(2,1)S(1)} collective-permute-done((bf16[1280,128]{1,0:T(8,128)(2,1)}, bf16[1280,128]{1,0:T(8,128)(2,1)S(1)}, u32[]{:S(2)}, u32[]{:S(2)}) %collective-permute-start) | collective-permute-done | bytes 327712 | tf_op jit(solution)/shard_map/ppermute | solution.py:58
  20.7 3.3 %collective-permute-start.3 = (bf16[4112,128]{1,0:T(8,128)(2,1)}, bf16[4112,128]{1,0:T(8,128)(2,1)}, u32[]{:S(2)}, u32[]{:S(2)}) collective-permute-start(bf16[4112,128]{1,0:T(8,128)(2,1)} %get-tuple-element.65), channel_id=1, source_target_pairs={{0,2},{1,7},{2,4},{3,1},{4,6},{5,3},{6,0},{7,5},{8,10},{9,15},{10,... | collective-permute-start | bytes 3158024 | tf_op jit(solution)/shard_map/ppermute | solution.py:58
  24.0 1.8 collective-permute-start.4
  27.6 10.7 %all-to-all-start = ((bf16[32,16,256]{2,1,0:T(8,128)(2,1)}), bf16[32,16,256]{2,1,0:T(8,128)(2,1)S(1)}, u32[]{:S(2)}, u32[]{:S(2)}) async-start(bf16[32,16,256]{2,1,0:T(8,128)(2,1)} %bitcast.7), calls=%async_computation | async-start | bytes 524288 | tf_op jit(solution)/shard_map/all_to_all | solution.py:75
  38.5 8.7 %all-to-all-done = bf16[32,16,256]{2,1,0:T(8,128)(2,1)S(1)} async-done(((bf16[32,16,256]{2,1,0:T(8,128)(2,1)}), bf16[32,16,256]{2,1,0:T(8,128)(2,1)S(1)}, u32[]{:S(2)}, u32[]{:S(2)}) %all-to-all-start) | async-done | bytes 262176 | tf_op jit(solution)/shard_map/all_to_all | solution.py:75
  49.5 5.6 %collective-permute-done.6.refs_5_ = bf16[512,256]{1,0:T(8,128)(2,1)S(1)} collective-permute-done((bf16[512,256]{1,0:T(8,128)(2,1)S(1)}, bf16[512,256]{1,0:T(8,128)(2,1)S(1)}, u32[]{:S(2)}, u32[]{:S(2)}) %collective-permute-start.6) | collective-permute-done | bytes 262176 | tf_op jit(solution)/shard_map/ppermute | solution.py:58
  58.4 2.4 %collective-permute-done.7.refs_6_ = bf16[512,256]{1,0:T(8,128)(2,1)S(1)} collective-permute-done((bf16[512,256]{1,0:T(8,128)(2,1)S(1)}, bf16[512,256]{1,0:T(8,128)(2,1)S(1)}, u32[]{:S(2)}, u32[]{:S(2)}) %collective-permute-start.7) | collective-permute-done | bytes 262176 | tf_op jit(solution)/shard_map/ppermute | solution.py:58
  60.8 4.9 %collective-permute-done.3.refs_1_ = bf16[4112,128]{1,0:T(8,128)(2,1)} collective-permute-done((bf16[4112,128]{1,0:T(8,128)(2,1)}, bf16[4112,128]{1,0:T(8,128)(2,1)}, u32[]{:S(2)}, u32[]{:S(2)}) %collective-permute-start.3) | collective-permute-done | bytes 1052704 | tf_op jit(solution)/shard_map/ppermute | solution.py:58
  65.6 4.1 %collective-permute-done.5.refs_3_ = bf16[4112,128]{1,0:T(8,128)(2,1)} collective-permute-done((bf16[4112,128]{1,0:T(8,128)(2,1)}, bf16[4112,128]{1,0:T(8,128)(2,1)}, u32[]{:S(2)}, u32[]{:S(2)}) %collective-permute-start.5) | collective-permute-done | bytes 1052704 | tf_op jit(solution)/shard_map/ppermute | solution.py:58
  73.0 6.1 %shard_map.108 = (f32[4096,128]{1,0:T(8,128)S(1)}, bf16[4096,128]{1,0:T(8,128)(2,1)S(1)}) custom-call(s32[512]{0:T(512)S(1)} %maximum_convert_fusion.codes, bf16[4112,128]{1,0:T(8,128)(2,1)S(1)} %copy-done.3, bf16[4112,128]{1,0:T(8,128)(2,1)} %collective-permute-done.3.refs_1_, bf16[4112,128]{1,0:T(8,128)(2,1)} %collective-permute-done.4.refs_2_, ...), custom_call_target="tpu_custom_call" | custom-call | flops 6000000000 | bytes 1000000 | tf_op jit(solution)/shard_map/pallas_call | solution.py:321
  81.1 1.6 collective-permute-done.9.refs_8_
  83.8 6.0 %shard_map.109 = (f32[512,256]{1,0:T(8,128)S(1)}, bf16[512,256]{1,0:T(8,128)(2,1)S(1)}, bf16[512,256]{1,0:T(8,128)(2,1)S(1)}, f32[512,256]{1,0:T(8,128)S(1)}) custom-call(s32[512]{0:T(512)S(1)} %maximum_convert_fusion.codes, bf16[4112,128]{1,0:T(8,128)(2,1)S(1)} %copy-done.4, bf16[4112,128]{1,0:T(8,128)(2,1)} %collective-permute-done.3.refs_1_, ...), custom_call_target="tpu_custom_call" | custom-call | flops 6000000000 | bytes 1000000 | tf_op jit(solution)/shard_map/pallas_call | solution.py:275
  91.5 2.2 %collective-permute-start.15 = (bf16[512,256]{1,0:T(8,128)(2,1)S(1)}, bf16[512,256]{1,0:T(8,128)(2,1)S(1)}, u32[]{:S(2)}, u32[]{:S(2)}) collective-permute-start(bf16[512,256]{1,0:T(8,128)(2,1)S(1)} %get-tuple-element.92), channel_id=1, source_target_pairs={{0,2},{1,7},{2,4},{3,1},{4,6},{5,3},{6,0},{7,5},{8,10},{9,15},{10,... | collective-permute-start | bytes 786440 | tf_op jit(solution)/shard_map/ppermute | solution.py:58
  94.8 1.8 %collective-permute-start.18 = (bf16[1024,128]{1,0:T(8,128)(2,1)S(1)}, bf16[1024,128]{1,0:T(8,128)(2,1)S(1)}, u32[]{:S(2)}, u32[]{:S(2)}) collective-permute-start(bf16[1024,128]{1,0:T(8,128)(2,1)S(1)} %get-tuple-element.119), channel_id=1, source_target_pairs={{0,24},{1,9},{2,26},{3,11},{4,28},{5,13},{6,30},{7,15},{8,0},{9,17... | collective-permute-start | bytes 786440 | tf_op jit(solution)/shard_map/ppermute | solution.py:58
  97.4 2.2 %collective-permute-done.15 = bf16[512,256]{1,0:T(8,128)(2,1)S(1)} collective-permute-done((bf16[512,256]{1,0:T(8,128)(2,1)S(1)}, bf16[512,256]{1,0:T(8,128)(2,1)S(1)}, u32[]{:S(2)}, u32[]{:S(2)}) %collective-permute-start.15) | collective-permute-done | bytes 262176 | tf_op jit(solution)/shard_map/ppermute | solution.py:58
  99.7 3.3 %collective-permute-start.16 = (bf16[512,256]{1,0:T(8,128)(2,1)S(1)}, bf16[512,256]{1,0:T(8,128)(2,1)S(1)}, u32[]{:S(2)}, u32[]{:S(2)}) collective-permute-start(bf16[512,256]{1,0:T(8,128)(2,1)S(1)} %add_convert_fusion.2), channel_id=1, source_target_pairs={{0,2},{1,7},{2,4},{3,1},{4,6},{5,3},{6,0},{7,5},{8,10},{9,15},{10,... | collective-permute-start | bytes 786440 | tf_op jit(solution)/shard_map/ppermute | solution.py:58
  103.0 6.1 %collective-permute-done.18 = bf16[1024,128]{1,0:T(8,128)(2,1)S(1)} collective-permute-done((bf16[1024,128]{1,0:T(8,128)(2,1)S(1)}, bf16[1024,128]{1,0:T(8,128)(2,1)S(1)}, u32[]{:S(2)}, u32[]{:S(2)}) %collective-permute-start.18) | collective-permute-done | bytes 262176 | tf_op jit(solution)/shard_map/ppermute | solution.py:58
  109.3 2.4 %collective-permute-start.20 = (bf16[512,256]{1,0:T(8,128)(2,1)S(1)}, bf16[512,256]{1,0:T(8,128)(2,1)S(1)}, u32[]{:S(2)}, u32[]{:S(2)}) collective-permute-start(bf16[512,256]{1,0:T(8,128)(2,1)S(1)} %add_convert_fusion.1.refs_4_), channel_id=1, source_target_pairs={{0,8},{1,25},{2,10},{3,27},{4,12},{5,29},{6,14},{7,31},{8,16},{9,1... | collective-permute-start | bytes 786440 | tf_op jit(solution)/shard_map/ppermute | solution.py:58
  111.8 1.7 collective-permute-start.27
  115.5 3.0 %collective-permute-start.21 = (bf16[512,256]{1,0:T(8,128)(2,1)S(1)}, bf16[512,256]{1,0:T(8,128)(2,1)S(1)}, u32[]{:S(2)}, u32[]{:S(2)}) collective-permute-start(bf16[512,256]{1,0:T(8,128)(2,1)S(1)} %collective-permute-done.20.refs_5_), channel_id=1, source_target_pairs={{0,8},{1,25},{2,10},{3,27},{4,12},{5,29},{6,14},{7,31},{8,16},{9,1... | collective-permute-start | bytes 786440 | tf_op jit(solution)/shard_map/ppermute | solution.py:58
  118.5 3.9 %collective-permute-done.27.refs_5_ = bf16[1024,128]{1,0:T(8,128)(2,1)S(1)} collective-permute-done((bf16[1024,128]{1,0:T(8,128)(2,1)S(1)}, bf16[1024,128]{1,0:T(8,128)(2,1)S(1)}, u32[]{:S(2)}, u32[]{:S(2)}) %collective-permute-start.27) | collective-permute-done | bytes 262176 | tf_op jit(solution)/shard_map/ppermute | solution.py:58
  123.4 2.8 %collective-permute-done.29.refs_7_ = bf16[1024,128]{1,0:T(8,128)(2,1)S(1)} collective-permute-done((bf16[1024,128]{1,0:T(8,128)(2,1)S(1)}, bf16[1024,128]{1,0:T(8,128)(2,1)S(1)}, u32[]{:S(2)}, u32[]{:S(2)}) %collective-permute-start.29) | collective-permute-done | bytes 262176 | tf_op jit(solution)/shard_map/ppermute | solution.py:58
  126.2 6.1 %shard_map.110 = (f32[4096,128]{1,0:T(8,128)S(1)}, bf16[4096,128]{1,0:T(8,128)(2,1)S(1)}) custom-call(s32[512]{0:T(512)S(1)} %maximum_convert_fusion.codes, bf16[4112,128]{1,0:T(8,128)(2,1)S(1)} %copy-done.4, bf16[4112,128]{1,0:T(8,128)(2,1)} %collective-permute-done.3.refs_1_, bf16[4112,128]{1,0:T(8,128)(2,1)} %collective-permute-done.4.refs_2_, ...), custom_call_target="tpu_custom_call" | custom-call | flops 6000000000 | bytes 1000000 | tf_op jit(solution)/shard_map/pallas_call | solution.py:321
  136.6 1.7 convert_add_fusion.1
  138.3 2.9 %collective-permute-start.34 = (bf16[1024,128]{1,0:T(8,128)(2,1)S(1)}, bf16[1024,128]{1,0:T(8,128)(2,1)S(1)}, u32[]{:S(2)}, u32[]{:S(2)}) collective-permute-start(bf16[1024,128]{1,0:T(8,128)(2,1)S(1)} %get-tuple-element.115), channel_id=1, source_target_pairs={{0,16},{1,17},{2,18},{3,19},{4,20},{5,21},{6,22},{7,23},{8,24},{9,... | collective-permute-start | bytes 786440 | tf_op jit(solution)/shard_map/ppermute | solution.py:58
  142.5 2.7 %collective-permute-start.36 = (bf16[1024,128]{1,0:T(8,128)(2,1)S(1)}, bf16[1024,128]{1,0:T(8,128)(2,1)S(1)}, u32[]{:S(2)}, u32[]{:S(2)}) collective-permute-start(bf16[1024,128]{1,0:T(8,128)(2,1)S(1)} %get-tuple-element.114), channel_id=1, source_target_pairs={{0,8},{1,25},{2,10},{3,27},{4,12},{5,29},{6,14},{7,31},{8,16},{9,1... | collective-permute-start | bytes 786440 | tf_op jit(solution)/shard_map/ppermute | solution.py:58
  145.1 6.0 %shard_map.111 = (f32[512,256]{1,0:T(8,128)S(1)}, bf16[512,256]{1,0:T(8,128)(2,1)S(1)}, bf16[512,256]{1,0:T(8,128)(2,1)S(1)}, f32[512,256]{1,0:T(8,128)S(1)}) custom-call(s32[512]{0:T(512)S(1)} %maximum_convert_fusion.codes, bf16[4112,128]{1,0:T(8,128)(2,1)S(1)} %copy-done.5, bf16[4112,128]{1,0:T(8,128)(2,1)} %collective-permute-done.3.refs_1_, ...), custom_call_target="tpu_custom_call" | custom-call | flops 6000000000 | bytes 1000000 | tf_op jit(solution)/shard_map/pallas_call | solution.py:275
  155.1 8.8 %all-to-all-start.1 = ((bf16[128,4,256]{2,1,0:T(4,128)(2,1)}), bf16[128,4,256]{2,1,0:T(4,128)(2,1)S(1)}, u32[]{:S(2)}, u32[]{:S(2)}) async-start(bf16[128,4,256]{2,1,0:T(4,128)(2,1)} %reshape.58), calls=%async_computation.1 | async-start | bytes 524288 | tf_op jit(solution)/shard_map/all_to_all | solution.py:64
  164.0 2.7 %collective-permute-start.33 = (bf16[512,256]{1,0:T(8,128)(2,1)S(1)}, bf16[512,256]{1,0:T(8,128)(2,1)S(1)}, u32[]{:S(2)}, u32[]{:S(2)}) collective-permute-start(bf16[512,256]{1,0:T(8,128)(2,1)S(1)} %add_convert_fusion), channel_id=1, source_target_pairs={{0,2},{1,7},{2,4},{3,1},{4,6},{5,3},{6,0},{7,5},{8,10},{9,15},{10,... | collective-permute-start | bytes 786440 | tf_op jit(solution)/shard_map/ppermute | solution.py:58
  166.9 8.1 %all-to-all-done.1 = bf16[128,4,256]{2,1,0:T(4,128)(2,1)S(1)} async-done(((bf16[128,4,256]{2,1,0:T(4,128)(2,1)}), bf16[128,4,256]{2,1,0:T(4,128)(2,1)S(1)}, u32[]{:S(2)}, u32[]{:S(2)}) %all-to-all-start.1) | async-done | bytes 262176 | tf_op jit(solution)/shard_map/all_to_all | solution.py:64
  (98 shorter events, 37.9 us)
Async XLA Ops:
  4.2 16.5 %collective-permute-start = (bf16[1280,128]{1,0:T(8,128)(2,1)}, bf16[1280,128]{1,0:T(8,128)(2,1)S(1)}, u32[]{:S(2)}, u32[]{:S(2)}) collective-permute-start(bf16[1280,128]{1,0:T(8,128)(2,1)} %get-tuple-element.59), channel_id=1, source_target_pairs={{0,2},{1,7},{2,4},{3,1},{4,6},{5,3},{6,0},{7,5},{8,10},{9,15},{10,... | collective-permute-start | bytes 983048 | tf_op jit(solution)/shard_map/ppermute | solution.py:58
  7.8 16.2 %collective-permute-start.1 = (bf16[1280,128]{1,0:T(8,128)(2,1)}, bf16[1280,128]{1,0:T(8,128)(2,1)S(1)}, u32[]{:S(2)}, u32[]{:S(2)}) collective-permute-start(bf16[1280,128]{1,0:T(8,128)(2,1)} %get-tuple-element.60), channel_id=1, source_target_pairs={{0,4},{1,5},{2,6},{3,7},{4,0},{5,1},{6,2},{7,3},{8,12},{9,13},{10,... | collective-permute-start | bytes 983048 | tf_op jit(solution)/shard_map/ppermute | solution.py:58
  8.1 15.9 %collective-permute-start.2 = (bf16[1280,128]{1,0:T(8,128)(2,1)}, bf16[1280,128]{1,0:T(8,128)(2,1)S(1)}, u32[]{:S(2)}, u32[]{:S(2)}) collective-permute-start(bf16[1280,128]{1,0:T(8,128)(2,1)} %get-tuple-element.61), channel_id=1, source_target_pairs={{0,6},{1,3},{2,0},{3,5},{4,2},{5,7},{6,4},{7,1},{8,14},{9,11},{10,... | collective-permute-start | bytes 983048 | tf_op jit(solution)/shard_map/ppermute | solution.py:58
  20.7 45.0 %collective-permute-start.3 = (bf16[4112,128]{1,0:T(8,128)(2,1)}, bf16[4112,128]{1,0:T(8,128)(2,1)}, u32[]{:S(2)}, u32[]{:S(2)}) collective-permute-start(bf16[4112,128]{1,0:T(8,128)(2,1)} %get-tuple-element.65), channel_id=1, source_target_pairs={{0,2},{1,7},{2,4},{3,1},{4,6},{5,3},{6,0},{7,5},{8,10},{9,15},{10,... | collective-permute-start | bytes 3158024 | tf_op jit(solution)/shard_map/ppermute | solution.py:58
  24.0 41.6 %collective-permute-start.4 = (bf16[4112,128]{1,0:T(8,128)(2,1)}, bf16[4112,128]{1,0:T(8,128)(2,1)}, u32[]{:S(2)}, u32[]{:S(2)}) collective-permute-start(bf16[4112,128]{1,0:T(8,128)(2,1)} %get-tuple-element.67), channel_id=1, source_target_pairs={{0,4},{1,5},{2,6},{3,7},{4,0},{5,1},{6,2},{7,3},{8,12},{9,13},{10,... | collective-permute-start | bytes 3158024 | tf_op jit(solution)/shard_map/ppermute | solution.py:58
  25.8 44.0 %collective-permute-start.5 = (bf16[4112,128]{1,0:T(8,128)(2,1)}, bf16[4112,128]{1,0:T(8,128)(2,1)}, u32[]{:S(2)}, u32[]{:S(2)}) collective-permute-start(bf16[4112,128]{1,0:T(8,128)(2,1)} %get-tuple-element.69), channel_id=1, source_target_pairs={{0,6},{1,3},{2,0},{3,5},{4,2},{5,7},{6,4},{7,1},{8,14},{9,11},{10,... | collective-permute-start | bytes 3158024 | tf_op jit(solution)/shard_map/ppermute | solution.py:58
  27.6 19.6 %all-to-all-start = ((bf16[32,16,256]{2,1,0:T(8,128)(2,1)}), bf16[32,16,256]{2,1,0:T(8,128)(2,1)S(1)}, u32[]{:S(2)}, u32[]{:S(2)}) async-start(bf16[32,16,256]{2,1,0:T(8,128)(2,1)} %bitcast.7), calls=%async_computation | async-start | bytes 524288 | tf_op jit(solution)/shard_map/all_to_all | solution.py:75
  48.0 7.2 %collective-permute-start.6 = (bf16[512,256]{1,0:T(8,128)(2,1)S(1)}, bf16[512,256]{1,0:T(8,128)(2,1)S(1)}, u32[]{:S(2)}, u32[]{:S(2)}) collective-permute-start(bf16[512,256]{1,0:T(8,128)(2,1)S(1)} %shard_map.106.refs_4_), channel_id=1, source_target_pairs={{0,8},{1,25},{2,10},{3,27},{4,12},{5,29},{6,14},{7,31},{8,16},{9,1... | collective-permute-start | bytes 786440 | tf_op jit(solution)/shard_map/ppermute | solution.py:58
  49.2 9.2 %collective-permute-start.8 = (bf16[512,256]{1,0:T(8,128)(2,1)S(1)}, bf16[512,256]{1,0:T(8,128)(2,1)S(1)}, u32[]{:S(2)}, u32[]{:S(2)}) collective-permute-start(bf16[512,256]{1,0:T(8,128)(2,1)S(1)} %shard_map.106.refs_4_), channel_id=1, source_target_pairs={{0,24},{1,9},{2,26},{3,11},{4,28},{5,13},{6,30},{7,15},{8,0},{9,17... | collective-permute-start | bytes 786440 | tf_op jit(solution)/shard_map/ppermute | solution.py:58
  79.1 10.7 %collective-permute-start.13 = (bf16[4096,128]{1,0:T(8,128)(2,1)S(1)}, bf16[4096,128]{1,0:T(8,128)(2,1)S(1)}, u32[]{:S(2)}, u32[]{:S(2)}) collective-permute-start(bf16[4096,128]{1,0:T(8,128)(2,1)S(1)} %get-tuple-element.88), channel_id=1, source_target_pairs={{0,1},{1,0},{2,3},{3,2},{4,5},{5,4},{6,7},{7,6},{8,9},{9,8},{10,11... | collective-permute-start | bytes 3145736 | tf_op jit(solution)/shard_map/ppermute | solution.py:58
  90.1 7.3 %collective-permute-start.14 = (bf16[512,256]{1,0:T(8,128)(2,1)S(1)}, bf16[512,256]{1,0:T(8,128)(2,1)S(1)}, u32[]{:S(2)}, u32[]{:S(2)}) collective-permute-start(bf16[512,256]{1,0:T(8,128)(2,1)S(1)} %get-tuple-element.90), channel_id=1, source_target_pairs={{0,6},{1,3},{2,0},{3,5},{4,2},{5,7},{6,4},{7,1},{8,14},{9,11},{10,... | collective-permute-start | bytes 786440 | tf_op jit(solution)/shard_map/ppermute | solution.py:58
  91.5 8.2 %collective-permute-start.15 = (bf16[512,256]{1,0:T(8,128)(2,1)S(1)}, bf16[512,256]{1,0:T(8,128)(2,1)S(1)}, u32[]{:S(2)}, u32[]{:S(2)}) collective-permute-start(bf16[512,256]{1,0:T(8,128)(2,1)S(1)} %get-tuple-element.92), channel_id=1, source_target_pairs={{0,2},{1,7},{2,4},{3,1},{4,6},{5,3},{6,0},{7,5},{8,10},{9,15},{10,... | collective-permute-start | bytes 786440 | tf_op jit(solution)/shard_map/ppermute | solution.py:58
  93.7 9.3 %collective-permute-start.17 = (bf16[1024,128]{1,0:T(8,128)(2,1)S(1)}, bf16[1024,128]{1,0:T(8,128)(2,1)S(1)}, u32[]{:S(2)}, u32[]{:S(2)}) collective-permute-start(bf16[1024,128]{1,0:T(8,128)(2,1)S(1)} %get-tuple-element.118), channel_id=1, source_target_pairs={{0,16},{1,17},{2,18},{3,19},{4,20},{5,21},{6,22},{7,23},{8,24},{9,... | collective-permute-start | bytes 786440 | tf_op jit(solution)/shard_map/ppermute | solution.py:58
  94.8 14.3 %collective-permute-start.18 = (bf16[1024,128]{1,0:T(8,128)(2,1)S(1)}, bf16[1024,128]{1,0:T(8,128)(2,1)S(1)}, u32[]{:S(2)}, u32[]{:S(2)}) collective-permute-start(bf16[1024,128]{1,0:T(8,128)(2,1)S(1)} %get-tuple-element.119), channel_id=1, source_target_pairs={{0,24},{1,9},{2,26},{3,11},{4,28},{5,13},{6,30},{7,15},{8,0},{9,17... | collective-permute-start | bytes 786440 | tf_op jit(solution)/shard_map/ppermute | solution.py:58
  96.6 12.5 %collective-permute-start.19 = (bf16[1024,128]{1,0:T(8,128)(2,1)S(1)}, bf16[1024,128]{1,0:T(8,128)(2,1)S(1)}, u32[]{:S(2)}, u32[]{:S(2)}) collective-permute-start(bf16[1024,128]{1,0:T(8,128)(2,1)S(1)} %get-tuple-element.117), channel_id=1, source_target_pairs={{0,8},{1,25},{2,10},{3,27},{4,12},{5,29},{6,14},{7,31},{8,16},{9,1... | collective-permute-start | bytes 786440 | tf_op jit(solution)/shard_map/ppermute | solution.py:58
  99.7 9.5 %collective-permute-start.16 = (bf16[512,256]{1,0:T(8,128)(2,1)S(1)}, bf16[512,256]{1,0:T(8,128)(2,1)S(1)}, u32[]{:S(2)}, u32[]{:S(2)}) collective-permute-start(bf16[512,256]{1,0:T(8,128)(2,1)S(1)} %add_convert_fusion.2), channel_id=1, source_target_pairs={{0,2},{1,7},{2,4},{3,1},{4,6},{5,3},{6,0},{7,5},{8,10},{9,15},{10,... | collective-permute-start | bytes 786440 | tf_op jit(solution)/shard_map/ppermute | solution.py:58
  111.8 10.6 %collective-permute-start.27 = (bf16[1024,128]{1,0:T(8,128)(2,1)S(1)}, bf16[1024,128]{1,0:T(8,128)(2,1)S(1)}, u32[]{:S(2)}, u32[]{:S(2)}) collective-permute-start(bf16[1024,128]{1,0:T(8,128)(2,1)S(1)} %fusion.1.refs_4_), channel_id=1, source_target_pairs={{0,2},{1,7},{2,4},{3,1},{4,6},{5,3},{6,0},{7,5},{8,10},{9,15},{10,... | collective-permute-start | bytes 786440 | tf_op jit(solution)/shard_map/ppermute | solution.py:58
  113.5 9.9 %collective-permute-start.28 = (bf16[1024,128]{1,0:T(8,128)(2,1)S(1)}, bf16[1024,128]{1,0:T(8,128)(2,1)S(1)}, u32[]{:S(2)}, u32[]{:S(2)}) collective-permute-start(bf16[1024,128]{1,0:T(8,128)(2,1)S(1)} %fusion.1.refs_4_), channel_id=1, source_target_pairs={{0,4},{1,5},{2,6},{3,7},{4,0},{5,1},{6,2},{7,3},{8,12},{9,13},{10,... | collective-permute-start | bytes 786440 | tf_op jit(solution)/shard_map/ppermute | solution.py:58
  114.7 11.5 %collective-permute-start.29 = (bf16[1024,128]{1,0:T(8,128)(2,1)S(1)}, bf16[1024,128]{1,0:T(8,128)(2,1)S(1)}, u32[]{:S(2)}, u32[]{:S(2)}) collective-permute-start(bf16[1024,128]{1,0:T(8,128)(2,1)S(1)} %fusion.1.refs_4_), channel_id=1, source_target_pairs={{0,6},{1,3},{2,0},{3,5},{4,2},{5,7},{6,4},{7,1},{8,14},{9,11},{10,... | collective-permute-start | bytes 786440 | tf_op jit(solution)/shard_map/ppermute | solution.py:58
  115.5 10.7 %collective-permute-start.22 = (bf16[512,256]{1,0:T(8,128)(2,1)S(1)}, bf16[512,256]{1,0:T(8,128)(2,1)S(1)}, u32[]{:S(2)}, u32[]{:S(2)}) collective-permute-start(bf16[512,256]{1,0:T(8,128)(2,1)S(1)} %add_convert_fusion.1.refs_4_), channel_id=1, source_target_pairs={{0,24},{1,9},{2,26},{3,11},{4,28},{5,13},{6,30},{7,15},{8,0},{9,17... | collective-permute-start | bytes 786440 | tf_op jit(solution)/shard_map/ppermute | solution.py:58
  115.5 10.7 %collective-permute-start.21 = (bf16[512,256]{1,0:T(8,128)(2,1)S(1)}, bf16[512,256]{1,0:T(8,128)(2,1)S(1)}, u32[]{:S(2)}, u32[]{:S(2)}) collective-permute-start(bf16[512,256]{1,0:T(8,128)(2,1)S(1)} %collective-permute-done.20.refs_5_), channel_id=1, source_target_pairs={{0,8},{1,25},{2,10},{3,27},{4,12},{5,29},{6,14},{7,31},{8,16},{9,1... | collective-permute-start | bytes 786440 | tf_op jit(solution)/shard_map/ppermute | solution.py:58
  134.3 8.1 %collective-permute-start.23 = (bf16[512,256]{1,0:T(8,128)(2,1)S(1)}, bf16[512,256]{1,0:T(8,128)(2,1)S(1)}, u32[]{:S(2)}, u32[]{:S(2)}) collective-permute-start(bf16[512,256]{1,0:T(8,128)(2,1)S(1)} %add_convert_fusion.1.refs_4_), channel_id=1, source_target_pairs={{0,1},{1,0},{2,3},{3,2},{4,5},{5,4},{6,7},{7,6},{8,9},{9,8},{10,11... | collective-permute-start | bytes 786440 | tf_op jit(solution)/shard_map/ppermute | solution.py:58
  134.4 8.1 %collective-permute-start.24 = (bf16[512,256]{1,0:T(8,128)(2,1)S(1)}, bf16[512,256]{1,0:T(8,128)(2,1)S(1)}, u32[]{:S(2)}, u32[]{:S(2)}) collective-permute-start(bf16[512,256]{1,0:T(8,128)(2,1)S(1)} %collective-permute-done.20.refs_5_), channel_id=1, source_target_pairs={{0,1},{1,0},{2,3},{3,2},{4,5},{5,4},{6,7},{7,6},{8,9},{9,8},{10,11... | collective-permute-start | bytes 786440 | tf_op jit(solution)/shard_map/ppermute | solution.py:58
  134.9 10.2 %collective-permute-start.26 = (bf16[512,256]{1,0:T(8,128)(2,1)S(1)}, bf16[512,256]{1,0:T(8,128)(2,1)S(1)}, u32[]{:S(2)}, u32[]{:S(2)}) collective-permute-start(bf16[512,256]{1,0:T(8,128)(2,1)S(1)} %collective-permute-done.22.refs_7_), channel_id=1, source_target_pairs={{0,1},{1,0},{2,3},{3,2},{4,5},{5,4},{6,7},{7,6},{8,9},{9,8},{10,11... | collective-permute-start | bytes 786440 | tf_op jit(solution)/shard_map/ppermute | solution.py:58
  135.0 10.1 %collective-permute-start.25 = (bf16[512,256]{1,0:T(8,128)(2,1)S(1)}, bf16[512,256]{1,0:T(8,128)(2,1)S(1)}, u32[]{:S(2)}, u32[]{:S(2)}) collective-permute-start(bf16[512,256]{1,0:T(8,128)(2,1)S(1)} %collective-permute-done.21.refs_6_), channel_id=1, source_target_pairs={{0,1},{1,0},{2,3},{3,2},{4,5},{5,4},{6,7},{7,6},{8,9},{9,8},{10,11... | collective-permute-start | bytes 786440 | tf_op jit(solution)/shard_map/ppermute | solution.py:58
  138.3 14.4 %collective-permute-start.34 = (bf16[1024,128]{1,0:T(8,128)(2,1)S(1)}, bf16[1024,128]{1,0:T(8,128)(2,1)S(1)}, u32[]{:S(2)}, u32[]{:S(2)}) collective-permute-start(bf16[1024,128]{1,0:T(8,128)(2,1)S(1)} %get-tuple-element.115), channel_id=1, source_target_pairs={{0,16},{1,17},{2,18},{3,19},{4,20},{5,21},{6,22},{7,23},{8,24},{9,... | collective-permute-start | bytes 786440 | tf_op jit(solution)/shard_map/ppermute | solution.py:58
  142.4 11.1 %collective-permute-start.35 = (bf16[1024,128]{1,0:T(8,128)(2,1)S(1)}, bf16[1024,128]{1,0:T(8,128)(2,1)S(1)}, u32[]{:S(2)}, u32[]{:S(2)}) collective-permute-start(bf16[1024,128]{1,0:T(8,128)(2,1)S(1)} %get-tuple-element.116), channel_id=1, source_target_pairs={{0,24},{1,9},{2,26},{3,11},{4,28},{5,13},{6,30},{7,15},{8,0},{9,17... | collective-permute-start | bytes 786440 | tf_op jit(solution)/shard_map/ppermute | solution.py:58
  142.5 11.0 %collective-permute-start.36 = (bf16[1024,128]{1,0:T(8,128)(2,1)S(1)}, bf16[1024,128]{1,0:T(8,128)(2,1)S(1)}, u32[]{:S(2)}, u32[]{:S(2)}) collective-permute-start(bf16[1024,128]{1,0:T(8,128)(2,1)S(1)} %get-tuple-element.114), channel_id=1, source_target_pairs={{0,8},{1,25},{2,10},{3,27},{4,12},{5,29},{6,14},{7,31},{8,16},{9,1... | collective-permute-start | bytes 786440 | tf_op jit(solution)/shard_map/ppermute | solution.py:58
  151.2 12.8 %collective-permute-start.32 = (bf16[512,256]{1,0:T(8,128)(2,1)S(1)}, bf16[512,256]{1,0:T(8,128)(2,1)S(1)}, u32[]{:S(2)}, u32[]{:S(2)}) collective-permute-start(bf16[512,256]{1,0:T(8,128)(2,1)S(1)} %get-tuple-element.112), channel_id=1, source_target_pairs={{0,2},{1,7},{2,4},{3,1},{4,6},{5,3},{6,0},{7,5},{8,10},{9,15},{10,... | collective-permute-start | bytes 786440 | tf_op jit(solution)/shard_map/ppermute | solution.py:58
  151.2 25.3 %collective-permute-start.31 = (bf16[512,256]{1,0:T(8,128)(2,1)S(1)}, bf16[512,256]{1,0:T(8,128)(2,1)S(1)}, u32[]{:S(2)}, u32[]{:S(2)}) collective-permute-start(bf16[512,256]{1,0:T(8,128)(2,1)S(1)} %get-tuple-element.110), channel_id=1, source_target_pairs={{0,6},{1,3},{2,0},{3,5},{4,2},{5,7},{6,4},{7,1},{8,14},{9,11},{10,... | collective-permute-start | bytes 786440 | tf_op jit(solution)/shard_map/ppermute | solution.py:58
  155.1 19.9 %all-to-all-start.1 = ((bf16[128,4,256]{2,1,0:T(4,128)(2,1)}), bf16[128,4,256]{2,1,0:T(4,128)(2,1)S(1)}, u32[]{:S(2)}, u32[]{:S(2)}) async-start(bf16[128,4,256]{2,1,0:T(4,128)(2,1)} %reshape.58), calls=%async_computation.1 | async-start | bytes 524288 | tf_op jit(solution)/shard_map/all_to_all | solution.py:64
  164.0 12.5 %collective-permute-start.33 = (bf16[512,256]{1,0:T(8,128)(2,1)S(1)}, bf16[512,256]{1,0:T(8,128)(2,1)S(1)}, u32[]{:S(2)}, u32[]{:S(2)}) collective-permute-start(bf16[512,256]{1,0:T(8,128)(2,1)S(1)} %add_convert_fusion), channel_id=1, source_target_pairs={{0,2},{1,7},{2,4},{3,1},{4,6},{5,3},{6,0},{7,5},{8,10},{9,15},{10,... | collective-permute-start | bytes 786440 | tf_op jit(solution)/shard_map/ppermute | solution.py:58
  (16 other events, 87.6 us)

commit v4 on v3

--- a/solution.py
+++ b/solution.py
@@ -18,6 +18,8 @@
 CAP = SIDE * CORES * OWNER_CAP
 CODE_ROWS = 16
 COUNT_LANE = 64
+UNROLL = 8
+CHUNK = 8
 PACKED = CAP * TILE + CODE_ROWS
 COLUMNS = CORES * SIDE * BLOCKS
 TURNED = BLOCKS * WIDTH
@@ -25,11 +27,12 @@
 SHIPPED = TURNED + PART * WIDTH // TILE
 BF16 = jnp.bfloat16
 F32 = jnp.float32
-VMEM_LIMIT = 24 * 1024 * 1024
+VMEM_LIMIT = 16 * 1024 * 1024
 VMEM_MOST = 62 * 1024 * 1024
 
 WHOLE = pl.BlockSpec(memory_space=pltpu.VMEM)
 FAR = pl.BlockSpec(memory_space=pltpu.HBM)
+ANY = pl.BlockSpec(memory_space=pl.ANY)
 SCALARS = pl.BlockSpec(memory_space=pltpu.SMEM)
 
 
@@ -223,11 +226,46 @@
     )(target, code, tiles)
 
 
-def slot_steps(codes):
-    most = codes[COUNT_LANE]
-    for k in range(1, SIDE):
-        most = jnp.maximum(most, codes[k * TILE + COUNT_LANE])
-    return (most + 1) // 2
+def fetch_packs(codes, packs, tiles, arrived):
+    rows = CHUNK * TILE
+    waits = []
+    for k in range(SIDE):
+        for i in range(CAP // CHUNK):
+            source = packs[k].at[pl.ds(i * rows, rows)]
+            place = tiles.at[pl.ds(k * CAP * TILE + i * rows, rows)]
+            copy = pltpu.make_async_copy(source, place, arrived.at[k * (CAP // CHUNK) + i])
+            used = codes[k * TILE + COUNT_LANE] > i * CHUNK
+            pl.when(used)(copy.start)
+            waits.append((used, copy))
+
+    def wait():
+        for used, copy in waits:
+            pl.when(used)(copy.wait)
+
+    return wait
+
+
+def list_slots(codes, slots):
+    total = jnp.int32(0)
+    for k in range(SIDE):
+
+        def note(n, at, k=k):
+            code = codes[k * TILE + n]
+            slots[0, at] = k * CAP + n
+            slots[1, at] = k * BLOCKS + code // COLUMNS
+            slots[2, at] = code % COLUMNS
+            return at + 1
+
+        total = lax.fori_loop(0, codes[k * TILE + COUNT_LANE], note, total)
+    for u in range(UNROLL):
+        slots[0, total + u] = SIDE * CAP
+        slots[1, total + u] = 0
+        slots[2, total + u] = 0
+    return (total + UNROLL - 1) // UNROLL
+
+
+def slot_block(slots, i, at, size):
+    return pl.ds(pl.multiple_of(slots[i, at] * size, size), size)
 
 
 def fetch(sources, places, arrived):
@@ -243,30 +281,29 @@
 def forward_kernel(codes, *refs):
     packs, refs = refs[:SIDE], refs[SIDE:]
     shards, refs = refs[: CORES * SIDE], refs[CORES * SIDE :]
-    outs, (tiles, features, arrived, *totals) = refs[:SIDE], refs[SIDE:]
-    places = [tiles.at[k] for k in range(SIDE)]
-    places += [features.at[pl.ds(j * NODES, NODES)] for j in range(CORES * SIDE)]
-    copies = fetch([*packs, *shards], places, arrived)
-    for k in range(SIDE):
-        totals[k][...] = jnp.zeros((NODES, WIDTH), F32)
+    outs, (tiles, features, totals, slots, arrived, fetched) = refs[:SIDE], refs[SIDE:]
+    places = [features.at[pl.ds(j * NODES, NODES)] for j in range(CORES * SIDE)]
+    wait = fetch_packs(codes, packs, tiles, fetched)
+    copies = fetch(shards, places, arrived)
+    totals[...] = jnp.zeros(totals.shape, F32)
+    tiles[SIDE * CAP * TILE :, :] = jnp.zeros((TILE, TILE), BF16)
+    steps = list_slots(codes, slots)
     for copy in copies:
         copy.wait()
+    wait()
 
     def step(i, carry):
-        for u in range(2):
-            n = i * 2 + u
-            for k in range(SIDE):
-                code = codes[k * TILE + n]
-                row = pl.multiple_of((code // COLUMNS) * TILE, TILE)
-                column = pl.multiple_of((code % COLUMNS) * TILE, TILE)
-                tile = tiles[k, pl.ds(pl.multiple_of(n * TILE, TILE), TILE), :]
-                block = features[pl.ds(column, TILE), :]
-                totals[k][pl.ds(row, TILE), :] += jnp.dot(tile, block, preferred_element_type=F32)
+        for u in range(UNROLL):
+            at = i * UNROLL + u
+            tile = tiles[slot_block(slots, 0, at, TILE), :]
+            block = features[slot_block(slots, 2, at, TILE), :]
+            to = slot_block(slots, 1, at, TILE)
+            totals[to, :] += jnp.dot(tile, block, preferred_element_type=F32)
         return carry
 
-    lax.fori_loop(0, slot_steps(codes), step, 0)
+    lax.fori_loop(0, steps, step, 0)
     for k in range(SIDE):
-        outs[k][...] = totals[k][...].astype(outs[k].dtype)
+        outs[k][...] = totals[k * NODES : (k + 1) * NODES, :].astype(outs[k].dtype)
 
 
 def forward_product(packs, codes, shards):
@@ -275,65 +312,71 @@
     return pl.pallas_call(
         forward_kernel,
         out_shape=[struct(shape, dtype) for dtype in (F32, BF16, BF16, F32)],
-        in_specs=[SCALARS] + [FAR] * inputs,
+        in_specs=[SCALARS] + [ANY] * inputs,
         out_specs=[WHOLE] * SIDE,
         scratch_shapes=[
-            pltpu.VMEM((SIDE, PACKED, TILE), BF16),
+            pltpu.VMEM(((SIDE * CAP + 1) * TILE, TILE), BF16),
             pltpu.VMEM((CORES * SIDE * NODES, WIDTH), BF16),
-            pltpu.SemaphoreType.DMA((inputs,)),
-        ]
-        + [pltpu.VMEM(shape, F32)] * SIDE,
-        compiler_params=params(),
-        cost_estimate=cost(6e9, 1e6),
-    )(codes, *packs, *shards)
-
-
-def backward_kernel(codes, *refs):
-    packs, refs = refs[:SIDE], refs[SIDE:]
-    shards, refs = refs[:SIDE], refs[SIDE:]
-    near, far, tiles, turned, arrived, totals = refs
-    places = [tiles.at[k] for k in range(SIDE)] + [turned.at[k] for k in range(SIDE)]
-    shards = [shard.at[pl.ds(0, TURNED)] for shard in shards]
-    copies = fetch([*packs, *shards], places, arrived)
-    totals[...] = jnp.zeros(totals.shape, F32)
-    for copy in copies:
-        copy.wait()
-
-    def step(i, carry):
-        for u in range(2):
-            n = i * 2 + u
-            for k in range(SIDE):
-                code = codes[k * TILE + n]
-                row = pl.multiple_of((code // COLUMNS) * WIDTH, WIDTH)
-                column = pl.multiple_of((code % COLUMNS) * WIDTH, WIDTH)
-                tile = tiles[k, pl.ds(pl.multiple_of(n * TILE, TILE), TILE), :]
-                block = turned[k, pl.ds(row, WIDTH), :]
-                totals[pl.ds(column, WIDTH), :] += jnp.dot(block, tile, preferred_element_type=F32)
-        return carry
-
-    lax.fori_loop(0, slot_steps(codes), step, 0)
-    near[...] = totals[: SIDE * TURNED, :]
-    far[...] = totals[SIDE * TURNED :, :].astype(BF16)
-
-
-def backward_product(packs, codes, shards):
-    shape = (SIDE * TURNED, TILE)
-    return pl.pallas_call(
-        backward_kernel,
-        out_shape=[struct(shape, F32), struct(shape, BF16)],
-        in_specs=[SCALARS] + [FAR] * (2 * SIDE),
-        out_specs=[WHOLE] * CORES,
-        scratch_shapes=[
-            pltpu.VMEM((SIDE, PACKED, TILE), BF16),
-            pltpu.VMEM((SIDE, TURNED, TILE), BF16),
-            pltpu.SemaphoreType.DMA((2 * SIDE,)),
-            pltpu.VMEM((CORES * SIDE * TURNED, TILE), F32),
+            pltpu.VMEM((SIDE * NODES, WIDTH), F32),
+            pltpu.SMEM((3, SIDE * CAP + UNROLL), jnp.int32),
+            pltpu.SemaphoreType.DMA((CORES * SIDE,)),
+            pltpu.SemaphoreType.DMA((SIDE * CAP // CHUNK,)),
         ],
         compiler_params=params(),
         cost_estimate=cost(6e9, 1e6),
     )(codes, *packs, *shards)
 
 
+def backward_kernel(codes, *refs):
+    packs, refs = refs[:SIDE], refs[SIDE:]
+    shards, refs = refs[:SIDE], refs[SIDE:]
+    near, refs = refs[:SIDE], refs[SIDE:]
+    far, tiles, turned, totals, slots, arrived, fetched = refs
+    places = [turned.at[pl.ds(k * TURNED, TURNED)] for k in range(SIDE)]
+    wait = fetch_packs(codes, packs, tiles, fetched)
+    copies = fetch([shard.at[pl.ds(0, TURNED)] for shard in shards], places, arrived)
+    totals[...] = jnp.zeros(totals.shape, F32)
+    tiles[SIDE * CAP * TILE :, :] = jnp.zeros((TILE, TILE), BF16)
+    steps = list_slots(codes, slots)
+    for copy in copies:
+        copy.wait()
+    wait()
+
+    def step(i, carry):
+        for u in range(UNROLL):
+            at = i * UNROLL + u
+            tile = tiles[slot_block(slots, 0, at, TILE), :]
+            block = turned[slot_block(slots, 1, at, WIDTH), :]
+            to = slot_block(slots, 2, at, WIDTH)
+            totals[to, :] += jnp.dot(block, tile, preferred_element_type=F32)
+        return carry
+
+    lax.fori_loop(0, steps, step, 0)
+    for j in range(SIDE):
+        near[j][...] = totals[j * TURNED : (j + 1) * TURNED, :]
+    far[...] = totals[SIDE * TURNED :, :].astype(BF16)
+
+
+def backward_product(packs, codes, shards):
+    *near, far = pl.pallas_call(
+        backward_kernel,
+        out_shape=[struct((TURNED, TILE), F32)] * SIDE + [struct((SIDE * TURNED, TILE), BF16)],
+        in_specs=[SCALARS] + [ANY] * (2 * SIDE),
+        out_specs=[WHOLE] * (SIDE + 1),
+        scratch_shapes=[
+            pltpu.VMEM(((SIDE * CAP + 1) * TILE, TILE), BF16),
+            pltpu.VMEM((SIDE * TURNED, TILE), BF16),
+            pltpu.VMEM((CORES * SIDE * TURNED, TILE), F32),
+            pltpu.SMEM((3, SIDE * CAP + UNROLL), jnp.int32),
+            pltpu.SemaphoreType.DMA((SIDE,)),
+            pltpu.SemaphoreType.DMA((SIDE * CAP // CHUNK,)),
+        ],
+        compiler_params=params(),
+        cost_estimate=cost(6e9, 1e6),
+    )(codes, *packs, *shards)
+    return near, far
+
+
 ORDER = (2, 1, 3)
 
 
@@ -356,7 +399,7 @@
 
 def add_cores(near, far):
     parts = [slice(j * TURNED, (j + 1) * TURNED) for j in range(SIDE)]
-    return [near[part] + far[part].astype(F32) for part in parts]
+    return [own + far[part].astype(F32) for own, part in zip(near, parts, strict=True)]
 
 
 def add_up(own, arrived):

time: 178 us -> 173 us (0.972)
  Pallas kernels: 34.3 us -> 31 us
    pallas_call x2, Pallas kernels: 12 us -> 9.96 us  [forward_product(): pl.pallas_call(forward_kernel, out_shape=[struct(shape, dtype) for dtype...]
  transfers between devices with their start and end apart: 39 -> 39, of which waited for: 19 -> 18; matrix products, arithmetic and copies ran while one was open for 3% -> 4% of each run, Pallas kernels for 12% -> 11%
where the time goes in v4:
time: 173 us; the launch traced here: 171 us
  starting transfers between devices  64.6 us (37%)
  waiting for transfers between devices  60.9 us (35%)
  Pallas kernels  31 us (18%)
  local copies, waits for them, and re-layouts  6.45 us (4%)
  other arithmetic  6.36 us (4%)
    ppermute x37, starting transfers between devices, move(): return lax.ppermute(array, 'col', pairs)  46.5 us
    ppermute x37, waiting for transfers between devices, move(): return lax.ppermute(array, 'col', pairs)  45 us
    pallas_call x2, Pallas kernels, backward_product(): pl.pallas_call(backward_kernel, out_shape=[struct((TURNED, TILE), F32)] *...  10.8 us
    all_to_all x1, starting transfers between devices, exchange_planes(): lax.all_to_all(direct, ('row', 'col'), split_axis=0, concat_axis=0, tiled...  10.7 us
    pallas_call x2, Pallas kernels, forward_product(): pl.pallas_call(forward_kernel, out_shape=[struct(shape, dtype) for dtype...  9.96 us
    all_to_all x1, waiting for transfers between devices, exchange_planes(): lax.all_to_all(direct, ('row', 'col'), split_axis=0, concat_axis=0, tiled...  8.75 us
    all_to_all x1, starting transfers between devices, reshuffle(): lax.all_to_all(direct, ('row', 'col'), split_axis=0, concat_axis=0, tiled...  7.3 us
    all_to_all x1, waiting for transfers between devices, reshuffle(): lax.all_to_all(direct, ('row', 'col'), split_axis=0, concat_axis=0, tiled...  7.17 us
  transfers between devices with their start and end apart: 39, of which 18 were waited for; matrix products, arithmetic and copies ran while one was open for 4% of the time, Pallas kernels for 11%

profile of v4, /device:TPU:1, one launch (start us, length us, event | category | flops | bytes accessed | tf_op | source)
XLA Modules:
  0.0 170.9 jit_solution(15253845171315638715)
XLA Ops:
  4.2 3.6 %collective-permute-start = (bf16[1280,128]{1,0:T(8,128)(2,1)}, bf16[1280,128]{1,0:T(8,128)(2,1)S(1)}, u32[]{:S(2)}, u32[]{:S(2)}) collective-permute-start(bf16[1280,128]{1,0:T(8,128)(2,1)} %get-tuple-element.68), channel_id=1, source_target_pairs={{0,2},{1,7},{2,4},{3,1},{4,6},{5,3},{6,0},{7,5},{8,10},{9,15},{10,... | collective-permute-start | bytes 983048 | tf_op jit(solution)/shard_map/ppermute | solution.py:61
  10.1 4.8 %shard_map.107 = (bf16[4112,128]{1,0:T(8,128)(2,1)}, bf16[4112,128]{1,0:T(8,128)(2,1)}, bf16[4112,128]{1,0:T(8,128)(2,1)}, bf16[4112,128]{1,0:T(8,128)(2,1)}) custom-call(s32[96]{0:T(128)} %get-tuple-element.71.target, s32[96]{0:T(128)} %get-tuple-element.140.code, bf16[96,128,128]{2,1,0:T(8,128)(2,1)} %source.1), custom_call_target="tpu_custom_call" | custom-call | flops 1000000 | bytes 7000000 | tf_op jit(solution)/shard_map/pallas_call | solution.py:212
  14.9 5.8 %collective-permute-done.refs_1_.refs_5_ = bf16[1280,128]{1,0:T(8,128)(2,1)S(1)} collective-permute-done((bf16[1280,128]{1,0:T(8,128)(2,1)}, bf16[1280,128]{1,0:T(8,128)(2,1)S(1)}, u32[]{:S(2)}, u32[]{:S(2)}) %collective-permute-start) | collective-permute-done | bytes 327712 | tf_op jit(solution)/shard_map/ppermute | solution.py:61
  20.7 3.3 %collective-permute-start.3 = (bf16[4112,128]{1,0:T(8,128)(2,1)}, bf16[4112,128]{1,0:T(8,128)(2,1)}, u32[]{:S(2)}, u32[]{:S(2)}) collective-permute-start(bf16[4112,128]{1,0:T(8,128)(2,1)} %get-tuple-element.74), channel_id=1, source_target_pairs={{0,2},{1,7},{2,4},{3,1},{4,6},{5,3},{6,0},{7,5},{8,10},{9,15},{10,... | collective-permute-start | bytes 3158024 | tf_op jit(solution)/shard_map/ppermute | solution.py:61
  24.0 1.8 %collective-permute-start.4 = (bf16[4112,128]{1,0:T(8,128)(2,1)}, bf16[4112,128]{1,0:T(8,128)(2,1)}, u32[]{:S(2)}, u32[]{:S(2)}) collective-permute-start(bf16[4112,128]{1,0:T(8,128)(2,1)} %get-tuple-element.76), channel_id=1, source_target_pairs={{0,4},{1,5},{2,6},{3,7},{4,0},{5,1},{6,2},{7,3},{8,12},{9,13},{10,... | collective-permute-start | bytes 3158024 | tf_op jit(solution)/shard_map/ppermute | solution.py:61
  27.6 10.7 %all-to-all-start = ((bf16[32,16,256]{2,1,0:T(8,128)(2,1)}), bf16[32,16,256]{2,1,0:T(8,128)(2,1)S(1)}, u32[]{:S(2)}, u32[]{:S(2)}) async-start(bf16[32,16,256]{2,1,0:T(8,128)(2,1)} %bitcast.7), calls=%async_computation | async-start | bytes 524288 | tf_op jit(solution)/shard_map/all_to_all | solution.py:78
  38.5 8.7 %all-to-all-done = bf16[32,16,256]{2,1,0:T(8,128)(2,1)S(1)} async-done(((bf16[32,16,256]{2,1,0:T(8,128)(2,1)}), bf16[32,16,256]{2,1,0:T(8,128)(2,1)S(1)}, u32[]{:S(2)}, u32[]{:S(2)}) %all-to-all-start) | async-done | bytes 262176 | tf_op jit(solution)/shard_map/all_to_all | solution.py:78
  49.5 5.7 %collective-permute-done.6.refs_5_ = bf16[512,256]{1,0:T(8,128)(2,1)S(1)} collective-permute-done((bf16[512,256]{1,0:T(8,128)(2,1)S(1)}, bf16[512,256]{1,0:T(8,128)(2,1)S(1)}, u32[]{:S(2)}, u32[]{:S(2)}) %collective-permute-start.6) | collective-permute-done | bytes 262176 | tf_op jit(solution)/shard_map/ppermute | solution.py:61
  58.4 2.4 %collective-permute-done.7.refs_6_ = bf16[512,256]{1,0:T(8,128)(2,1)S(1)} collective-permute-done((bf16[512,256]{1,0:T(8,128)(2,1)S(1)}, bf16[512,256]{1,0:T(8,128)(2,1)S(1)}, u32[]{:S(2)}, u32[]{:S(2)}) %collective-permute-start.7) | collective-permute-done | bytes 262176 | tf_op jit(solution)/shard_map/ppermute | solution.py:61
  60.8 4.9 %collective-permute-done.3.refs_1_ = bf16[4112,128]{1,0:T(8,128)(2,1)} collective-permute-done((bf16[4112,128]{1,0:T(8,128)(2,1)}, bf16[4112,128]{1,0:T(8,128)(2,1)}, u32[]{:S(2)}, u32[]{:S(2)}) %collective-permute-start.3) | collective-permute-done | bytes 1052704 | tf_op jit(solution)/shard_map/ppermute | solution.py:61
  65.7 4.1 %collective-permute-done.5.refs_3_ = bf16[4112,128]{1,0:T(8,128)(2,1)} collective-permute-done((bf16[4112,128]{1,0:T(8,128)(2,1)}, bf16[4112,128]{1,0:T(8,128)(2,1)}, u32[]{:S(2)}, u32[]{:S(2)}) %collective-permute-start.5) | collective-permute-done | bytes 1052704 | tf_op jit(solution)/shard_map/ppermute | solution.py:61
  73.1 4.9 %shard_map.108 = (f32[1024,128]{1,0:T(8,128)S(1)}, f32[1024,128]{1,0:T(8,128)S(1)}, f32[1024,128]{1,0:T(8,128)S(1)}, f32[1024,128]{1,0:T(8,128)S(1)}, bf16[4096,128]{1,0:T(8,128)(2,1)S(1)}) custom-call(s32[512]{0:T(512)S(1)} %maximum_convert_fusion.codes, bf16[4112,128]{1,0:T(8,128)(2,1)S(1)} %copy-done.2, bf16[4112,128]{1,0:T(8,128)(2,1)} %collective-permute-done.3.refs_1_, ...), custom_call_target="tpu_custom_call" | custom-call | flops 6000000000 | bytes 1000000 | tf_op jit(solution)/shard_map/pallas_call | solution.py:361
  79.2 1.9 %collective-permute-done.9.refs_8_ = bf16[512,256]{1,0:T(8,128)(2,1)S(1)} collective-permute-done((bf16[512,256]{1,0:T(8,128)(2,1)S(1)}, bf16[512,256]{1,0:T(8,128)(2,1)S(1)}, u32[]{:S(2)}, u32[]{:S(2)}) %collective-permute-start.9) | collective-permute-done | bytes 262176 | tf_op jit(solution)/shard_map/ppermute | solution.py:61
  82.2 4.9 %shard_map.109 = (f32[512,256]{1,0:T(8,128)S(1)}, bf16[512,256]{1,0:T(8,128)(2,1)S(1)}, bf16[512,256]{1,0:T(8,128)(2,1)S(1)}, f32[512,256]{1,0:T(8,128)S(1)}) custom-call(s32[512]{0:T(512)S(1)} %maximum_convert_fusion.codes, bf16[4112,128]{1,0:T(8,128)(2,1)S(1)} %copy-done.3, bf16[4112,128]{1,0:T(8,128)(2,1)} %collective-permute-done.3.refs_1_, ...), custom_call_target="tpu_custom_call" | custom-call | flops 6000000000 | bytes 1000000 | tf_op jit(solution)/shard_map/pallas_call | solution.py:312
  87.4 2.8 %collective-permute-start.14 = (bf16[512,256]{1,0:T(8,128)(2,1)S(1)}, bf16[512,256]{1,0:T(8,128)(2,1)S(1)}, u32[]{:S(2)}, u32[]{:S(2)}) collective-permute-start(bf16[512,256]{1,0:T(8,128)(2,1)S(1)} %get-tuple-element.105), channel_id=1, source_target_pairs={{0,6},{1,3},{2,0},{3,5},{4,2},{5,7},{6,4},{7,1},{8,14},{9,11},{10,... | collective-permute-start | bytes 786440 | tf_op jit(solution)/shard_map/ppermute | solution.py:61
  90.2 4.1 %collective-permute-start.17 = (bf16[1024,128]{1,0:T(8,128)(2,1)S(1)}, bf16[1024,128]{1,0:T(8,128)(2,1)S(1)}, u32[]{:S(2)}, u32[]{:S(2)}) collective-permute-start(bf16[1024,128]{1,0:T(8,128)(2,1)S(1)} %get-tuple-element.136), channel_id=1, source_target_pairs={{0,16},{1,17},{2,18},{3,19},{4,20},{5,21},{6,22},{7,23},{8,24},{9,... | collective-permute-start | bytes 786440 | tf_op jit(solution)/shard_map/ppermute | solution.py:61
  94.3 2.7 %collective-permute-start.19 = (bf16[1024,128]{1,0:T(8,128)(2,1)S(1)}, bf16[1024,128]{1,0:T(8,128)(2,1)S(1)}, u32[]{:S(2)}, u32[]{:S(2)}) collective-permute-start(bf16[1024,128]{1,0:T(8,128)(2,1)S(1)} %get-tuple-element.135), channel_id=1, source_target_pairs={{0,8},{1,25},{2,10},{3,27},{4,12},{5,29},{6,14},{7,31},{8,16},{9,1... | collective-permute-start | bytes 786440 | tf_op jit(solution)/shard_map/ppermute | solution.py:61
  97.0 1.6 collective-permute-start.16
  98.7 2.3 %collective-permute-done.17 = bf16[1024,128]{1,0:T(8,128)(2,1)S(1)} collective-permute-done((bf16[1024,128]{1,0:T(8,128)(2,1)S(1)}, bf16[1024,128]{1,0:T(8,128)(2,1)S(1)}, u32[]{:S(2)}, u32[]{:S(2)}) %collective-permute-start.17) | collective-permute-done | bytes 262176 | tf_op jit(solution)/shard_map/ppermute | solution.py:61
  100.9 3.8 %collective-permute-done.18 = bf16[1024,128]{1,0:T(8,128)(2,1)S(1)} collective-permute-done((bf16[1024,128]{1,0:T(8,128)(2,1)S(1)}, bf16[1024,128]{1,0:T(8,128)(2,1)S(1)}, u32[]{:S(2)}, u32[]{:S(2)}) %collective-permute-start.18) | collective-permute-done | bytes 262176 | tf_op jit(solution)/shard_map/ppermute | solution.py:61
  109.5 1.5 collective-permute-start.22
  111.0 2.2 %collective-permute-start.21 = (bf16[512,256]{1,0:T(8,128)(2,1)S(1)}, bf16[512,256]{1,0:T(8,128)(2,1)}, u32[]{:S(2)}, u32[]{:S(2)}) collective-permute-start(bf16[512,256]{1,0:T(8,128)(2,1)S(1)} %collective-permute-done.20.refs_5_), channel_id=1, source_target_pairs={{0,8},{1,25},{2,10},{3,27},{4,12},{5,29},{6,14},{7,31},{8,16},{9,1... | collective-permute-start | bytes 786440 | tf_op jit(solution)/shard_map/ppermute | solution.py:61
  113.2 3.4 %collective-permute-done.28.refs_6_ = bf16[1024,128]{1,0:T(8,128)(2,1)S(1)} collective-permute-done((bf16[1024,128]{1,0:T(8,128)(2,1)S(1)}, bf16[1024,128]{1,0:T(8,128)(2,1)S(1)}, u32[]{:S(2)}, u32[]{:S(2)}) %collective-permute-start.28) | collective-permute-done | bytes 262176 | tf_op jit(solution)/shard_map/ppermute | solution.py:61
  116.6 4.6 %collective-permute-done.29.refs_7_ = bf16[1024,128]{1,0:T(8,128)(2,1)S(1)} collective-permute-done((bf16[1024,128]{1,0:T(8,128)(2,1)S(1)}, bf16[1024,128]{1,0:T(8,128)(2,1)S(1)}, u32[]{:S(2)}, u32[]{:S(2)}) %collective-permute-start.29) | collective-permute-done | bytes 262176 | tf_op jit(solution)/shard_map/ppermute | solution.py:61
  121.2 5.8 %shard_map.110 = (f32[1024,128]{1,0:T(8,128)S(1)}, f32[1024,128]{1,0:T(8,128)S(1)}, f32[1024,128]{1,0:T(8,128)S(1)}, f32[1024,128]{1,0:T(8,128)S(1)}, bf16[4096,128]{1,0:T(8,128)(2,1)}) custom-call(s32[512]{0:T(512)S(1)} %maximum_convert_fusion.codes, bf16[4112,128]{1,0:T(8,128)(2,1)S(1)} %copy-done.3, bf16[4112,128]{1,0:T(8,128)(2,1)} %collective-permute-done.3.refs_1_, ...), custom_call_target="tpu_custom_call" | custom-call | flops 6000000000 | bytes 1000000 | tf_op jit(solution)/shard_map/pallas_call | solution.py:361
  132.3 3.7 %collective-permute-start.34 = (bf16[1024,128]{1,0:T(8,128)(2,1)S(1)}, bf16[1024,128]{1,0:T(8,128)(2,1)S(1)}, u32[]{:S(2)}, u32[]{:S(2)}) collective-permute-start(bf16[1024,128]{1,0:T(8,128)(2,1)S(1)} %get-tuple-element.133), channel_id=1, source_target_pairs={{0,16},{1,17},{2,18},{3,19},{4,20},{5,21},{6,22},{7,23},{8,24},{9,... | collective-permute-start | bytes 786440 | tf_op jit(solution)/shard_map/ppermute | solution.py:61
  137.1 2.7 %collective-permute-start.36 = (bf16[1024,128]{1,0:T(8,128)(2,1)S(1)}, bf16[1024,128]{1,0:T(8,128)(2,1)S(1)}, u32[]{:S(2)}, u32[]{:S(2)}) collective-permute-start(bf16[1024,128]{1,0:T(8,128)(2,1)S(1)} %get-tuple-element.132), channel_id=1, source_target_pairs={{0,8},{1,25},{2,10},{3,27},{4,12},{5,29},{6,14},{7,31},{8,16},{9,1... | collective-permute-start | bytes 786440 | tf_op jit(solution)/shard_map/ppermute | solution.py:61
  139.7 5.1 %shard_map.111 = (f32[512,256]{1,0:T(8,128)S(1)}, bf16[512,256]{1,0:T(8,128)(2,1)S(1)}, bf16[512,256]{1,0:T(8,128)(2,1)S(1)}, f32[512,256]{1,0:T(8,128)S(1)}) custom-call(s32[512]{0:T(512)S(1)} %maximum_convert_fusion.codes, bf16[4112,128]{1,0:T(8,128)(2,1)S(1)} %copy-done.4, bf16[4112,128]{1,0:T(8,128)(2,1)} %collective-permute-done.3.refs_1_, ...), custom_call_target="tpu_custom_call" | custom-call | flops 6000000000 | bytes 1000000 | tf_op jit(solution)/shard_map/pallas_call | solution.py:312
  146.4 2.1 %collective-permute-done.35 = bf16[1024,128]{1,0:T(8,128)(2,1)S(1)} collective-permute-done((bf16[1024,128]{1,0:T(8,128)(2,1)S(1)}, bf16[1024,128]{1,0:T(8,128)(2,1)S(1)}, u32[]{:S(2)}, u32[]{:S(2)}) %collective-permute-start.35) | collective-permute-done | bytes 262176 | tf_op jit(solution)/shard_map/ppermute | solution.py:61
  150.1 7.3 %all-to-all-start.1 = ((bf16[128,4,256]{2,1,0:T(4,128)(2,1)}), bf16[128,4,256]{2,1,0:T(4,128)(2,1)S(1)}, u32[]{:S(2)}, u32[]{:S(2)}) async-start(bf16[128,4,256]{2,1,0:T(4,128)(2,1)} %reshape.58), calls=%async_computation.1 | async-start | bytes 524288 | tf_op jit(solution)/shard_map/all_to_all | solution.py:67
  158.5 2.7 %collective-permute-start.33 = (bf16[512,256]{1,0:T(8,128)(2,1)S(1)}, bf16[512,256]{1,0:T(8,128)(2,1)S(1)}, u32[]{:S(2)}, u32[]{:S(2)}) collective-permute-start(bf16[512,256]{1,0:T(8,128)(2,1)S(1)} %add_convert_fusion), channel_id=1, source_target_pairs={{0,2},{1,7},{2,4},{3,1},{4,6},{5,3},{6,0},{7,5},{8,10},{9,15},{10,... | collective-permute-start | bytes 786440 | tf_op jit(solution)/shard_map/ppermute | solution.py:61
  161.4 7.2 %all-to-all-done.1 = bf16[128,4,256]{2,1,0:T(4,128)(2,1)S(1)} async-done(((bf16[128,4,256]{2,1,0:T(4,128)(2,1)}), bf16[128,4,256]{2,1,0:T(4,128)(2,1)S(1)}, u32[]{:S(2)}, u32[]{:S(2)}) %all-to-all-start.1) | async-done | bytes 262176 | tf_op jit(solution)/shard_map/all_to_all | solution.py:67
  (96 shorter events, 36.2 us)
Async XLA Ops:
  4.2 16.5 %collective-permute-start = (bf16[1280,128]{1,0:T(8,128)(2,1)}, bf16[1280,128]{1,0:T(8,128)(2,1)S(1)}, u32[]{:S(2)}, u32[]{:S(2)}) collective-permute-start(bf16[1280,128]{1,0:T(8,128)(2,1)} %get-tuple-element.68), channel_id=1, source_target_pairs={{0,2},{1,7},{2,4},{3,1},{4,6},{5,3},{6,0},{7,5},{8,10},{9,15},{10,... | collective-permute-start | bytes 983048 | tf_op jit(solution)/shard_map/ppermute | solution.py:61
  7.8 16.2 %collective-permute-start.1 = (bf16[1280,128]{1,0:T(8,128)(2,1)}, bf16[1280,128]{1,0:T(8,128)(2,1)S(1)}, u32[]{:S(2)}, u32[]{:S(2)}) collective-permute-start(bf16[1280,128]{1,0:T(8,128)(2,1)} %get-tuple-element.69), channel_id=1, source_target_pairs={{0,4},{1,5},{2,6},{3,7},{4,0},{5,1},{6,2},{7,3},{8,12},{9,13},{10,... | collective-permute-start | bytes 983048 | tf_op jit(solution)/shard_map/ppermute | solution.py:61
  8.1 15.9 %collective-permute-start.2 = (bf16[1280,128]{1,0:T(8,128)(2,1)}, bf16[1280,128]{1,0:T(8,128)(2,1)S(1)}, u32[]{:S(2)}, u32[]{:S(2)}) collective-permute-start(bf16[1280,128]{1,0:T(8,128)(2,1)} %get-tuple-element.70), channel_id=1, source_target_pairs={{0,6},{1,3},{2,0},{3,5},{4,2},{5,7},{6,4},{7,1},{8,14},{9,11},{10,... | collective-permute-start | bytes 983048 | tf_op jit(solution)/shard_map/ppermute | solution.py:61
  20.7 45.0 %collective-permute-start.3 = (bf16[4112,128]{1,0:T(8,128)(2,1)}, bf16[4112,128]{1,0:T(8,128)(2,1)}, u32[]{:S(2)}, u32[]{:S(2)}) collective-permute-start(bf16[4112,128]{1,0:T(8,128)(2,1)} %get-tuple-element.74), channel_id=1, source_target_pairs={{0,2},{1,7},{2,4},{3,1},{4,6},{5,3},{6,0},{7,5},{8,10},{9,15},{10,... | collective-permute-start | bytes 3158024 | tf_op jit(solution)/shard_map/ppermute | solution.py:61
  24.0 41.6 %collective-permute-start.4 = (bf16[4112,128]{1,0:T(8,128)(2,1)}, bf16[4112,128]{1,0:T(8,128)(2,1)}, u32[]{:S(2)}, u32[]{:S(2)}) collective-permute-start(bf16[4112,128]{1,0:T(8,128)(2,1)} %get-tuple-element.76), channel_id=1, source_target_pairs={{0,4},{1,5},{2,6},{3,7},{4,0},{5,1},{6,2},{7,3},{8,12},{9,13},{10,... | collective-permute-start | bytes 3158024 | tf_op jit(solution)/shard_map/ppermute | solution.py:61
  25.8 44.0 %collective-permute-start.5 = (bf16[4112,128]{1,0:T(8,128)(2,1)}, bf16[4112,128]{1,0:T(8,128)(2,1)}, u32[]{:S(2)}, u32[]{:S(2)}) collective-permute-start(bf16[4112,128]{1,0:T(8,128)(2,1)} %get-tuple-element.78), channel_id=1, source_target_pairs={{0,6},{1,3},{2,0},{3,5},{4,2},{5,7},{6,4},{7,1},{8,14},{9,11},{10,... | collective-permute-start | bytes 3158024 | tf_op jit(solution)/shard_map/ppermute | solution.py:61
  27.6 19.6 %all-to-all-start = ((bf16[32,16,256]{2,1,0:T(8,128)(2,1)}), bf16[32,16,256]{2,1,0:T(8,128)(2,1)S(1)}, u32[]{:S(2)}, u32[]{:S(2)}) async-start(bf16[32,16,256]{2,1,0:T(8,128)(2,1)} %bitcast.7), calls=%async_computation | async-start | bytes 524288 | tf_op jit(solution)/shard_map/all_to_all | solution.py:78
  48.0 7.2 %collective-permute-start.6 = (bf16[512,256]{1,0:T(8,128)(2,1)S(1)}, bf16[512,256]{1,0:T(8,128)(2,1)S(1)}, u32[]{:S(2)}, u32[]{:S(2)}) collective-permute-start(bf16[512,256]{1,0:T(8,128)(2,1)S(1)} %shard_map.106.refs_4_), channel_id=1, source_target_pairs={{0,8},{1,25},{2,10},{3,27},{4,12},{5,29},{6,14},{7,31},{8,16},{9,1... | collective-permute-start | bytes 786440 | tf_op jit(solution)/shard_map/ppermute | solution.py:61
  49.2 9.2 %collective-permute-start.8 = (bf16[512,256]{1,0:T(8,128)(2,1)S(1)}, bf16[512,256]{1,0:T(8,128)(2,1)S(1)}, u32[]{:S(2)}, u32[]{:S(2)}) collective-permute-start(bf16[512,256]{1,0:T(8,128)(2,1)S(1)} %shard_map.106.refs_4_), channel_id=1, source_target_pairs={{0,24},{1,9},{2,26},{3,11},{4,28},{5,13},{6,30},{7,15},{8,0},{9,17... | collective-permute-start | bytes 786440 | tf_op jit(solution)/shard_map/ppermute | solution.py:61
  78.0 9.1 %collective-permute-start.13 = (bf16[4096,128]{1,0:T(8,128)(2,1)S(1)}, bf16[4096,128]{1,0:T(8,128)(2,1)S(1)}, u32[]{:S(2)}, u32[]{:S(2)}) collective-permute-start(bf16[4096,128]{1,0:T(8,128)(2,1)S(1)} %get-tuple-element.100), channel_id=1, source_target_pairs={{0,1},{1,0},{2,3},{3,2},{4,5},{5,4},{6,7},{7,6},{8,9},{9,8},{10,11... | collective-permute-start | bytes 3145736 | tf_op jit(solution)/shard_map/ppermute | solution.py:61
  87.4 9.6 %collective-permute-start.14 = (bf16[512,256]{1,0:T(8,128)(2,1)S(1)}, bf16[512,256]{1,0:T(8,128)(2,1)S(1)}, u32[]{:S(2)}, u32[]{:S(2)}) collective-permute-start(bf16[512,256]{1,0:T(8,128)(2,1)S(1)} %get-tuple-element.105), channel_id=1, source_target_pairs={{0,6},{1,3},{2,0},{3,5},{4,2},{5,7},{6,4},{7,1},{8,14},{9,11},{10,... | collective-permute-start | bytes 786440 | tf_op jit(solution)/shard_map/ppermute | solution.py:61
  90.2 6.8 %collective-permute-start.15 = (bf16[512,256]{1,0:T(8,128)(2,1)S(1)}, bf16[512,256]{1,0:T(8,128)(2,1)S(1)}, u32[]{:S(2)}, u32[]{:S(2)}) collective-permute-start(bf16[512,256]{1,0:T(8,128)(2,1)S(1)} %get-tuple-element.107), channel_id=1, source_target_pairs={{0,2},{1,7},{2,4},{3,1},{4,6},{5,3},{6,0},{7,5},{8,10},{9,15},{10,... | collective-permute-start | bytes 786440 | tf_op jit(solution)/shard_map/ppermute | solution.py:61
  90.2 10.7 %collective-permute-start.17 = (bf16[1024,128]{1,0:T(8,128)(2,1)S(1)}, bf16[1024,128]{1,0:T(8,128)(2,1)S(1)}, u32[]{:S(2)}, u32[]{:S(2)}) collective-permute-start(bf16[1024,128]{1,0:T(8,128)(2,1)S(1)} %get-tuple-element.136), channel_id=1, source_target_pairs={{0,16},{1,17},{2,18},{3,19},{4,20},{5,21},{6,22},{7,23},{8,24},{9,... | collective-permute-start | bytes 786440 | tf_op jit(solution)/shard_map/ppermute | solution.py:61
  94.3 10.5 %collective-permute-start.18 = (bf16[1024,128]{1,0:T(8,128)(2,1)S(1)}, bf16[1024,128]{1,0:T(8,128)(2,1)S(1)}, u32[]{:S(2)}, u32[]{:S(2)}) collective-permute-start(bf16[1024,128]{1,0:T(8,128)(2,1)S(1)} %get-tuple-element.137), channel_id=1, source_target_pairs={{0,24},{1,9},{2,26},{3,11},{4,28},{5,13},{6,30},{7,15},{8,0},{9,17... | collective-permute-start | bytes 786440 | tf_op jit(solution)/shard_map/ppermute | solution.py:61
  94.3 10.5 %collective-permute-start.19 = (bf16[1024,128]{1,0:T(8,128)(2,1)S(1)}, bf16[1024,128]{1,0:T(8,128)(2,1)S(1)}, u32[]{:S(2)}, u32[]{:S(2)}) collective-permute-start(bf16[1024,128]{1,0:T(8,128)(2,1)S(1)} %get-tuple-element.135), channel_id=1, source_target_pairs={{0,8},{1,25},{2,10},{3,27},{4,12},{5,29},{6,14},{7,31},{8,16},{9,1... | collective-permute-start | bytes 786440 | tf_op jit(solution)/shard_map/ppermute | solution.py:61
  97.0 7.9 %collective-permute-start.16 = (bf16[512,256]{1,0:T(8,128)(2,1)S(1)}, bf16[512,256]{1,0:T(8,128)(2,1)S(1)}, u32[]{:S(2)}, u32[]{:S(2)}) collective-permute-start(bf16[512,256]{1,0:T(8,128)(2,1)S(1)} %add_convert_fusion.2), channel_id=1, source_target_pairs={{0,2},{1,7},{2,4},{3,1},{4,6},{5,3},{6,0},{7,5},{8,10},{9,15},{10,... | collective-permute-start | bytes 786440 | tf_op jit(solution)/shard_map/ppermute | solution.py:61
  106.5 6.7 %collective-permute-start.27 = (bf16[1024,128]{1,0:T(8,128)(2,1)S(1)}, bf16[1024,128]{1,0:T(8,128)(2,1)S(1)}, u32[]{:S(2)}, u32[]{:S(2)}) collective-permute-start(bf16[1024,128]{1,0:T(8,128)(2,1)S(1)} %fusion.1.refs_4_), channel_id=1, source_target_pairs={{0,2},{1,7},{2,4},{3,1},{4,6},{5,3},{6,0},{7,5},{8,10},{9,15},{10,... | collective-permute-start | bytes 786440 | tf_op jit(solution)/shard_map/ppermute | solution.py:61
  107.7 8.8 %collective-permute-start.28 = (bf16[1024,128]{1,0:T(8,128)(2,1)S(1)}, bf16[1024,128]{1,0:T(8,128)(2,1)S(1)}, u32[]{:S(2)}, u32[]{:S(2)}) collective-permute-start(bf16[1024,128]{1,0:T(8,128)(2,1)S(1)} %fusion.1.refs_4_), channel_id=1, source_target_pairs={{0,4},{1,5},{2,6},{3,7},{4,0},{5,1},{6,2},{7,3},{8,12},{9,13},{10,... | collective-permute-start | bytes 786440 | tf_op jit(solution)/shard_map/ppermute | solution.py:61
  109.1 12.0 %collective-permute-start.29 = (bf16[1024,128]{1,0:T(8,128)(2,1)S(1)}, bf16[1024,128]{1,0:T(8,128)(2,1)S(1)}, u32[]{:S(2)}, u32[]{:S(2)}) collective-permute-start(bf16[1024,128]{1,0:T(8,128)(2,1)S(1)} %fusion.1.refs_4_), channel_id=1, source_target_pairs={{0,6},{1,3},{2,0},{3,5},{4,2},{5,7},{6,4},{7,1},{8,14},{9,11},{10,... | collective-permute-start | bytes 786440 | tf_op jit(solution)/shard_map/ppermute | solution.py:61
  109.5 11.6 %collective-permute-start.22 = (bf16[512,256]{1,0:T(8,128)(2,1)S(1)}, bf16[512,256]{1,0:T(8,128)(2,1)}, u32[]{:S(2)}, u32[]{:S(2)}) collective-permute-start(bf16[512,256]{1,0:T(8,128)(2,1)S(1)} %add_convert_fusion.1.refs_4_), channel_id=1, source_target_pairs={{0,24},{1,9},{2,26},{3,11},{4,28},{5,13},{6,30},{7,15},{8,0},{9,17... | collective-permute-start | bytes 786440 | tf_op jit(solution)/shard_map/ppermute | solution.py:61
  111.0 10.2 %collective-permute-start.21 = (bf16[512,256]{1,0:T(8,128)(2,1)S(1)}, bf16[512,256]{1,0:T(8,128)(2,1)}, u32[]{:S(2)}, u32[]{:S(2)}) collective-permute-start(bf16[512,256]{1,0:T(8,128)(2,1)S(1)} %collective-permute-done.20.refs_5_), channel_id=1, source_target_pairs={{0,8},{1,25},{2,10},{3,27},{4,12},{5,29},{6,14},{7,31},{8,16},{9,1... | collective-permute-start | bytes 786440 | tf_op jit(solution)/shard_map/ppermute | solution.py:61
  128.5 8.5 %collective-permute-start.23 = (bf16[512,256]{1,0:T(8,128)(2,1)S(1)}, bf16[512,256]{1,0:T(8,128)(2,1)S(1)}, u32[]{:S(2)}, u32[]{:S(2)}) collective-permute-start(bf16[512,256]{1,0:T(8,128)(2,1)S(1)} %add_convert_fusion.1.refs_4_), channel_id=1, source_target_pairs={{0,1},{1,0},{2,3},{3,2},{4,5},{5,4},{6,7},{7,6},{8,9},{9,8},{10,11... | collective-permute-start | bytes 786440 | tf_op jit(solution)/shard_map/ppermute | solution.py:61
  128.6 8.5 %collective-permute-start.24 = (bf16[512,256]{1,0:T(8,128)(2,1)S(1)}, bf16[512,256]{1,0:T(8,128)(2,1)S(1)}, u32[]{:S(2)}, u32[]{:S(2)}) collective-permute-start(bf16[512,256]{1,0:T(8,128)(2,1)S(1)} %collective-permute-done.20.refs_5_), channel_id=1, source_target_pairs={{0,1},{1,0},{2,3},{3,2},{4,5},{5,4},{6,7},{7,6},{8,9},{9,8},{10,11... | collective-permute-start | bytes 786440 | tf_op jit(solution)/shard_map/ppermute | solution.py:61
  129.1 10.7 %collective-permute-start.26 = (bf16[512,256]{1,0:T(8,128)(2,1)}, bf16[512,256]{1,0:T(8,128)(2,1)S(1)}, u32[]{:S(2)}, u32[]{:S(2)}) collective-permute-start(bf16[512,256]{1,0:T(8,128)(2,1)} %collective-permute-done.22.refs_7_), channel_id=1, source_target_pairs={{0,1},{1,0},{2,3},{3,2},{4,5},{5,4},{6,7},{7,6},{8,9},{9,8},{10,11... | collective-permute-start | bytes 786440 | tf_op jit(solution)/shard_map/ppermute | solution.py:61
  129.2 10.6 %collective-permute-start.25 = (bf16[512,256]{1,0:T(8,128)(2,1)}, bf16[512,256]{1,0:T(8,128)(2,1)S(1)}, u32[]{:S(2)}, u32[]{:S(2)}) collective-permute-start(bf16[512,256]{1,0:T(8,128)(2,1)} %collective-permute-done.21.refs_6_), channel_id=1, source_target_pairs={{0,1},{1,0},{2,3},{3,2},{4,5},{5,4},{6,7},{7,6},{8,9},{9,8},{10,11... | collective-permute-start | bytes 786440 | tf_op jit(solution)/shard_map/ppermute | solution.py:61
  132.3 14.1 %collective-permute-start.34 = (bf16[1024,128]{1,0:T(8,128)(2,1)S(1)}, bf16[1024,128]{1,0:T(8,128)(2,1)S(1)}, u32[]{:S(2)}, u32[]{:S(2)}) collective-permute-start(bf16[1024,128]{1,0:T(8,128)(2,1)S(1)} %get-tuple-element.133), channel_id=1, source_target_pairs={{0,16},{1,17},{2,18},{3,19},{4,20},{5,21},{6,22},{7,23},{8,24},{9,... | collective-permute-start | bytes 786440 | tf_op jit(solution)/shard_map/ppermute | solution.py:61
  137.0 11.5 %collective-permute-start.35 = (bf16[1024,128]{1,0:T(8,128)(2,1)S(1)}, bf16[1024,128]{1,0:T(8,128)(2,1)S(1)}, u32[]{:S(2)}, u32[]{:S(2)}) collective-permute-start(bf16[1024,128]{1,0:T(8,128)(2,1)S(1)} %get-tuple-element.134), channel_id=1, source_target_pairs={{0,24},{1,9},{2,26},{3,11},{4,28},{5,13},{6,30},{7,15},{8,0},{9,17... | collective-permute-start | bytes 786440 | tf_op jit(solution)/shard_map/ppermute | solution.py:61
  137.1 11.4 %collective-permute-start.36 = (bf16[1024,128]{1,0:T(8,128)(2,1)S(1)}, bf16[1024,128]{1,0:T(8,128)(2,1)S(1)}, u32[]{:S(2)}, u32[]{:S(2)}) collective-permute-start(bf16[1024,128]{1,0:T(8,128)(2,1)S(1)} %get-tuple-element.132), channel_id=1, source_target_pairs={{0,8},{1,25},{2,10},{3,27},{4,12},{5,29},{6,14},{7,31},{8,16},{9,1... | collective-permute-start | bytes 786440 | tf_op jit(solution)/shard_map/ppermute | solution.py:61
  144.8 12.6 %collective-permute-start.32 = (bf16[512,256]{1,0:T(8,128)(2,1)S(1)}, bf16[512,256]{1,0:T(8,128)(2,1)}, u32[]{:S(2)}, u32[]{:S(2)}) collective-permute-start(bf16[512,256]{1,0:T(8,128)(2,1)S(1)} %get-tuple-element.130), channel_id=1, source_target_pairs={{0,2},{1,7},{2,4},{3,1},{4,6},{5,3},{6,0},{7,5},{8,10},{9,15},{10,... | collective-permute-start | bytes 786440 | tf_op jit(solution)/shard_map/ppermute | solution.py:61
  144.9 25.1 %collective-permute-start.31 = (bf16[512,256]{1,0:T(8,128)(2,1)S(1)}, bf16[512,256]{1,0:T(8,128)(2,1)S(1)}, u32[]{:S(2)}, u32[]{:S(2)}) collective-permute-start(bf16[512,256]{1,0:T(8,128)(2,1)S(1)} %get-tuple-element.128), channel_id=1, source_target_pairs={{0,6},{1,3},{2,0},{3,5},{4,2},{5,7},{6,4},{7,1},{8,14},{9,11},{10,... | collective-permute-start | bytes 786440 | tf_op jit(solution)/shard_map/ppermute | solution.py:61
  150.1 18.4 %all-to-all-start.1 = ((bf16[128,4,256]{2,1,0:T(4,128)(2,1)}), bf16[128,4,256]{2,1,0:T(4,128)(2,1)S(1)}, u32[]{:S(2)}, u32[]{:S(2)}) async-start(bf16[128,4,256]{2,1,0:T(4,128)(2,1)} %reshape.58), calls=%async_computation.1 | async-start | bytes 524288 | tf_op jit(solution)/shard_map/all_to_all | solution.py:67
  158.5 11.5 %collective-permute-start.33 = (bf16[512,256]{1,0:T(8,128)(2,1)S(1)}, bf16[512,256]{1,0:T(8,128)(2,1)S(1)}, u32[]{:S(2)}, u32[]{:S(2)}) collective-permute-start(bf16[512,256]{1,0:T(8,128)(2,1)S(1)} %add_convert_fusion), channel_id=1, source_target_pairs={{0,2},{1,7},{2,4},{3,1},{4,6},{5,3},{6,0},{7,5},{8,10},{9,15},{10,... | collective-permute-start | bytes 786440 | tf_op jit(solution)/shard_map/ppermute | solution.py:61
  (15 other events, 86.2 us)

commit v5 on v4

--- a/solution.py
+++ b/solution.py
@@ -18,7 +18,7 @@
 CAP = SIDE * CORES * OWNER_CAP
 CODE_ROWS = 16
 COUNT_LANE = 64
-UNROLL = 8
+UNROLL = 16
 CHUNK = 8
 PACKED = CAP * TILE + CODE_ROWS
 COLUMNS = CORES * SIDE * BLOCKS
@@ -353,14 +353,16 @@
 
     lax.fori_loop(0, steps, step, 0)
     for j in range(SIDE):
-        near[j][...] = totals[j * TURNED : (j + 1) * TURNED, :]
+        near[j][...] = totals[j * TURNED : (j + 1) * TURNED, :].astype(near[j].dtype)
     far[...] = totals[SIDE * TURNED :, :].astype(BF16)
 
 
 def backward_product(packs, codes, shards):
     *near, far = pl.pallas_call(
         backward_kernel,
-        out_shape=[struct((TURNED, TILE), F32)] * SIDE + [struct((SIDE * TURNED, TILE), BF16)],
+        out_shape=[struct((TURNED, TILE), F32)]
+        + [struct((TURNED, TILE), BF16)] * (SIDE - 1)
+        + [struct((SIDE * TURNED, TILE), BF16)],
         in_specs=[SCALARS] + [ANY] * (2 * SIDE),
         out_specs=[WHOLE] * (SIDE + 1),
         scratch_shapes=[
@@ -399,7 +401,8 @@
 
 def add_cores(near, far):
     parts = [slice(j * TURNED, (j + 1) * TURNED) for j in range(SIDE)]
-    return [own + far[part].astype(F32) for own, part in zip(near, parts, strict=True)]
+    pairs = zip(near, parts, strict=True)
+    return [own.astype(F32) + far[part].astype(F32) for own, part in pairs]
 
 
 def add_up(own, arrived):

time: 173 us -> 169 us (0.977); the launches traced: 171 us -> 169 us
  waiting for transfers between devices: 60.9 us -> 69.7 us
  Pallas kernels: 31 us -> 25.1 us
  starting transfers between devices: 64.6 us -> 60.8 us
    ppermute x37, waiting for transfers between devices: 45 us -> 53.4 us  [move(): return lax.ppermute(array, 'col', pairs)]
    ppermute x37, starting transfers between devices: 46.5 us -> 42.6 us  [move(): return lax.ppermute(array, 'col', pairs)]
    pallas_call x2, Pallas kernels: 10.8 us -> 7.35 us  [backward_product(): pl.pallas_call(backward_kernel, out_shape=[struct((TURNED, TILE), F32)] +...]
    add x4 -> x0, other arithmetic: 2.54 us -> none  [add_cores(): own + far[part].astype(F32)]
    pallas_call x2, Pallas kernels: 9.96 us -> 7.51 us  [forward_product(): pl.pallas_call(forward_kernel, out_shape=[struct(shape, dtype) for dtype...]
    convert_element_type x0 -> x2, other arithmetic: none -> 1.76 us  [both_products(): got = {j: move(columns[j].astype(BF16), 'x', -j) for j in ORDER}]
  transfers between devices with their start and end apart: 39 -> 39, of which waited for: 18 -> 20; matrix products, arithmetic and copies ran while one was open for 4% -> 3% of each run, Pallas kernels for 11% -> 10%
where the time goes in v5:
time: 169 us
  waiting for transfers between devices  69.7 us (41%)
  starting transfers between devices  60.8 us (36%)
  Pallas kernels  25.1 us (15%)
  local copies, waits for them, and re-layouts  6.45 us (4%)
  other arithmetic  5.31 us (3%)
    ppermute x37, waiting for transfers between devices, move(): return lax.ppermute(array, 'col', pairs)  53.4 us
    ppermute x37, starting transfers between devices, move(): return lax.ppermute(array, 'col', pairs)  42.6 us
    all_to_all x1, starting transfers between devices, exchange_planes(): lax.all_to_all(direct, ('row', 'col'), split_axis=0, concat_axis=0, tiled...  10.7 us
    all_to_all x1, waiting for transfers between devices, exchange_planes(): lax.all_to_all(direct, ('row', 'col'), split_axis=0, concat_axis=0, tiled...  8.75 us
    all_to_all x1, waiting for transfers between devices, reshuffle(): lax.all_to_all(direct, ('row', 'col'), split_axis=0, concat_axis=0, tiled...  7.51 us
    pallas_call x2, Pallas kernels, forward_product(): pl.pallas_call(forward_kernel, out_shape=[struct(shape, dtype) for dtype...  7.51 us
    all_to_all x1, starting transfers between devices, reshuffle(): lax.all_to_all(direct, ('row', 'col'), split_axis=0, concat_axis=0, tiled...  7.44 us
    pallas_call x2, Pallas kernels, backward_product(): pl.pallas_call(backward_kernel, out_shape=[struct((TURNED, TILE), F32)] +...  7.35 us
  transfers between devices with their start and end apart: 39, of which 20 were waited for; matrix products, arithmetic and copies ran while one was open for 3% of the time, Pallas kernels for 10%

profile of v5, /device:TPU:1, one launch (start us, length us, event | category | flops | bytes accessed | tf_op | source)
XLA Modules:
  0.0 169.0 jit_solution(10067426605401230434)
XLA Ops:
  4.2 3.6 %collective-permute-start = (bf16[1280,128]{1,0:T(8,128)(2,1)}, bf16[1280,128]{1,0:T(8,128)(2,1)S(1)}, u32[]{:S(2)}, u32[]{:S(2)}) collective-permute-start(bf16[1280,128]{1,0:T(8,128)(2,1)} %get-tuple-element.68), channel_id=1, source_target_pairs={{0,2},{1,7},{2,4},{3,1},{4,6},{5,3},{6,0},{7,5},{8,10},{9,15},{10,... | collective-permute-start | bytes 983048 | tf_op jit(solution)/shard_map/ppermute | solution.py:61
  10.1 4.8 %shard_map.107 = (bf16[4112,128]{1,0:T(8,128)(2,1)}, bf16[4112,128]{1,0:T(8,128)(2,1)}, bf16[4112,128]{1,0:T(8,128)(2,1)}, bf16[4112,128]{1,0:T(8,128)(2,1)}) custom-call(s32[96]{0:T(128)} %get-tuple-element.71.target, s32[96]{0:T(128)} %get-tuple-element.142.code, bf16[96,128,128]{2,1,0:T(8,128)(2,1)} %source.1), custom_call_target="tpu_custom_call" | custom-call | flops 1000000 | bytes 7000000 | tf_op jit(solution)/shard_map/pallas_call | solution.py:212
  14.9 5.8 %collective-permute-done.refs_1_.refs_5_ = bf16[1280,128]{1,0:T(8,128)(2,1)S(1)} collective-permute-done((bf16[1280,128]{1,0:T(8,128)(2,1)}, bf16[1280,128]{1,0:T(8,128)(2,1)S(1)}, u32[]{:S(2)}, u32[]{:S(2)}) %collective-permute-start) | collective-permute-done | bytes 327712 | tf_op jit(solution)/shard_map/ppermute | solution.py:61
  20.7 3.3 %collective-permute-start.3 = (bf16[4112,128]{1,0:T(8,128)(2,1)}, bf16[4112,128]{1,0:T(8,128)(2,1)}, u32[]{:S(2)}, u32[]{:S(2)}) collective-permute-start(bf16[4112,128]{1,0:T(8,128)(2,1)} %get-tuple-element.74), channel_id=1, source_target_pairs={{0,2},{1,7},{2,4},{3,1},{4,6},{5,3},{6,0},{7,5},{8,10},{9,15},{10,... | collective-permute-start | bytes 3158024 | tf_op jit(solution)/shard_map/ppermute | solution.py:61
  24.0 1.8 %collective-permute-start.4 = (bf16[4112,128]{1,0:T(8,128)(2,1)}, bf16[4112,128]{1,0:T(8,128)(2,1)}, u32[]{:S(2)}, u32[]{:S(2)}) collective-permute-start(bf16[4112,128]{1,0:T(8,128)(2,1)} %get-tuple-element.76), channel_id=1, source_target_pairs={{0,4},{1,5},{2,6},{3,7},{4,0},{5,1},{6,2},{7,3},{8,12},{9,13},{10,... | collective-permute-start | bytes 3158024 | tf_op jit(solution)/shard_map/ppermute | solution.py:61
  27.6 10.7 %all-to-all-start = ((bf16[32,16,256]{2,1,0:T(8,128)(2,1)}), bf16[32,16,256]{2,1,0:T(8,128)(2,1)S(1)}, u32[]{:S(2)}, u32[]{:S(2)}) async-start(bf16[32,16,256]{2,1,0:T(8,128)(2,1)} %bitcast.7), calls=%async_computation | async-start | bytes 524288 | tf_op jit(solution)/shard_map/all_to_all | solution.py:78
  38.5 8.7 %all-to-all-done = bf16[32,16,256]{2,1,0:T(8,128)(2,1)S(1)} async-done(((bf16[32,16,256]{2,1,0:T(8,128)(2,1)}), bf16[32,16,256]{2,1,0:T(8,128)(2,1)S(1)}, u32[]{:S(2)}, u32[]{:S(2)}) %all-to-all-start) | async-done | bytes 262176 | tf_op jit(solution)/shard_map/all_to_all | solution.py:78
  49.5 5.7 %collective-permute-done.6.refs_5_ = bf16[512,256]{1,0:T(8,128)(2,1)S(1)} collective-permute-done((bf16[512,256]{1,0:T(8,128)(2,1)S(1)}, bf16[512,256]{1,0:T(8,128)(2,1)S(1)}, u32[]{:S(2)}, u32[]{:S(2)}) %collective-permute-start.6) | collective-permute-done | bytes 262176 | tf_op jit(solution)/shard_map/ppermute | solution.py:61
  56.9 1.5 collective-permute-done.8.refs_7_
  58.4 2.4 %collective-permute-done.7.refs_6_ = bf16[512,256]{1,0:T(8,128)(2,1)S(1)} collective-permute-done((bf16[512,256]{1,0:T(8,128)(2,1)S(1)}, bf16[512,256]{1,0:T(8,128)(2,1)S(1)}, u32[]{:S(2)}, u32[]{:S(2)}) %collective-permute-start.7) | collective-permute-done | bytes 262176 | tf_op jit(solution)/shard_map/ppermute | solution.py:61
  60.8 4.9 %collective-permute-done.3.refs_1_ = bf16[4112,128]{1,0:T(8,128)(2,1)} collective-permute-done((bf16[4112,128]{1,0:T(8,128)(2,1)}, bf16[4112,128]{1,0:T(8,128)(2,1)}, u32[]{:S(2)}, u32[]{:S(2)}) %collective-permute-start.3) | collective-permute-done | bytes 1052704 | tf_op jit(solution)/shard_map/ppermute | solution.py:61
  65.7 4.1 %collective-permute-done.5.refs_3_ = bf16[4112,128]{1,0:T(8,128)(2,1)} collective-permute-done((bf16[4112,128]{1,0:T(8,128)(2,1)}, bf16[4112,128]{1,0:T(8,128)(2,1)}, u32[]{:S(2)}, u32[]{:S(2)}) %collective-permute-start.5) | collective-permute-done | bytes 1052704 | tf_op jit(solution)/shard_map/ppermute | solution.py:61
  73.1 3.7 %shard_map.108 = (f32[1024,128]{1,0:T(8,128)S(1)}, bf16[1024,128]{1,0:T(8,128)(2,1)S(1)}, bf16[1024,128]{1,0:T(8,128)(2,1)S(1)}, bf16[1024,128]{1,0:T(8,128)(2,1)S(1)}, bf16[4096,128]{1,0:T(8,128)(2,1)S(1)}) custom-call(s32[512]{0:T(512)S(1)} %maximum_convert_fusion.codes, bf16[4112,128]{1,0:T(8,128)(2,1)S(1)} %copy-done.2, ...), custom_call_target="tpu_custom_call" | custom-call | flops 6000000000 | bytes 1000000 | tf_op jit(solution)/shard_map/pallas_call | solution.py:361
  78.3 1.6 collective-permute-done.9.refs_8_
  81.1 3.6 %shard_map.109 = (f32[512,256]{1,0:T(8,128)S(1)}, bf16[512,256]{1,0:T(8,128)(2,1)S(1)}, bf16[512,256]{1,0:T(8,128)(2,1)S(1)}, f32[512,256]{1,0:T(8,128)S(1)}) custom-call(s32[512]{0:T(512)S(1)} %maximum_convert_fusion.codes, bf16[4112,128]{1,0:T(8,128)(2,1)S(1)} %copy-done.3, bf16[4112,128]{1,0:T(8,128)(2,1)} %collective-permute-done.3.refs_1_, ...), custom_call_target="tpu_custom_call" | custom-call | flops 6000000000 | bytes 1000000 | tf_op jit(solution)/shard_map/pallas_call | solution.py:312
  85.7 2.9 %collective-permute-start.15 = (bf16[512,256]{1,0:T(8,128)(2,1)S(1)}, bf16[512,256]{1,0:T(8,128)(2,1)S(1)}, u32[]{:S(2)}, u32[]{:S(2)}) collective-permute-start(bf16[512,256]{1,0:T(8,128)(2,1)S(1)} %get-tuple-element.107), channel_id=1, source_target_pairs={{0,2},{1,7},{2,4},{3,1},{4,6},{5,3},{6,0},{7,5},{8,10},{9,15},{10,... | collective-permute-start | bytes 786440 | tf_op jit(solution)/shard_map/ppermute | solution.py:61
  88.6 3.8 %collective-permute-start.17 = (bf16[1024,128]{1,0:T(8,128)(2,1)S(1)}, bf16[1024,128]{1,0:T(8,128)(2,1)S(1)}, u32[]{:S(2)}, u32[]{:S(2)}) collective-permute-start(bf16[1024,128]{1,0:T(8,128)(2,1)S(1)} %get-tuple-element.136), channel_id=1, source_target_pairs={{0,16},{1,17},{2,18},{3,19},{4,20},{5,21},{6,22},{7,23},{8,24},{9,... | collective-permute-start | bytes 786440 | tf_op jit(solution)/shard_map/ppermute | solution.py:61
  92.4 2.7 %collective-permute-start.19 = (bf16[1024,128]{1,0:T(8,128)(2,1)S(1)}, bf16[1024,128]{1,0:T(8,128)(2,1)S(1)}, u32[]{:S(2)}, u32[]{:S(2)}) collective-permute-start(bf16[1024,128]{1,0:T(8,128)(2,1)S(1)} %get-tuple-element.138), channel_id=1, source_target_pairs={{0,8},{1,25},{2,10},{3,27},{4,12},{5,29},{6,14},{7,31},{8,16},{9,1... | collective-permute-start | bytes 786440 | tf_op jit(solution)/shard_map/ppermute | solution.py:61
  95.1 2.6 %collective-permute-start.16 = (bf16[512,256]{1,0:T(8,128)(2,1)S(1)}, bf16[512,256]{1,0:T(8,128)(2,1)S(1)}, u32[]{:S(2)}, u32[]{:S(2)}) collective-permute-start(bf16[512,256]{1,0:T(8,128)(2,1)S(1)} %add_convert_fusion.2), channel_id=1, source_target_pairs={{0,2},{1,7},{2,4},{3,1},{4,6},{5,3},{6,0},{7,5},{8,10},{9,15},{10,... | collective-permute-start | bytes 786440 | tf_op jit(solution)/shard_map/ppermute | solution.py:61
  98.5 6.2 %collective-permute-done.18 = bf16[1024,128]{1,0:T(8,128)(2,1)S(1)} collective-permute-done((bf16[1024,128]{1,0:T(8,128)(2,1)S(1)}, bf16[1024,128]{1,0:T(8,128)(2,1)S(1)}, u32[]{:S(2)}, u32[]{:S(2)}) %collective-permute-start.18) | collective-permute-done | bytes 262176 | tf_op jit(solution)/shard_map/ppermute | solution.py:61
  105.5 2.1 %collective-permute-start.27 = (bf16[1024,128]{1,0:T(8,128)(2,1)S(1)}, bf16[1024,128]{1,0:T(8,128)(2,1)S(1)}, u32[]{:S(2)}, u32[]{:S(2)}) collective-permute-start(bf16[1024,128]{1,0:T(8,128)(2,1)S(1)} %fusion.1.refs_4_), channel_id=1, source_target_pairs={{0,2},{1,7},{2,4},{3,1},{4,6},{5,3},{6,0},{7,5},{8,10},{9,15},{10,... | collective-permute-start | bytes 786440 | tf_op jit(solution)/shard_map/ppermute | solution.py:61
  108.6 2.2 %collective-permute-done.20.refs_5_ = bf16[512,256]{1,0:T(8,128)(2,1)} collective-permute-done((bf16[512,256]{1,0:T(8,128)(2,1)S(1)}, bf16[512,256]{1,0:T(8,128)(2,1)}, u32[]{:S(2)}, u32[]{:S(2)}) %collective-permute-start.20) | collective-permute-done | bytes 262176 | tf_op jit(solution)/shard_map/ppermute | solution.py:61
  112.0 5.2 %collective-permute-done.27.refs_5_ = bf16[1024,128]{1,0:T(8,128)(2,1)S(1)} collective-permute-done((bf16[1024,128]{1,0:T(8,128)(2,1)S(1)}, bf16[1024,128]{1,0:T(8,128)(2,1)S(1)}, u32[]{:S(2)}, u32[]{:S(2)}) %collective-permute-start.27) | collective-permute-done | bytes 262176 | tf_op jit(solution)/shard_map/ppermute | solution.py:61
  117.4 4.6 %collective-permute-done.29.refs_7_ = bf16[1024,128]{1,0:T(8,128)(2,1)S(1)} collective-permute-done((bf16[1024,128]{1,0:T(8,128)(2,1)S(1)}, bf16[1024,128]{1,0:T(8,128)(2,1)S(1)}, u32[]{:S(2)}, u32[]{:S(2)}) %collective-permute-start.29) | collective-permute-done | bytes 262176 | tf_op jit(solution)/shard_map/ppermute | solution.py:61
  122.0 3.7 %shard_map.110 = (f32[1024,128]{1,0:T(8,128)S(1)}, bf16[1024,128]{1,0:T(8,128)(2,1)S(1)}, bf16[1024,128]{1,0:T(8,128)(2,1)S(1)}, bf16[1024,128]{1,0:T(8,128)(2,1)S(1)}, bf16[4096,128]{1,0:T(8,128)(2,1)S(1)}) custom-call(s32[512]{0:T(512)S(1)} %maximum_convert_fusion.codes, bf16[4112,128]{1,0:T(8,128)(2,1)S(1)} %copy-done.3, ...), custom_call_target="tpu_custom_call" | custom-call | flops 6000000000 | bytes 1000000 | tf_op jit(solution)/shard_map/pallas_call | solution.py:361
  129.4 1.5 fusion.45
  132.4 2.7 %collective-permute-start.36 = (bf16[1024,128]{1,0:T(8,128)(2,1)S(1)}, bf16[1024,128]{1,0:T(8,128)(2,1)S(1)}, u32[]{:S(2)}, u32[]{:S(2)}) collective-permute-start(bf16[1024,128]{1,0:T(8,128)(2,1)S(1)} %get-tuple-element.134), channel_id=1, source_target_pairs={{0,8},{1,25},{2,10},{3,27},{4,12},{5,29},{6,14},{7,31},{8,16},{9,1... | collective-permute-start | bytes 786440 | tf_op jit(solution)/shard_map/ppermute | solution.py:61
  135.0 3.9 %shard_map.111 = (f32[512,256]{1,0:T(8,128)S(1)}, bf16[512,256]{1,0:T(8,128)(2,1)S(1)}, bf16[512,256]{1,0:T(8,128)(2,1)S(1)}, f32[512,256]{1,0:T(8,128)S(1)}) custom-call(s32[512]{0:T(512)S(1)} %maximum_convert_fusion.codes, bf16[4112,128]{1,0:T(8,128)(2,1)S(1)} %copy-done.4, bf16[4112,128]{1,0:T(8,128)(2,1)} %collective-permute-done.3.refs_1_, ...), custom_call_target="tpu_custom_call" | custom-call | flops 6000000000 | bytes 1000000 | tf_op jit(solution)/shard_map/pallas_call | solution.py:312
  140.5 5.9 %collective-permute-done.35 = bf16[1024,128]{1,0:T(8,128)(2,1)S(1)} collective-permute-done((bf16[1024,128]{1,0:T(8,128)(2,1)S(1)}, bf16[1024,128]{1,0:T(8,128)(2,1)S(1)}, u32[]{:S(2)}, u32[]{:S(2)}) %collective-permute-start.35) | collective-permute-done | bytes 262176 | tf_op jit(solution)/shard_map/ppermute | solution.py:61
  148.0 7.4 %all-to-all-start.1 = ((bf16[128,4,256]{2,1,0:T(4,128)(2,1)}), bf16[128,4,256]{2,1,0:T(4,128)(2,1)S(1)}, u32[]{:S(2)}, u32[]{:S(2)}) async-start(bf16[128,4,256]{2,1,0:T(4,128)(2,1)} %reshape.58), calls=%async_computation.1 | async-start | bytes 524288 | tf_op jit(solution)/shard_map/all_to_all | solution.py:67
  156.3 2.6 %collective-permute-start.33 = (bf16[512,256]{1,0:T(8,128)(2,1)}, bf16[512,256]{1,0:T(8,128)(2,1)S(1)}, u32[]{:S(2)}, u32[]{:S(2)}) collective-permute-start(bf16[512,256]{1,0:T(8,128)(2,1)} %add_convert_fusion), channel_id=1, source_target_pairs={{0,2},{1,7},{2,4},{3,1},{4,6},{5,3},{6,0},{7,5},{8,10},{9,15},{10,... | collective-permute-start | bytes 786440 | tf_op jit(solution)/shard_map/ppermute | solution.py:61
  159.1 7.5 %all-to-all-done.1 = bf16[128,4,256]{2,1,0:T(4,128)(2,1)S(1)} async-done(((bf16[128,4,256]{2,1,0:T(4,128)(2,1)}), bf16[128,4,256]{2,1,0:T(4,128)(2,1)S(1)}, u32[]{:S(2)}, u32[]{:S(2)}) %all-to-all-start.1) | async-done | bytes 262176 | tf_op jit(solution)/shard_map/all_to_all | solution.py:67
  (94 shorter events, 33.6 us)
Async XLA Ops:
  4.2 16.5 %collective-permute-start = (bf16[1280,128]{1,0:T(8,128)(2,1)}, bf16[1280,128]{1,0:T(8,128)(2,1)S(1)}, u32[]{:S(2)}, u32[]{:S(2)}) collective-permute-start(bf16[1280,128]{1,0:T(8,128)(2,1)} %get-tuple-element.68), channel_id=1, source_target_pairs={{0,2},{1,7},{2,4},{3,1},{4,6},{5,3},{6,0},{7,5},{8,10},{9,15},{10,... | collective-permute-start | bytes 983048 | tf_op jit(solution)/shard_map/ppermute | solution.py:61
  7.8 16.2 %collective-permute-start.1 = (bf16[1280,128]{1,0:T(8,128)(2,1)}, bf16[1280,128]{1,0:T(8,128)(2,1)S(1)}, u32[]{:S(2)}, u32[]{:S(2)}) collective-permute-start(bf16[1280,128]{1,0:T(8,128)(2,1)} %get-tuple-element.69), channel_id=1, source_target_pairs={{0,4},{1,5},{2,6},{3,7},{4,0},{5,1},{6,2},{7,3},{8,12},{9,13},{10,... | collective-permute-start | bytes 983048 | tf_op jit(solution)/shard_map/ppermute | solution.py:61
  8.1 15.9 %collective-permute-start.2 = (bf16[1280,128]{1,0:T(8,128)(2,1)}, bf16[1280,128]{1,0:T(8,128)(2,1)S(1)}, u32[]{:S(2)}, u32[]{:S(2)}) collective-permute-start(bf16[1280,128]{1,0:T(8,128)(2,1)} %get-tuple-element.70), channel_id=1, source_target_pairs={{0,6},{1,3},{2,0},{3,5},{4,2},{5,7},{6,4},{7,1},{8,14},{9,11},{10,... | collective-permute-start | bytes 983048 | tf_op jit(solution)/shard_map/ppermute | solution.py:61
  20.7 45.0 %collective-permute-start.3 = (bf16[4112,128]{1,0:T(8,128)(2,1)}, bf16[4112,128]{1,0:T(8,128)(2,1)}, u32[]{:S(2)}, u32[]{:S(2)}) collective-permute-start(bf16[4112,128]{1,0:T(8,128)(2,1)} %get-tuple-element.74), channel_id=1, source_target_pairs={{0,2},{1,7},{2,4},{3,1},{4,6},{5,3},{6,0},{7,5},{8,10},{9,15},{10,... | collective-permute-start | bytes 3158024 | tf_op jit(solution)/shard_map/ppermute | solution.py:61
  24.0 41.6 %collective-permute-start.4 = (bf16[4112,128]{1,0:T(8,128)(2,1)}, bf16[4112,128]{1,0:T(8,128)(2,1)}, u32[]{:S(2)}, u32[]{:S(2)}) collective-permute-start(bf16[4112,128]{1,0:T(8,128)(2,1)} %get-tuple-element.76), channel_id=1, source_target_pairs={{0,4},{1,5},{2,6},{3,7},{4,0},{5,1},{6,2},{7,3},{8,12},{9,13},{10,... | collective-permute-start | bytes 3158024 | tf_op jit(solution)/shard_map/ppermute | solution.py:61
  25.8 44.0 %collective-permute-start.5 = (bf16[4112,128]{1,0:T(8,128)(2,1)}, bf16[4112,128]{1,0:T(8,128)(2,1)}, u32[]{:S(2)}, u32[]{:S(2)}) collective-permute-start(bf16[4112,128]{1,0:T(8,128)(2,1)} %get-tuple-element.78), channel_id=1, source_target_pairs={{0,6},{1,3},{2,0},{3,5},{4,2},{5,7},{6,4},{7,1},{8,14},{9,11},{10,... | collective-permute-start | bytes 3158024 | tf_op jit(solution)/shard_map/ppermute | solution.py:61
  27.6 19.6 %all-to-all-start = ((bf16[32,16,256]{2,1,0:T(8,128)(2,1)}), bf16[32,16,256]{2,1,0:T(8,128)(2,1)S(1)}, u32[]{:S(2)}, u32[]{:S(2)}) async-start(bf16[32,16,256]{2,1,0:T(8,128)(2,1)} %bitcast.7), calls=%async_computation | async-start | bytes 524288 | tf_op jit(solution)/shard_map/all_to_all | solution.py:78
  48.0 7.2 %collective-permute-start.6 = (bf16[512,256]{1,0:T(8,128)(2,1)S(1)}, bf16[512,256]{1,0:T(8,128)(2,1)S(1)}, u32[]{:S(2)}, u32[]{:S(2)}) collective-permute-start(bf16[512,256]{1,0:T(8,128)(2,1)S(1)} %shard_map.106.refs_4_), channel_id=1, source_target_pairs={{0,8},{1,25},{2,10},{3,27},{4,12},{5,29},{6,14},{7,31},{8,16},{9,1... | collective-permute-start | bytes 786440 | tf_op jit(solution)/shard_map/ppermute | solution.py:61
  49.2 9.2 %collective-permute-start.8 = (bf16[512,256]{1,0:T(8,128)(2,1)S(1)}, bf16[512,256]{1,0:T(8,128)(2,1)S(1)}, u32[]{:S(2)}, u32[]{:S(2)}) collective-permute-start(bf16[512,256]{1,0:T(8,128)(2,1)S(1)} %shard_map.106.refs_4_), channel_id=1, source_target_pairs={{0,24},{1,9},{2,26},{3,11},{4,28},{5,13},{6,30},{7,15},{8,0},{9,17... | collective-permute-start | bytes 786440 | tf_op jit(solution)/shard_map/ppermute | solution.py:61
  55.2 5.6 %collective-permute-start.7 = (bf16[512,256]{1,0:T(8,128)(2,1)S(1)}, bf16[512,256]{1,0:T(8,128)(2,1)S(1)}, u32[]{:S(2)}, u32[]{:S(2)}) collective-permute-start(bf16[512,256]{1,0:T(8,128)(2,1)S(1)} %collective-permute-done.6.refs_5_), channel_id=1, source_target_pairs={{0,8},{1,25},{2,10},{3,27},{4,12},{5,29},{6,14},{7,31},{8,16},{9,1... | collective-permute-start | bytes 786440 | tf_op jit(solution)/shard_map/ppermute | solution.py:61
  76.7 8.0 %collective-permute-start.13 = (bf16[4096,128]{1,0:T(8,128)(2,1)S(1)}, bf16[4096,128]{1,0:T(8,128)(2,1)S(1)}, u32[]{:S(2)}, u32[]{:S(2)}) collective-permute-start(bf16[4096,128]{1,0:T(8,128)(2,1)S(1)} %get-tuple-element.100), channel_id=1, source_target_pairs={{0,1},{1,0},{2,3},{3,2},{4,5},{5,4},{6,7},{7,6},{8,9},{9,8},{10,11... | collective-permute-start | bytes 3145736 | tf_op jit(solution)/shard_map/ppermute | solution.py:61
  85.0 10.1 %collective-permute-start.14 = (bf16[512,256]{1,0:T(8,128)(2,1)S(1)}, bf16[512,256]{1,0:T(8,128)(2,1)S(1)}, u32[]{:S(2)}, u32[]{:S(2)}) collective-permute-start(bf16[512,256]{1,0:T(8,128)(2,1)S(1)} %get-tuple-element.105), channel_id=1, source_target_pairs={{0,6},{1,3},{2,0},{3,5},{4,2},{5,7},{6,4},{7,1},{8,14},{9,11},{10,... | collective-permute-start | bytes 786440 | tf_op jit(solution)/shard_map/ppermute | solution.py:61
  85.7 9.4 %collective-permute-start.15 = (bf16[512,256]{1,0:T(8,128)(2,1)S(1)}, bf16[512,256]{1,0:T(8,128)(2,1)S(1)}, u32[]{:S(2)}, u32[]{:S(2)}) collective-permute-start(bf16[512,256]{1,0:T(8,128)(2,1)S(1)} %get-tuple-element.107), channel_id=1, source_target_pairs={{0,2},{1,7},{2,4},{3,1},{4,6},{5,3},{6,0},{7,5},{8,10},{9,15},{10,... | collective-permute-start | bytes 786440 | tf_op jit(solution)/shard_map/ppermute | solution.py:61
  88.6 9.9 %collective-permute-start.17 = (bf16[1024,128]{1,0:T(8,128)(2,1)S(1)}, bf16[1024,128]{1,0:T(8,128)(2,1)S(1)}, u32[]{:S(2)}, u32[]{:S(2)}) collective-permute-start(bf16[1024,128]{1,0:T(8,128)(2,1)S(1)} %get-tuple-element.136), channel_id=1, source_target_pairs={{0,16},{1,17},{2,18},{3,19},{4,20},{5,21},{6,22},{7,23},{8,24},{9,... | collective-permute-start | bytes 786440 | tf_op jit(solution)/shard_map/ppermute | solution.py:61
  92.4 12.4 %collective-permute-start.18 = (bf16[1024,128]{1,0:T(8,128)(2,1)S(1)}, bf16[1024,128]{1,0:T(8,128)(2,1)S(1)}, u32[]{:S(2)}, u32[]{:S(2)}) collective-permute-start(bf16[1024,128]{1,0:T(8,128)(2,1)S(1)} %get-tuple-element.137), channel_id=1, source_target_pairs={{0,24},{1,9},{2,26},{3,11},{4,28},{5,13},{6,30},{7,15},{8,0},{9,17... | collective-permute-start | bytes 786440 | tf_op jit(solution)/shard_map/ppermute | solution.py:61
  92.4 12.4 %collective-permute-start.19 = (bf16[1024,128]{1,0:T(8,128)(2,1)S(1)}, bf16[1024,128]{1,0:T(8,128)(2,1)S(1)}, u32[]{:S(2)}, u32[]{:S(2)}) collective-permute-start(bf16[1024,128]{1,0:T(8,128)(2,1)S(1)} %get-tuple-element.138), channel_id=1, source_target_pairs={{0,8},{1,25},{2,10},{3,27},{4,12},{5,29},{6,14},{7,31},{8,16},{9,1... | collective-permute-start | bytes 786440 | tf_op jit(solution)/shard_map/ppermute | solution.py:61
  95.1 9.8 %collective-permute-start.16 = (bf16[512,256]{1,0:T(8,128)(2,1)S(1)}, bf16[512,256]{1,0:T(8,128)(2,1)S(1)}, u32[]{:S(2)}, u32[]{:S(2)}) collective-permute-start(bf16[512,256]{1,0:T(8,128)(2,1)S(1)} %add_convert_fusion.2), channel_id=1, source_target_pairs={{0,2},{1,7},{2,4},{3,1},{4,6},{5,3},{6,0},{7,5},{8,10},{9,15},{10,... | collective-permute-start | bytes 786440 | tf_op jit(solution)/shard_map/ppermute | solution.py:61
  105.1 5.7 %collective-permute-start.20 = (bf16[512,256]{1,0:T(8,128)(2,1)S(1)}, bf16[512,256]{1,0:T(8,128)(2,1)}, u32[]{:S(2)}, u32[]{:S(2)}) collective-permute-start(bf16[512,256]{1,0:T(8,128)(2,1)S(1)} %add_convert_fusion.1.refs_4_), channel_id=1, source_target_pairs={{0,8},{1,25},{2,10},{3,27},{4,12},{5,29},{6,14},{7,31},{8,16},{9,1... | collective-permute-start | bytes 786440 | tf_op jit(solution)/shard_map/ppermute | solution.py:61
  105.5 11.7 %collective-permute-start.27 = (bf16[1024,128]{1,0:T(8,128)(2,1)S(1)}, bf16[1024,128]{1,0:T(8,128)(2,1)S(1)}, u32[]{:S(2)}, u32[]{:S(2)}) collective-permute-start(bf16[1024,128]{1,0:T(8,128)(2,1)S(1)} %fusion.1.refs_4_), channel_id=1, source_target_pairs={{0,2},{1,7},{2,4},{3,1},{4,6},{5,3},{6,0},{7,5},{8,10},{9,15},{10,... | collective-permute-start | bytes 786440 | tf_op jit(solution)/shard_map/ppermute | solution.py:61
  107.6 9.8 %collective-permute-start.28 = (bf16[1024,128]{1,0:T(8,128)(2,1)S(1)}, bf16[1024,128]{1,0:T(8,128)(2,1)S(1)}, u32[]{:S(2)}, u32[]{:S(2)}) collective-permute-start(bf16[1024,128]{1,0:T(8,128)(2,1)S(1)} %fusion.1.refs_4_), channel_id=1, source_target_pairs={{0,4},{1,5},{2,6},{3,7},{4,0},{5,1},{6,2},{7,3},{8,12},{9,13},{10,... | collective-permute-start | bytes 786440 | tf_op jit(solution)/shard_map/ppermute | solution.py:61
  107.6 14.4 %collective-permute-start.29 = (bf16[1024,128]{1,0:T(8,128)(2,1)S(1)}, bf16[1024,128]{1,0:T(8,128)(2,1)S(1)}, u32[]{:S(2)}, u32[]{:S(2)}) collective-permute-start(bf16[1024,128]{1,0:T(8,128)(2,1)S(1)} %fusion.1.refs_4_), channel_id=1, source_target_pairs={{0,6},{1,3},{2,0},{3,5},{4,2},{5,7},{6,4},{7,1},{8,14},{9,11},{10,... | collective-permute-start | bytes 786440 | tf_op jit(solution)/shard_map/ppermute | solution.py:61
  108.1 13.8 %collective-permute-start.22 = (bf16[512,256]{1,0:T(8,128)(2,1)S(1)}, bf16[512,256]{1,0:T(8,128)(2,1)}, u32[]{:S(2)}, u32[]{:S(2)}) collective-permute-start(bf16[512,256]{1,0:T(8,128)(2,1)S(1)} %add_convert_fusion.1.refs_4_), channel_id=1, source_target_pairs={{0,24},{1,9},{2,26},{3,11},{4,28},{5,13},{6,30},{7,15},{8,0},{9,17... | collective-permute-start | bytes 786440 | tf_op jit(solution)/shard_map/ppermute | solution.py:61
  110.8 11.2 %collective-permute-start.21 = (bf16[512,256]{1,0:T(8,128)(2,1)}, bf16[512,256]{1,0:T(8,128)(2,1)}, u32[]{:S(2)}, u32[]{:S(2)}) collective-permute-start(bf16[512,256]{1,0:T(8,128)(2,1)} %collective-permute-done.20.refs_5_), channel_id=1, source_target_pairs={{0,8},{1,25},{2,10},{3,27},{4,12},{5,29},{6,14},{7,31},{8,16},{9,1... | collective-permute-start | bytes 786440 | tf_op jit(solution)/shard_map/ppermute | solution.py:61
  127.1 3.8 %collective-permute-start.23 = (bf16[512,256]{1,0:T(8,128)(2,1)S(1)}, bf16[512,256]{1,0:T(8,128)(2,1)S(1)}, u32[]{:S(2)}, u32[]{:S(2)}) collective-permute-start(bf16[512,256]{1,0:T(8,128)(2,1)S(1)} %add_convert_fusion.1.refs_4_), channel_id=1, source_target_pairs={{0,1},{1,0},{2,3},{3,2},{4,5},{5,4},{6,7},{7,6},{8,9},{9,8},{10,11... | collective-permute-start | bytes 786440 | tf_op jit(solution)/shard_map/ppermute | solution.py:61
  127.2 3.7 %collective-permute-start.24 = (bf16[512,256]{1,0:T(8,128)(2,1)}, bf16[512,256]{1,0:T(8,128)(2,1)S(1)}, u32[]{:S(2)}, u32[]{:S(2)}) collective-permute-start(bf16[512,256]{1,0:T(8,128)(2,1)} %collective-permute-done.20.refs_5_), channel_id=1, source_target_pairs={{0,1},{1,0},{2,3},{3,2},{4,5},{5,4},{6,7},{7,6},{8,9},{9,8},{10,11... | collective-permute-start | bytes 786440 | tf_op jit(solution)/shard_map/ppermute | solution.py:61
  130.9 9.5 %collective-permute-start.34 = (bf16[1024,128]{1,0:T(8,128)(2,1)S(1)}, bf16[1024,128]{1,0:T(8,128)(2,1)S(1)}, u32[]{:S(2)}, u32[]{:S(2)}) collective-permute-start(bf16[1024,128]{1,0:T(8,128)(2,1)S(1)} %get-tuple-element.132), channel_id=1, source_target_pairs={{0,16},{1,17},{2,18},{3,19},{4,20},{5,21},{6,22},{7,23},{8,24},{9,... | collective-permute-start | bytes 786440 | tf_op jit(solution)/shard_map/ppermute | solution.py:61
  132.4 14.0 %collective-permute-start.35 = (bf16[1024,128]{1,0:T(8,128)(2,1)S(1)}, bf16[1024,128]{1,0:T(8,128)(2,1)S(1)}, u32[]{:S(2)}, u32[]{:S(2)}) collective-permute-start(bf16[1024,128]{1,0:T(8,128)(2,1)S(1)} %get-tuple-element.133), channel_id=1, source_target_pairs={{0,24},{1,9},{2,26},{3,11},{4,28},{5,13},{6,30},{7,15},{8,0},{9,17... | collective-permute-start | bytes 786440 | tf_op jit(solution)/shard_map/ppermute | solution.py:61
  132.4 14.0 %collective-permute-start.36 = (bf16[1024,128]{1,0:T(8,128)(2,1)S(1)}, bf16[1024,128]{1,0:T(8,128)(2,1)S(1)}, u32[]{:S(2)}, u32[]{:S(2)}) collective-permute-start(bf16[1024,128]{1,0:T(8,128)(2,1)S(1)} %get-tuple-element.134), channel_id=1, source_target_pairs={{0,8},{1,25},{2,10},{3,27},{4,12},{5,29},{6,14},{7,31},{8,16},{9,1... | collective-permute-start | bytes 786440 | tf_op jit(solution)/shard_map/ppermute | solution.py:61
  138.9 16.6 %collective-permute-start.32 = (bf16[512,256]{1,0:T(8,128)(2,1)S(1)}, bf16[512,256]{1,0:T(8,128)(2,1)S(1)}, u32[]{:S(2)}, u32[]{:S(2)}) collective-permute-start(bf16[512,256]{1,0:T(8,128)(2,1)S(1)} %get-tuple-element.130), channel_id=1, source_target_pairs={{0,2},{1,7},{2,4},{3,1},{4,6},{5,3},{6,0},{7,5},{8,10},{9,15},{10,... | collective-permute-start | bytes 786440 | tf_op jit(solution)/shard_map/ppermute | solution.py:61
  139.7 28.4 %collective-permute-start.31 = (bf16[512,256]{1,0:T(8,128)(2,1)S(1)}, bf16[512,256]{1,0:T(8,128)(2,1)S(1)}, u32[]{:S(2)}, u32[]{:S(2)}) collective-permute-start(bf16[512,256]{1,0:T(8,128)(2,1)S(1)} %get-tuple-element.128), channel_id=1, source_target_pairs={{0,6},{1,3},{2,0},{3,5},{4,2},{5,7},{6,4},{7,1},{8,14},{9,11},{10,... | collective-permute-start | bytes 786440 | tf_op jit(solution)/shard_map/ppermute | solution.py:61
  148.0 18.5 %all-to-all-start.1 = ((bf16[128,4,256]{2,1,0:T(4,128)(2,1)}), bf16[128,4,256]{2,1,0:T(4,128)(2,1)S(1)}, u32[]{:S(2)}, u32[]{:S(2)}) async-start(bf16[128,4,256]{2,1,0:T(4,128)(2,1)} %reshape.58), calls=%async_computation.1 | async-start | bytes 524288 | tf_op jit(solution)/shard_map/all_to_all | solution.py:67
  156.3 11.8 %collective-permute-start.33 = (bf16[512,256]{1,0:T(8,128)(2,1)}, bf16[512,256]{1,0:T(8,128)(2,1)S(1)}, u32[]{:S(2)}, u32[]{:S(2)}) collective-permute-start(bf16[512,256]{1,0:T(8,128)(2,1)} %add_convert_fusion), channel_id=1, source_target_pairs={{0,2},{1,7},{2,4},{3,1},{4,6},{5,3},{6,0},{7,5},{8,10},{9,15},{10,... | collective-permute-start | bytes 786440 | tf_op jit(solution)/shard_map/ppermute | solution.py:61
  (15 other events, 77.1 us)

commit v6 on v5

--- a/solution.py
+++ b/solution.py
@@ -103,12 +103,46 @@
     out[...] = total.astype(BF16)
 
 
-def restore_kernel(key_row, key_col, data, out):
+def restoring(key_row, key_col):
     below = (key_row[...] < key_col[...]).astype(jnp.int32)
     rank = jnp.sum(below, axis=1, keepdims=True)
     spot = lax.broadcasted_iota(jnp.int32, (NODES, NODES), 1)
-    select = (spot == rank).astype(F32).astype(BF16)
+    return (spot == rank).astype(F32).astype(BF16)
+
+
+def restore_kernel(key_row, key_col, data, out):
+    select = restoring(key_row, key_col)
     out[...] = jnp.dot(select, data[...], preferred_element_type=F32).astype(BF16)
+
+
+def select_kernel(key_row, key_col, out):
+    out[...] = restoring(key_row, key_col)
+
+
+def pick_kernel(select, data, out):
+    out[...] = jnp.dot(select[...], data[...], preferred_element_type=F32).astype(BF16)
+
+
+def selection(key):
+    return pl.pallas_call(
+        select_kernel,
+        out_shape=struct((NODES, NODES), BF16),
+        in_specs=[WHOLE] * 2,
+        out_specs=WHOLE,
+        compiler_params=params(),
+        cost_estimate=cost(NODES * NODES * 8, 2 * NODES * NODES),
+    )(key.reshape(1, NODES), key.reshape(NODES, 1))
+
+
+def pick(select, data):
+    return pl.pallas_call(
+        pick_kernel,
+        out_shape=struct((NODES, WIDTH), BF16),
+        in_specs=[WHOLE] * 2,
+        out_specs=WHOLE,
+        compiler_params=params(),
+        cost_estimate=cost(2 * NODES * NODES * WIDTH, 4 * NODES * WIDTH),
+    )(select, data)
 
 
 def ship_kernel(key_row, key_col, data, turned, *outs):
@@ -450,8 +484,7 @@
     shipped = ship(key * NODES + hash_target % NODES, embeddings, turned)
     packs = bucket(tile_values, after(target, shipped[0]), tile_row * COLUMNS + column)
     shipped = [shipped[0]] + [move(shipped[k], "y", k) for k in range(1, SIDE)]
-    moved = {d: move(after(packs[d], shipped[1]), "y", d) for d in (1, 3)}
-    moved[2] = move(after(packs[2], shipped), "y", 2)
+    moved = {d: move(after(packs[d], shipped[1]), "y", d) for d in ORDER}
 
     incoming = exchange_planes(regroup(shipped, devices))
     plane, line_y = by_plane(partition_source // NODES)
@@ -491,7 +524,7 @@
     layer_two, back_zero = both_products(features, after(gradients, line), False)
     grad_part = (turned.astype(F32) / 3.0 + back_zero).astype(BF16)
     returned = reshuffle(permute_call(order_turned_kernel, part_key, grad_part))
-    embed_grad = permute_call(restore_kernel, hash_target, returned)
+    embed_grad = pick(selection(hash_target), returned)
     propagated = ((initial.astype(F32) + layer_one.astype(F32) + layer_two) / 3.0).astype(BF16)
     return propagated, embed_grad
 

time: 169 us -> 170 us (level)
  Pallas kernels: 25.1 us -> 29.6 us
  starting transfers between devices: 60.8 us -> 58.8 us
    pallas_call x2, Pallas kernels: 7.51 us -> 9.78 us  [forward_product(): pl.pallas_call(forward_kernel, out_shape=[struct(shape, dtype) for dtype...]
    pallas_call x2, Pallas kernels: 7.35 us -> 9.62 us  [backward_product(): pl.pallas_call(backward_kernel, out_shape=[struct((TURNED, TILE), F32)] +...]
    all_to_all x1, starting transfers between devices: 7.44 us -> 5.39 us  [reshuffle(): lax.all_to_all(direct, ('row', 'col'), split_axis=0, concat_axis=0, tiled...]
  transfers between devices with their start and end apart: 39 -> 39, of which waited for: 20 -> 23; matrix products, arithmetic and copies ran while one was open for 3% -> 3% of each run, Pallas kernels for 10% -> 11%
where the time goes in v6:
time: 170 us; the launch traced here: 169 us
  waiting for transfers between devices  68.4 us (40%)
  starting transfers between devices  58.8 us (35%)
  Pallas kernels  29.6 us (17%)
  local copies, waits for them, and re-layouts  6.45 us (4%)
  other arithmetic  4.62 us (3%)
    ppermute x37, waiting for transfers between devices, move(): return lax.ppermute(array, 'col', pairs)  51.8 us
    ppermute x37, starting transfers between devices, move(): return lax.ppermute(array, 'col', pairs)  42.2 us
    all_to_all x1, starting transfers between devices, exchange_planes(): lax.all_to_all(direct, ('row', 'col'), split_axis=0, concat_axis=0, tiled...  11.1 us
    pallas_call x2, Pallas kernels, forward_product(): pl.pallas_call(forward_kernel, out_shape=[struct(shape, dtype) for dtype...  9.78 us
    pallas_call x2, Pallas kernels, backward_product(): pl.pallas_call(backward_kernel, out_shape=[struct((TURNED, TILE), F32)] +...  9.62 us
    all_to_all x1, waiting for transfers between devices, exchange_planes(): lax.all_to_all(direct, ('row', 'col'), split_axis=0, concat_axis=0, tiled...  8.75 us
    all_to_all x1, waiting for transfers between devices, reshuffle(): lax.all_to_all(direct, ('row', 'col'), split_axis=0, concat_axis=0, tiled...  7.78 us
    all_to_all x1, starting transfers between devices, reshuffle(): lax.all_to_all(direct, ('row', 'col'), split_axis=0, concat_axis=0, tiled...  5.39 us
  transfers between devices with their start and end apart: 39, of which 23 were waited for; matrix products, arithmetic and copies ran while one was open for 3% of the time, Pallas kernels for 11%

profile of v6, /device:TPU:1, one launch (start us, length us, event | category | flops | bytes accessed | tf_op | source)
XLA Modules:
  0.0 169.4 jit_solution(10869483755935055715)
XLA Ops:
  4.2 3.6 %collective-permute-start = (bf16[1280,128]{1,0:T(8,128)(2,1)}, bf16[1280,128]{1,0:T(8,128)(2,1)S(1)}, u32[]{:S(2)}, u32[]{:S(2)}) collective-permute-start(bf16[1280,128]{1,0:T(8,128)(2,1)} %get-tuple-element.68), channel_id=1, source_target_pairs={{0,2},{1,7},{2,4},{3,1},{4,6},{5,3},{6,0},{7,5},{8,10},{9,15},{10,... | collective-permute-start | bytes 983048 | tf_op jit(solution)/shard_map/ppermute | solution.py:61
  10.0 4.9 %shard_map.107 = (bf16[4112,128]{1,0:T(8,128)(2,1)}, bf16[4112,128]{1,0:T(8,128)(2,1)}, bf16[4112,128]{1,0:T(8,128)(2,1)}, bf16[4112,128]{1,0:T(8,128)(2,1)}) custom-call(s32[96]{0:T(128)} %get-tuple-element.71.target, s32[96]{0:T(128)} %get-tuple-element.142.code, bf16[96,128,128]{2,1,0:T(8,128)(2,1)} %source.1), custom_call_target="tpu_custom_call" | custom-call | flops 1000000 | bytes 7000000 | tf_op jit(solution)/shard_map/pallas_call | solution.py:246
  14.9 5.8 %collective-permute-done.refs_1_.refs_5_ = bf16[1280,128]{1,0:T(8,128)(2,1)S(1)} collective-permute-done((bf16[1280,128]{1,0:T(8,128)(2,1)}, bf16[1280,128]{1,0:T(8,128)(2,1)S(1)}, u32[]{:S(2)}, u32[]{:S(2)}) %collective-permute-start) | collective-permute-done | bytes 327712 | tf_op jit(solution)/shard_map/ppermute | solution.py:61
  20.7 3.3 %collective-permute-start.3 = (bf16[4112,128]{1,0:T(8,128)(2,1)}, bf16[4112,128]{1,0:T(8,128)(2,1)}, u32[]{:S(2)}, u32[]{:S(2)}) collective-permute-start(bf16[4112,128]{1,0:T(8,128)(2,1)} %get-tuple-element.74), channel_id=1, source_target_pairs={{0,2},{1,7},{2,4},{3,1},{4,6},{5,3},{6,0},{7,5},{8,10},{9,15},{10,... | collective-permute-start | bytes 3158024 | tf_op jit(solution)/shard_map/ppermute | solution.py:61
  25.7 11.1 %all-to-all-start = ((bf16[32,16,256]{2,1,0:T(8,128)(2,1)}), bf16[32,16,256]{2,1,0:T(8,128)(2,1)S(1)}, u32[]{:S(2)}, u32[]{:S(2)}) async-start(bf16[32,16,256]{2,1,0:T(8,128)(2,1)} %bitcast.7), calls=%async_computation | async-start | bytes 524288 | tf_op jit(solution)/shard_map/all_to_all | solution.py:78
  37.0 8.7 %all-to-all-done = bf16[32,16,256]{2,1,0:T(8,128)(2,1)S(1)} async-done(((bf16[32,16,256]{2,1,0:T(8,128)(2,1)}), bf16[32,16,256]{2,1,0:T(8,128)(2,1)S(1)}, u32[]{:S(2)}, u32[]{:S(2)}) %all-to-all-start) | async-done | bytes 262176 | tf_op jit(solution)/shard_map/all_to_all | solution.py:78
  48.0 5.7 %collective-permute-done.6.refs_5_ = bf16[512,256]{1,0:T(8,128)(2,1)S(1)} collective-permute-done((bf16[512,256]{1,0:T(8,128)(2,1)S(1)}, bf16[512,256]{1,0:T(8,128)(2,1)S(1)}, u32[]{:S(2)}, u32[]{:S(2)}) %collective-permute-start.6) | collective-permute-done | bytes 262176 | tf_op jit(solution)/shard_map/ppermute | solution.py:61
  56.9 2.4 %collective-permute-done.7.refs_6_ = bf16[512,256]{1,0:T(8,128)(2,1)S(1)} collective-permute-done((bf16[512,256]{1,0:T(8,128)(2,1)S(1)}, bf16[512,256]{1,0:T(8,128)(2,1)S(1)}, u32[]{:S(2)}, u32[]{:S(2)}) %collective-permute-start.7) | collective-permute-done | bytes 262176 | tf_op jit(solution)/shard_map/ppermute | solution.py:61
  59.3 8.2 %collective-permute-done.3.refs_1_ = bf16[4112,128]{1,0:T(8,128)(2,1)} collective-permute-done((bf16[4112,128]{1,0:T(8,128)(2,1)}, bf16[4112,128]{1,0:T(8,128)(2,1)}, u32[]{:S(2)}, u32[]{:S(2)}) %collective-permute-start.3) | collective-permute-done | bytes 1052704 | tf_op jit(solution)/shard_map/ppermute | solution.py:61
  67.5 2.3 %collective-permute-done.5.refs_3_ = bf16[4112,128]{1,0:T(8,128)(2,1)} collective-permute-done((bf16[4112,128]{1,0:T(8,128)(2,1)}, bf16[4112,128]{1,0:T(8,128)(2,1)}, u32[]{:S(2)}, u32[]{:S(2)}) %collective-permute-start.5) | collective-permute-done | bytes 1052704 | tf_op jit(solution)/shard_map/ppermute | solution.py:61
  73.0 4.8 %shard_map.108 = (f32[1024,128]{1,0:T(8,128)S(1)}, bf16[1024,128]{1,0:T(8,128)(2,1)S(1)}, bf16[1024,128]{1,0:T(8,128)(2,1)S(1)}, bf16[1024,128]{1,0:T(8,128)(2,1)S(1)}, bf16[4096,128]{1,0:T(8,128)(2,1)S(1)}) custom-call(s32[512]{0:T(512)S(1)} %maximum_convert_fusion.codes, bf16[4112,128]{1,0:T(8,128)(2,1)S(1)} %copy-done.2, ...), custom_call_target="tpu_custom_call" | custom-call | flops 6000000000 | bytes 1000000 | tf_op jit(solution)/shard_map/pallas_call | solution.py:395
  79.0 1.9 %collective-permute-done.9.refs_8_ = bf16[512,256]{1,0:T(8,128)(2,1)S(1)} collective-permute-done((bf16[512,256]{1,0:T(8,128)(2,1)S(1)}, bf16[512,256]{1,0:T(8,128)(2,1)S(1)}, u32[]{:S(2)}, u32[]{:S(2)}) %collective-permute-start.9) | collective-permute-done | bytes 262176 | tf_op jit(solution)/shard_map/ppermute | solution.py:61
  82.1 4.8 %shard_map.109 = (f32[512,256]{1,0:T(8,128)S(1)}, bf16[512,256]{1,0:T(8,128)(2,1)S(1)}, bf16[512,256]{1,0:T(8,128)(2,1)S(1)}, f32[512,256]{1,0:T(8,128)S(1)}) custom-call(s32[512]{0:T(512)S(1)} %maximum_convert_fusion.codes, bf16[4112,128]{1,0:T(8,128)(2,1)S(1)} %copy-done.3, bf16[4112,128]{1,0:T(8,128)(2,1)} %collective-permute-done.3.refs_1_, ...), custom_call_target="tpu_custom_call" | custom-call | flops 6000000000 | bytes 1000000 | tf_op jit(solution)/shard_map/pallas_call | solution.py:346
  87.1 2.0 %collective-permute-start.14 = (bf16[512,256]{1,0:T(8,128)(2,1)S(1)}, bf16[512,256]{1,0:T(8,128)(2,1)S(1)}, u32[]{:S(2)}, u32[]{:S(2)}) collective-permute-start(bf16[512,256]{1,0:T(8,128)(2,1)S(1)} %get-tuple-element.105), channel_id=1, source_target_pairs={{0,6},{1,3},{2,0},{3,5},{4,2},{5,7},{6,4},{7,1},{8,14},{9,11},{10,... | collective-permute-start | bytes 786440 | tf_op jit(solution)/shard_map/ppermute | solution.py:61
  89.1 1.5 collective-permute-start.15
  92.1 2.8 %collective-permute-start.18 = (bf16[1024,128]{1,0:T(8,128)(2,1)S(1)}, bf16[1024,128]{1,0:T(8,128)(2,1)S(1)}, u32[]{:S(2)}, u32[]{:S(2)}) collective-permute-start(bf16[1024,128]{1,0:T(8,128)(2,1)S(1)} %get-tuple-element.137), channel_id=1, source_target_pairs={{0,24},{1,9},{2,26},{3,11},{4,28},{5,13},{6,30},{7,15},{8,0},{9,17... | collective-permute-start | bytes 786440 | tf_op jit(solution)/shard_map/ppermute | solution.py:61
  95.6 3.6 %collective-permute-start.16 = (bf16[512,256]{1,0:T(8,128)(2,1)S(1)}, bf16[512,256]{1,0:T(8,128)(2,1)S(1)}, u32[]{:S(2)}, u32[]{:S(2)}) collective-permute-start(bf16[512,256]{1,0:T(8,128)(2,1)S(1)} %add_convert_fusion.2), channel_id=1, source_target_pairs={{0,2},{1,7},{2,4},{3,1},{4,6},{5,3},{6,0},{7,5},{8,10},{9,15},{10,... | collective-permute-start | bytes 786440 | tf_op jit(solution)/shard_map/ppermute | solution.py:61
  99.4 4.6 %collective-permute-done.18 = bf16[1024,128]{1,0:T(8,128)(2,1)S(1)} collective-permute-done((bf16[1024,128]{1,0:T(8,128)(2,1)S(1)}, bf16[1024,128]{1,0:T(8,128)(2,1)S(1)}, u32[]{:S(2)}, u32[]{:S(2)}) %collective-permute-start.18) | collective-permute-done | bytes 262176 | tf_op jit(solution)/shard_map/ppermute | solution.py:61
  104.0 2.2 %collective-permute-done.19 = bf16[1024,128]{1,0:T(8,128)(2,1)S(1)} collective-permute-done((bf16[1024,128]{1,0:T(8,128)(2,1)S(1)}, bf16[1024,128]{1,0:T(8,128)(2,1)S(1)}, u32[]{:S(2)}, u32[]{:S(2)}) %collective-permute-start.19) | collective-permute-done | bytes 262176 | tf_op jit(solution)/shard_map/ppermute | solution.py:61
  106.6 3.5 %collective-permute-start.20 = (bf16[512,256]{1,0:T(8,128)(2,1)S(1)}, bf16[512,256]{1,0:T(8,128)(2,1)}, u32[]{:S(2)}, u32[]{:S(2)}) collective-permute-start(bf16[512,256]{1,0:T(8,128)(2,1)S(1)} %add_convert_fusion.1.refs_4_), channel_id=1, source_target_pairs={{0,8},{1,25},{2,10},{3,27},{4,12},{5,29},{6,14},{7,31},{8,16},{9,1... | collective-permute-start | bytes 786440 | tf_op jit(solution)/shard_map/ppermute | solution.py:61
  113.4 3.4 %collective-permute-start.21 = (bf16[512,256]{1,0:T(8,128)(2,1)}, bf16[512,256]{1,0:T(8,128)(2,1)}, u32[]{:S(2)}, u32[]{:S(2)}) collective-permute-start(bf16[512,256]{1,0:T(8,128)(2,1)} %collective-permute-done.20.refs_5_), channel_id=1, source_target_pairs={{0,8},{1,25},{2,10},{3,27},{4,12},{5,29},{6,14},{7,31},{8,16},{9,1... | collective-permute-start | bytes 786440 | tf_op jit(solution)/shard_map/ppermute | solution.py:61
  116.8 2.4 %collective-permute-done.27.refs_5_ = bf16[1024,128]{1,0:T(8,128)(2,1)S(1)} collective-permute-done((bf16[1024,128]{1,0:T(8,128)(2,1)S(1)}, bf16[1024,128]{1,0:T(8,128)(2,1)S(1)}, u32[]{:S(2)}, u32[]{:S(2)}) %collective-permute-start.27) | collective-permute-done | bytes 262176 | tf_op jit(solution)/shard_map/ppermute | solution.py:61
  119.2 1.5 collective-permute-done.28.refs_6_
  120.7 3.4 %collective-permute-done.29.refs_7_ = bf16[1024,128]{1,0:T(8,128)(2,1)S(1)} collective-permute-done((bf16[1024,128]{1,0:T(8,128)(2,1)S(1)}, bf16[1024,128]{1,0:T(8,128)(2,1)S(1)}, u32[]{:S(2)}, u32[]{:S(2)}) %collective-permute-start.29) | collective-permute-done | bytes 262176 | tf_op jit(solution)/shard_map/ppermute | solution.py:61
  124.1 4.8 %shard_map.110 = (f32[1024,128]{1,0:T(8,128)S(1)}, bf16[1024,128]{1,0:T(8,128)(2,1)S(1)}, bf16[1024,128]{1,0:T(8,128)(2,1)S(1)}, bf16[1024,128]{1,0:T(8,128)(2,1)S(1)}, bf16[4096,128]{1,0:T(8,128)(2,1)S(1)}) custom-call(s32[512]{0:T(512)S(1)} %maximum_convert_fusion.codes, bf16[4112,128]{1,0:T(8,128)(2,1)S(1)} %copy-done.3, ...), custom_call_target="tpu_custom_call" | custom-call | flops 6000000000 | bytes 1000000 | tf_op jit(solution)/shard_map/pallas_call | solution.py:395
  131.8 1.5 fusion.45
  134.9 2.7 %collective-permute-start.35 = (bf16[1024,128]{1,0:T(8,128)(2,1)S(1)}, bf16[1024,128]{1,0:T(8,128)(2,1)S(1)}, u32[]{:S(2)}, u32[]{:S(2)}) collective-permute-start(bf16[1024,128]{1,0:T(8,128)(2,1)S(1)} %get-tuple-element.133), channel_id=1, source_target_pairs={{0,24},{1,9},{2,26},{3,11},{4,28},{5,13},{6,30},{7,15},{8,0},{9,17... | collective-permute-start | bytes 786440 | tf_op jit(solution)/shard_map/ppermute | solution.py:61
  137.6 5.0 %shard_map.111 = (f32[512,256]{1,0:T(8,128)S(1)}, bf16[512,256]{1,0:T(8,128)(2,1)S(1)}, bf16[512,256]{1,0:T(8,128)(2,1)S(1)}, f32[512,256]{1,0:T(8,128)S(1)}) custom-call(s32[512]{0:T(512)S(1)} %maximum_convert_fusion.codes, bf16[4112,128]{1,0:T(8,128)(2,1)S(1)} %copy-done.4, bf16[4112,128]{1,0:T(8,128)(2,1)} %collective-permute-done.3.refs_1_, ...), custom_call_target="tpu_custom_call" | custom-call | flops 6000000000 | bytes 1000000 | tf_op jit(solution)/shard_map/pallas_call | solution.py:346
  144.2 4.7 %collective-permute-done.35 = bf16[1024,128]{1,0:T(8,128)(2,1)S(1)} collective-permute-done((bf16[1024,128]{1,0:T(8,128)(2,1)S(1)}, bf16[1024,128]{1,0:T(8,128)(2,1)S(1)}, u32[]{:S(2)}, u32[]{:S(2)}) %collective-permute-start.35) | collective-permute-done | bytes 262176 | tf_op jit(solution)/shard_map/ppermute | solution.py:61
  151.0 5.4 %all-to-all-start.1 = ((bf16[128,4,256]{2,1,0:T(4,128)(2,1)}), bf16[128,4,256]{2,1,0:T(4,128)(2,1)S(1)}, u32[]{:S(2)}, u32[]{:S(2)}) async-start(bf16[128,4,256]{2,1,0:T(4,128)(2,1)} %reshape.58), calls=%async_computation.1 | async-start | bytes 524288 | tf_op jit(solution)/shard_map/all_to_all | solution.py:67
  156.5 2.7 %collective-permute-start.33 = (bf16[512,256]{1,0:T(8,128)(2,1)S(1)}, bf16[512,256]{1,0:T(8,128)(2,1)S(1)}, u32[]{:S(2)}, u32[]{:S(2)}) collective-permute-start(bf16[512,256]{1,0:T(8,128)(2,1)S(1)} %add_convert_fusion), channel_id=1, source_target_pairs={{0,2},{1,7},{2,4},{3,1},{4,6},{5,3},{6,0},{7,5},{8,10},{9,15},{10,... | collective-permute-start | bytes 786440 | tf_op jit(solution)/shard_map/ppermute | solution.py:61
  159.7 7.8 %all-to-all-done.1 = bf16[128,4,256]{2,1,0:T(4,128)(2,1)S(1)} async-done(((bf16[128,4,256]{2,1,0:T(4,128)(2,1)}), bf16[128,4,256]{2,1,0:T(4,128)(2,1)S(1)}, u32[]{:S(2)}, u32[]{:S(2)}) %all-to-all-start.1) | async-done | bytes 262176 | tf_op jit(solution)/shard_map/all_to_all | solution.py:67
  (95 shorter events, 34.7 us)
Async XLA Ops:
  4.2 16.5 %collective-permute-start = (bf16[1280,128]{1,0:T(8,128)(2,1)}, bf16[1280,128]{1,0:T(8,128)(2,1)S(1)}, u32[]{:S(2)}, u32[]{:S(2)}) collective-permute-start(bf16[1280,128]{1,0:T(8,128)(2,1)} %get-tuple-element.68), channel_id=1, source_target_pairs={{0,2},{1,7},{2,4},{3,1},{4,6},{5,3},{6,0},{7,5},{8,10},{9,15},{10,... | collective-permute-start | bytes 983048 | tf_op jit(solution)/shard_map/ppermute | solution.py:61
  7.8 16.8 %collective-permute-start.1 = (bf16[1280,128]{1,0:T(8,128)(2,1)}, bf16[1280,128]{1,0:T(8,128)(2,1)S(1)}, u32[]{:S(2)}, u32[]{:S(2)}) collective-permute-start(bf16[1280,128]{1,0:T(8,128)(2,1)} %get-tuple-element.69), channel_id=1, source_target_pairs={{0,4},{1,5},{2,6},{3,7},{4,0},{5,1},{6,2},{7,3},{8,12},{9,13},{10,... | collective-permute-start | bytes 983048 | tf_op jit(solution)/shard_map/ppermute | solution.py:61
  8.1 16.5 %collective-permute-start.2 = (bf16[1280,128]{1,0:T(8,128)(2,1)}, bf16[1280,128]{1,0:T(8,128)(2,1)S(1)}, u32[]{:S(2)}, u32[]{:S(2)}) collective-permute-start(bf16[1280,128]{1,0:T(8,128)(2,1)} %get-tuple-element.70), channel_id=1, source_target_pairs={{0,6},{1,3},{2,0},{3,5},{4,2},{5,7},{6,4},{7,1},{8,14},{9,11},{10,... | collective-permute-start | bytes 983048 | tf_op jit(solution)/shard_map/ppermute | solution.py:61
  20.7 46.8 %collective-permute-start.3 = (bf16[4112,128]{1,0:T(8,128)(2,1)}, bf16[4112,128]{1,0:T(8,128)(2,1)}, u32[]{:S(2)}, u32[]{:S(2)}) collective-permute-start(bf16[4112,128]{1,0:T(8,128)(2,1)} %get-tuple-element.74), channel_id=1, source_target_pairs={{0,2},{1,7},{2,4},{3,1},{4,6},{5,3},{6,0},{7,5},{8,10},{9,15},{10,... | collective-permute-start | bytes 3158024 | tf_op jit(solution)/shard_map/ppermute | solution.py:61
  24.0 43.5 %collective-permute-start.4 = (bf16[4112,128]{1,0:T(8,128)(2,1)}, bf16[4112,128]{1,0:T(8,128)(2,1)}, u32[]{:S(2)}, u32[]{:S(2)}) collective-permute-start(bf16[4112,128]{1,0:T(8,128)(2,1)} %get-tuple-element.76), channel_id=1, source_target_pairs={{0,4},{1,5},{2,6},{3,7},{4,0},{5,1},{6,2},{7,3},{8,12},{9,13},{10,... | collective-permute-start | bytes 3158024 | tf_op jit(solution)/shard_map/ppermute | solution.py:61
  24.0 45.8 %collective-permute-start.5 = (bf16[4112,128]{1,0:T(8,128)(2,1)}, bf16[4112,128]{1,0:T(8,128)(2,1)}, u32[]{:S(2)}, u32[]{:S(2)}) collective-permute-start(bf16[4112,128]{1,0:T(8,128)(2,1)} %get-tuple-element.78), channel_id=1, source_target_pairs={{0,6},{1,3},{2,0},{3,5},{4,2},{5,7},{6,4},{7,1},{8,14},{9,11},{10,... | collective-permute-start | bytes 3158024 | tf_op jit(solution)/shard_map/ppermute | solution.py:61
  25.7 20.1 %all-to-all-start = ((bf16[32,16,256]{2,1,0:T(8,128)(2,1)}), bf16[32,16,256]{2,1,0:T(8,128)(2,1)S(1)}, u32[]{:S(2)}, u32[]{:S(2)}) async-start(bf16[32,16,256]{2,1,0:T(8,128)(2,1)} %bitcast.7), calls=%async_computation | async-start | bytes 524288 | tf_op jit(solution)/shard_map/all_to_all | solution.py:78
  46.5 7.2 %collective-permute-start.6 = (bf16[512,256]{1,0:T(8,128)(2,1)S(1)}, bf16[512,256]{1,0:T(8,128)(2,1)S(1)}, u32[]{:S(2)}, u32[]{:S(2)}) collective-permute-start(bf16[512,256]{1,0:T(8,128)(2,1)S(1)} %shard_map.106.refs_4_), channel_id=1, source_target_pairs={{0,8},{1,25},{2,10},{3,27},{4,12},{5,29},{6,14},{7,31},{8,16},{9,1... | collective-permute-start | bytes 786440 | tf_op jit(solution)/shard_map/ppermute | solution.py:61
  47.7 9.2 %collective-permute-start.8 = (bf16[512,256]{1,0:T(8,128)(2,1)S(1)}, bf16[512,256]{1,0:T(8,128)(2,1)S(1)}, u32[]{:S(2)}, u32[]{:S(2)}) collective-permute-start(bf16[512,256]{1,0:T(8,128)(2,1)S(1)} %shard_map.106.refs_4_), channel_id=1, source_target_pairs={{0,24},{1,9},{2,26},{3,11},{4,28},{5,13},{6,30},{7,15},{8,0},{9,17... | collective-permute-start | bytes 786440 | tf_op jit(solution)/shard_map/ppermute | solution.py:61
  53.7 5.6 %collective-permute-start.7 = (bf16[512,256]{1,0:T(8,128)(2,1)S(1)}, bf16[512,256]{1,0:T(8,128)(2,1)S(1)}, u32[]{:S(2)}, u32[]{:S(2)}) collective-permute-start(bf16[512,256]{1,0:T(8,128)(2,1)S(1)} %collective-permute-done.6.refs_5_), channel_id=1, source_target_pairs={{0,8},{1,25},{2,10},{3,27},{4,12},{5,29},{6,14},{7,31},{8,16},{9,1... | collective-permute-start | bytes 786440 | tf_op jit(solution)/shard_map/ppermute | solution.py:61
  77.8 9.0 %collective-permute-start.13 = (bf16[4096,128]{1,0:T(8,128)(2,1)S(1)}, bf16[4096,128]{1,0:T(8,128)(2,1)S(1)}, u32[]{:S(2)}, u32[]{:S(2)}) collective-permute-start(bf16[4096,128]{1,0:T(8,128)(2,1)S(1)} %get-tuple-element.100), channel_id=1, source_target_pairs={{0,1},{1,0},{2,3},{3,2},{4,5},{5,4},{6,7},{7,6},{8,9},{9,8},{10,11... | collective-permute-start | bytes 3145736 | tf_op jit(solution)/shard_map/ppermute | solution.py:61
  87.1 8.4 %collective-permute-start.14 = (bf16[512,256]{1,0:T(8,128)(2,1)S(1)}, bf16[512,256]{1,0:T(8,128)(2,1)S(1)}, u32[]{:S(2)}, u32[]{:S(2)}) collective-permute-start(bf16[512,256]{1,0:T(8,128)(2,1)S(1)} %get-tuple-element.105), channel_id=1, source_target_pairs={{0,6},{1,3},{2,0},{3,5},{4,2},{5,7},{6,4},{7,1},{8,14},{9,11},{10,... | collective-permute-start | bytes 786440 | tf_op jit(solution)/shard_map/ppermute | solution.py:61
  89.1 6.4 %collective-permute-start.15 = (bf16[512,256]{1,0:T(8,128)(2,1)S(1)}, bf16[512,256]{1,0:T(8,128)(2,1)S(1)}, u32[]{:S(2)}, u32[]{:S(2)}) collective-permute-start(bf16[512,256]{1,0:T(8,128)(2,1)S(1)} %get-tuple-element.107), channel_id=1, source_target_pairs={{0,2},{1,7},{2,4},{3,1},{4,6},{5,3},{6,0},{7,5},{8,10},{9,15},{10,... | collective-permute-start | bytes 786440 | tf_op jit(solution)/shard_map/ppermute | solution.py:61
  90.6 8.8 %collective-permute-start.17 = (bf16[1024,128]{1,0:T(8,128)(2,1)S(1)}, bf16[1024,128]{1,0:T(8,128)(2,1)S(1)}, u32[]{:S(2)}, u32[]{:S(2)}) collective-permute-start(bf16[1024,128]{1,0:T(8,128)(2,1)S(1)} %get-tuple-element.136), channel_id=1, source_target_pairs={{0,16},{1,17},{2,18},{3,19},{4,20},{5,21},{6,22},{7,23},{8,24},{9,... | collective-permute-start | bytes 786440 | tf_op jit(solution)/shard_map/ppermute | solution.py:61
  92.1 11.9 %collective-permute-start.18 = (bf16[1024,128]{1,0:T(8,128)(2,1)S(1)}, bf16[1024,128]{1,0:T(8,128)(2,1)S(1)}, u32[]{:S(2)}, u32[]{:S(2)}) collective-permute-start(bf16[1024,128]{1,0:T(8,128)(2,1)S(1)} %get-tuple-element.137), channel_id=1, source_target_pairs={{0,24},{1,9},{2,26},{3,11},{4,28},{5,13},{6,30},{7,15},{8,0},{9,17... | collective-permute-start | bytes 786440 | tf_op jit(solution)/shard_map/ppermute | solution.py:61
  94.9 11.4 %collective-permute-start.19 = (bf16[1024,128]{1,0:T(8,128)(2,1)S(1)}, bf16[1024,128]{1,0:T(8,128)(2,1)S(1)}, u32[]{:S(2)}, u32[]{:S(2)}) collective-permute-start(bf16[1024,128]{1,0:T(8,128)(2,1)S(1)} %get-tuple-element.138), channel_id=1, source_target_pairs={{0,8},{1,25},{2,10},{3,27},{4,12},{5,29},{6,14},{7,31},{8,16},{9,1... | collective-permute-start | bytes 786440 | tf_op jit(solution)/shard_map/ppermute | solution.py:61
  95.6 10.8 %collective-permute-start.16 = (bf16[512,256]{1,0:T(8,128)(2,1)S(1)}, bf16[512,256]{1,0:T(8,128)(2,1)S(1)}, u32[]{:S(2)}, u32[]{:S(2)}) collective-permute-start(bf16[512,256]{1,0:T(8,128)(2,1)S(1)} %add_convert_fusion.2), channel_id=1, source_target_pairs={{0,2},{1,7},{2,4},{3,1},{4,6},{5,3},{6,0},{7,5},{8,10},{9,15},{10,... | collective-permute-start | bytes 786440 | tf_op jit(solution)/shard_map/ppermute | solution.py:61
  106.6 6.8 %collective-permute-start.20 = (bf16[512,256]{1,0:T(8,128)(2,1)S(1)}, bf16[512,256]{1,0:T(8,128)(2,1)}, u32[]{:S(2)}, u32[]{:S(2)}) collective-permute-start(bf16[512,256]{1,0:T(8,128)(2,1)S(1)} %add_convert_fusion.1.refs_4_), channel_id=1, source_target_pairs={{0,8},{1,25},{2,10},{3,27},{4,12},{5,29},{6,14},{7,31},{8,16},{9,1... | collective-permute-start | bytes 786440 | tf_op jit(solution)/shard_map/ppermute | solution.py:61
  110.0 9.1 %collective-permute-start.27 = (bf16[1024,128]{1,0:T(8,128)(2,1)S(1)}, bf16[1024,128]{1,0:T(8,128)(2,1)S(1)}, u32[]{:S(2)}, u32[]{:S(2)}) collective-permute-start(bf16[1024,128]{1,0:T(8,128)(2,1)S(1)} %fusion.1.refs_4_), channel_id=1, source_target_pairs={{0,2},{1,7},{2,4},{3,1},{4,6},{5,3},{6,0},{7,5},{8,10},{9,15},{10,... | collective-permute-start | bytes 786440 | tf_op jit(solution)/shard_map/ppermute | solution.py:61
  110.8 9.9 %collective-permute-start.28 = (bf16[1024,128]{1,0:T(8,128)(2,1)S(1)}, bf16[1024,128]{1,0:T(8,128)(2,1)S(1)}, u32[]{:S(2)}, u32[]{:S(2)}) collective-permute-start(bf16[1024,128]{1,0:T(8,128)(2,1)S(1)} %fusion.1.refs_4_), channel_id=1, source_target_pairs={{0,4},{1,5},{2,6},{3,7},{4,0},{5,1},{6,2},{7,3},{8,12},{9,13},{10,... | collective-permute-start | bytes 786440 | tf_op jit(solution)/shard_map/ppermute | solution.py:61
  111.1 13.0 %collective-permute-start.29 = (bf16[1024,128]{1,0:T(8,128)(2,1)S(1)}, bf16[1024,128]{1,0:T(8,128)(2,1)S(1)}, u32[]{:S(2)}, u32[]{:S(2)}) collective-permute-start(bf16[1024,128]{1,0:T(8,128)(2,1)S(1)} %fusion.1.refs_4_), channel_id=1, source_target_pairs={{0,6},{1,3},{2,0},{3,5},{4,2},{5,7},{6,4},{7,1},{8,14},{9,11},{10,... | collective-permute-start | bytes 786440 | tf_op jit(solution)/shard_map/ppermute | solution.py:61
  112.0 12.1 %collective-permute-start.22 = (bf16[512,256]{1,0:T(8,128)(2,1)S(1)}, bf16[512,256]{1,0:T(8,128)(2,1)}, u32[]{:S(2)}, u32[]{:S(2)}) collective-permute-start(bf16[512,256]{1,0:T(8,128)(2,1)S(1)} %add_convert_fusion.1.refs_4_), channel_id=1, source_target_pairs={{0,24},{1,9},{2,26},{3,11},{4,28},{5,13},{6,30},{7,15},{8,0},{9,17... | collective-permute-start | bytes 786440 | tf_op jit(solution)/shard_map/ppermute | solution.py:61
  113.4 10.8 %collective-permute-start.21 = (bf16[512,256]{1,0:T(8,128)(2,1)}, bf16[512,256]{1,0:T(8,128)(2,1)}, u32[]{:S(2)}, u32[]{:S(2)}) collective-permute-start(bf16[512,256]{1,0:T(8,128)(2,1)} %collective-permute-done.20.refs_5_), channel_id=1, source_target_pairs={{0,8},{1,25},{2,10},{3,27},{4,12},{5,29},{6,14},{7,31},{8,16},{9,1... | collective-permute-start | bytes 786440 | tf_op jit(solution)/shard_map/ppermute | solution.py:61
  129.2 4.2 %collective-permute-start.23 = (bf16[512,256]{1,0:T(8,128)(2,1)S(1)}, bf16[512,256]{1,0:T(8,128)(2,1)S(1)}, u32[]{:S(2)}, u32[]{:S(2)}) collective-permute-start(bf16[512,256]{1,0:T(8,128)(2,1)S(1)} %add_convert_fusion.1.refs_4_), channel_id=1, source_target_pairs={{0,1},{1,0},{2,3},{3,2},{4,5},{5,4},{6,7},{7,6},{8,9},{9,8},{10,11... | collective-permute-start | bytes 786440 | tf_op jit(solution)/shard_map/ppermute | solution.py:61
  129.8 3.6 %collective-permute-start.24 = (bf16[512,256]{1,0:T(8,128)(2,1)}, bf16[512,256]{1,0:T(8,128)(2,1)S(1)}, u32[]{:S(2)}, u32[]{:S(2)}) collective-permute-start(bf16[512,256]{1,0:T(8,128)(2,1)} %collective-permute-done.20.refs_5_), channel_id=1, source_target_pairs={{0,1},{1,0},{2,3},{3,2},{4,5},{5,4},{6,7},{7,6},{8,9},{9,8},{10,11... | collective-permute-start | bytes 786440 | tf_op jit(solution)/shard_map/ppermute | solution.py:61
  133.4 10.7 %collective-permute-start.34 = (bf16[1024,128]{1,0:T(8,128)(2,1)S(1)}, bf16[1024,128]{1,0:T(8,128)(2,1)S(1)}, u32[]{:S(2)}, u32[]{:S(2)}) collective-permute-start(bf16[1024,128]{1,0:T(8,128)(2,1)S(1)} %get-tuple-element.132), channel_id=1, source_target_pairs={{0,16},{1,17},{2,18},{3,19},{4,20},{5,21},{6,22},{7,23},{8,24},{9,... | collective-permute-start | bytes 786440 | tf_op jit(solution)/shard_map/ppermute | solution.py:61
  134.9 14.0 %collective-permute-start.35 = (bf16[1024,128]{1,0:T(8,128)(2,1)S(1)}, bf16[1024,128]{1,0:T(8,128)(2,1)S(1)}, u32[]{:S(2)}, u32[]{:S(2)}) collective-permute-start(bf16[1024,128]{1,0:T(8,128)(2,1)S(1)} %get-tuple-element.133), channel_id=1, source_target_pairs={{0,24},{1,9},{2,26},{3,11},{4,28},{5,13},{6,30},{7,15},{8,0},{9,17... | collective-permute-start | bytes 786440 | tf_op jit(solution)/shard_map/ppermute | solution.py:61
  137.6 11.7 %collective-permute-start.36 = (bf16[1024,128]{1,0:T(8,128)(2,1)S(1)}, bf16[1024,128]{1,0:T(8,128)(2,1)S(1)}, u32[]{:S(2)}, u32[]{:S(2)}) collective-permute-start(bf16[1024,128]{1,0:T(8,128)(2,1)S(1)} %get-tuple-element.134), channel_id=1, source_target_pairs={{0,8},{1,25},{2,10},{3,27},{4,12},{5,29},{6,14},{7,31},{8,16},{9,1... | collective-permute-start | bytes 786440 | tf_op jit(solution)/shard_map/ppermute | solution.py:61
  142.6 13.8 %collective-permute-start.32 = (bf16[512,256]{1,0:T(8,128)(2,1)S(1)}, bf16[512,256]{1,0:T(8,128)(2,1)S(1)}, u32[]{:S(2)}, u32[]{:S(2)}) collective-permute-start(bf16[512,256]{1,0:T(8,128)(2,1)S(1)} %get-tuple-element.130), channel_id=1, source_target_pairs={{0,2},{1,7},{2,4},{3,1},{4,6},{5,3},{6,0},{7,5},{8,10},{9,15},{10,... | collective-permute-start | bytes 786440 | tf_op jit(solution)/shard_map/ppermute | solution.py:61
  143.5 25.0 %collective-permute-start.31 = (bf16[512,256]{1,0:T(8,128)(2,1)S(1)}, bf16[512,256]{1,0:T(8,128)(2,1)S(1)}, u32[]{:S(2)}, u32[]{:S(2)}) collective-permute-start(bf16[512,256]{1,0:T(8,128)(2,1)S(1)} %get-tuple-element.128), channel_id=1, source_target_pairs={{0,6},{1,3},{2,0},{3,5},{4,2},{5,7},{6,4},{7,1},{8,14},{9,11},{10,... | collective-permute-start | bytes 786440 | tf_op jit(solution)/shard_map/ppermute | solution.py:61
  151.0 16.5 %all-to-all-start.1 = ((bf16[128,4,256]{2,1,0:T(4,128)(2,1)}), bf16[128,4,256]{2,1,0:T(4,128)(2,1)S(1)}, u32[]{:S(2)}, u32[]{:S(2)}) async-start(bf16[128,4,256]{2,1,0:T(4,128)(2,1)} %reshape.58), calls=%async_computation.1 | async-start | bytes 524288 | tf_op jit(solution)/shard_map/all_to_all | solution.py:67
  156.5 12.1 %collective-permute-start.33 = (bf16[512,256]{1,0:T(8,128)(2,1)S(1)}, bf16[512,256]{1,0:T(8,128)(2,1)S(1)}, u32[]{:S(2)}, u32[]{:S(2)}) collective-permute-start(bf16[512,256]{1,0:T(8,128)(2,1)S(1)} %add_convert_fusion), channel_id=1, source_target_pairs={{0,2},{1,7},{2,4},{3,1},{4,6},{5,3},{6,0},{7,5},{8,10},{9,15},{10,... | collective-permute-start | bytes 786440 | tf_op jit(solution)/shard_map/ppermute | solution.py:61
  (15 other events, 75.4 us)

commit v7 on v5

--- a/solution.py
+++ b/solution.py
@@ -18,7 +18,7 @@
 CAP = SIDE * CORES * OWNER_CAP
 CODE_ROWS = 16
 COUNT_LANE = 64
-UNROLL = 16
+UNROLL = 32
 CHUNK = 8
 PACKED = CAP * TILE + CODE_ROWS
 COLUMNS = CORES * SIDE * BLOCKS

time: 169 us -> 170 us (level)
  Pallas kernels: 25.1 us -> 22.1 us
  starting transfers between devices: 60.8 us -> 63.6 us
    ppermute x37, starting transfers between devices: 42.6 us -> 45.1 us  [move(): return lax.ppermute(array, 'col', pairs)]
  transfers between devices with their start and end apart: 39 -> 39, of which waited for: 20 -> 19; matrix products, arithmetic and copies ran while one was open for 3% -> 3% of each run, Pallas kernels for 10% -> 9%
where the time goes in v7:
time: 170 us
  waiting for transfers between devices  70.9 us (42%)
  starting transfers between devices  63.6 us (37%)
  Pallas kernels  22.1 us (13%)
  local copies, waits for them, and re-layouts  6.45 us (4%)
  other arithmetic  5.31 us (3%)
    ppermute x37, waiting for transfers between devices, move(): return lax.ppermute(array, 'col', pairs)  54.6 us
    ppermute x37, starting transfers between devices, move(): return lax.ppermute(array, 'col', pairs)  45.1 us
    all_to_all x1, starting transfers between devices, exchange_planes(): lax.all_to_all(direct, ('row', 'col'), split_axis=0, concat_axis=0, tiled...  10.7 us
    all_to_all x1, waiting for transfers between devices, exchange_planes(): lax.all_to_all(direct, ('row', 'col'), split_axis=0, concat_axis=0, tiled...  8.75 us
    all_to_all x1, starting transfers between devices, reshuffle(): lax.all_to_all(direct, ('row', 'col'), split_axis=0, concat_axis=0, tiled...  7.7 us
    all_to_all x1, waiting for transfers between devices, reshuffle(): lax.all_to_all(direct, ('row', 'col'), split_axis=0, concat_axis=0, tiled...  7.51 us
    pallas_call x2, Pallas kernels, forward_product(): pl.pallas_call(forward_kernel, out_shape=[struct(shape, dtype) for dtype...  6 us
    pallas_call x2, Pallas kernels, backward_product(): pl.pallas_call(backward_kernel, out_shape=[struct((TURNED, TILE), F32)] +...  5.85 us
  transfers between devices with their start and end apart: 39, of which 19 were waited for; matrix products, arithmetic and copies ran while one was open for 3% of the time, Pallas kernels for 9%

profile of v7, /device:TPU:1, one launch (start us, length us, event | category | flops | bytes accessed | tf_op | source)
XLA Modules:
  0.0 169.9 jit_solution(4955845200356408752)
XLA Ops:
  4.2 3.6 %collective-permute-start = (bf16[1280,128]{1,0:T(8,128)(2,1)}, bf16[1280,128]{1,0:T(8,128)(2,1)S(1)}, u32[]{:S(2)}, u32[]{:S(2)}) collective-permute-start(bf16[1280,128]{1,0:T(8,128)(2,1)} %get-tuple-element.68), channel_id=1, source_target_pairs={{0,2},{1,7},{2,4},{3,1},{4,6},{5,3},{6,0},{7,5},{8,10},{9,15},{10,... | collective-permute-start | bytes 983048 | tf_op jit(solution)/shard_map/ppermute | solution.py:61
  10.1 4.8 %shard_map.107 = (bf16[4112,128]{1,0:T(8,128)(2,1)}, bf16[4112,128]{1,0:T(8,128)(2,1)}, bf16[4112,128]{1,0:T(8,128)(2,1)}, bf16[4112,128]{1,0:T(8,128)(2,1)}) custom-call(s32[96]{0:T(128)} %get-tuple-element.71.target, s32[96]{0:T(128)} %get-tuple-element.142.code, bf16[96,128,128]{2,1,0:T(8,128)(2,1)} %source.1), custom_call_target="tpu_custom_call" | custom-call | flops 1000000 | bytes 7000000 | tf_op jit(solution)/shard_map/pallas_call | solution.py:212
  14.9 5.8 %collective-permute-done.refs_1_.refs_5_ = bf16[1280,128]{1,0:T(8,128)(2,1)S(1)} collective-permute-done((bf16[1280,128]{1,0:T(8,128)(2,1)}, bf16[1280,128]{1,0:T(8,128)(2,1)S(1)}, u32[]{:S(2)}, u32[]{:S(2)}) %collective-permute-start) | collective-permute-done | bytes 327712 | tf_op jit(solution)/shard_map/ppermute | solution.py:61
  20.7 3.3 %collective-permute-start.3 = (bf16[4112,128]{1,0:T(8,128)(2,1)}, bf16[4112,128]{1,0:T(8,128)(2,1)}, u32[]{:S(2)}, u32[]{:S(2)}) collective-permute-start(bf16[4112,128]{1,0:T(8,128)(2,1)} %get-tuple-element.74), channel_id=1, source_target_pairs={{0,2},{1,7},{2,4},{3,1},{4,6},{5,3},{6,0},{7,5},{8,10},{9,15},{10,... | collective-permute-start | bytes 3158024 | tf_op jit(solution)/shard_map/ppermute | solution.py:61
  24.0 1.8 %collective-permute-start.4 = (bf16[4112,128]{1,0:T(8,128)(2,1)}, bf16[4112,128]{1,0:T(8,128)(2,1)}, u32[]{:S(2)}, u32[]{:S(2)}) collective-permute-start(bf16[4112,128]{1,0:T(8,128)(2,1)} %get-tuple-element.76), channel_id=1, source_target_pairs={{0,4},{1,5},{2,6},{3,7},{4,0},{5,1},{6,2},{7,3},{8,12},{9,13},{10,... | collective-permute-start | bytes 3158024 | tf_op jit(solution)/shard_map/ppermute | solution.py:61
  27.6 10.7 %all-to-all-start = ((bf16[32,16,256]{2,1,0:T(8,128)(2,1)}), bf16[32,16,256]{2,1,0:T(8,128)(2,1)S(1)}, u32[]{:S(2)}, u32[]{:S(2)}) async-start(bf16[32,16,256]{2,1,0:T(8,128)(2,1)} %bitcast.7), calls=%async_computation | async-start | bytes 524288 | tf_op jit(solution)/shard_map/all_to_all | solution.py:78
  38.5 8.7 %all-to-all-done = bf16[32,16,256]{2,1,0:T(8,128)(2,1)S(1)} async-done(((bf16[32,16,256]{2,1,0:T(8,128)(2,1)}), bf16[32,16,256]{2,1,0:T(8,128)(2,1)S(1)}, u32[]{:S(2)}, u32[]{:S(2)}) %all-to-all-start) | async-done | bytes 262176 | tf_op jit(solution)/shard_map/all_to_all | solution.py:78
  49.5 5.7 %collective-permute-done.6.refs_5_ = bf16[512,256]{1,0:T(8,128)(2,1)S(1)} collective-permute-done((bf16[512,256]{1,0:T(8,128)(2,1)S(1)}, bf16[512,256]{1,0:T(8,128)(2,1)S(1)}, u32[]{:S(2)}, u32[]{:S(2)}) %collective-permute-start.6) | collective-permute-done | bytes 262176 | tf_op jit(solution)/shard_map/ppermute | solution.py:61
  58.4 2.4 %collective-permute-done.7.refs_6_ = bf16[512,256]{1,0:T(8,128)(2,1)S(1)} collective-permute-done((bf16[512,256]{1,0:T(8,128)(2,1)S(1)}, bf16[512,256]{1,0:T(8,128)(2,1)S(1)}, u32[]{:S(2)}, u32[]{:S(2)}) %collective-permute-start.7) | collective-permute-done | bytes 262176 | tf_op jit(solution)/shard_map/ppermute | solution.py:61
  60.8 4.9 %collective-permute-done.3.refs_1_ = bf16[4112,128]{1,0:T(8,128)(2,1)} collective-permute-done((bf16[4112,128]{1,0:T(8,128)(2,1)}, bf16[4112,128]{1,0:T(8,128)(2,1)}, u32[]{:S(2)}, u32[]{:S(2)}) %collective-permute-start.3) | collective-permute-done | bytes 1052704 | tf_op jit(solution)/shard_map/ppermute | solution.py:61
  65.7 4.1 %collective-permute-done.5.refs_3_ = bf16[4112,128]{1,0:T(8,128)(2,1)} collective-permute-done((bf16[4112,128]{1,0:T(8,128)(2,1)}, bf16[4112,128]{1,0:T(8,128)(2,1)}, u32[]{:S(2)}, u32[]{:S(2)}) %collective-permute-start.5) | collective-permute-done | bytes 1052704 | tf_op jit(solution)/shard_map/ppermute | solution.py:61
  73.1 2.9 %shard_map.108 = (f32[1024,128]{1,0:T(8,128)S(1)}, bf16[1024,128]{1,0:T(8,128)(2,1)S(1)}, bf16[1024,128]{1,0:T(8,128)(2,1)S(1)}, bf16[1024,128]{1,0:T(8,128)(2,1)S(1)}, bf16[4096,128]{1,0:T(8,128)(2,1)S(1)}) custom-call(s32[512]{0:T(512)S(1)} %maximum_convert_fusion.codes, bf16[4112,128]{1,0:T(8,128)(2,1)S(1)} %copy-done.2, ...), custom_call_target="tpu_custom_call" | custom-call | flops 6000000000 | bytes 1000000 | tf_op jit(solution)/shard_map/pallas_call | solution.py:361
  78.6 1.6 collective-permute-done.9.refs_8_
  81.3 2.9 %shard_map.109 = (f32[512,256]{1,0:T(8,128)S(1)}, bf16[512,256]{1,0:T(8,128)(2,1)S(1)}, bf16[512,256]{1,0:T(8,128)(2,1)S(1)}, f32[512,256]{1,0:T(8,128)S(1)}) custom-call(s32[512]{0:T(512)S(1)} %maximum_convert_fusion.codes, bf16[4112,128]{1,0:T(8,128)(2,1)S(1)} %copy-done.3, bf16[4112,128]{1,0:T(8,128)(2,1)} %collective-permute-done.3.refs_1_, ...), custom_call_target="tpu_custom_call" | custom-call | flops 6000000000 | bytes 1000000 | tf_op jit(solution)/shard_map/pallas_call | solution.py:312
  84.7 3.3 %collective-permute-start.15 = (bf16[512,256]{1,0:T(8,128)(2,1)S(1)}, bf16[512,256]{1,0:T(8,128)(2,1)S(1)}, u32[]{:S(2)}, u32[]{:S(2)}) collective-permute-start(bf16[512,256]{1,0:T(8,128)(2,1)S(1)} %get-tuple-element.107), channel_id=1, source_target_pairs={{0,2},{1,7},{2,4},{3,1},{4,6},{5,3},{6,0},{7,5},{8,10},{9,15},{10,... | collective-permute-start | bytes 786440 | tf_op jit(solution)/shard_map/ppermute | solution.py:61
  88.0 4.8 %collective-permute-start.17 = (bf16[1024,128]{1,0:T(8,128)(2,1)S(1)}, bf16[1024,128]{1,0:T(8,128)(2,1)S(1)}, u32[]{:S(2)}, u32[]{:S(2)}) collective-permute-start(bf16[1024,128]{1,0:T(8,128)(2,1)S(1)} %get-tuple-element.136), channel_id=1, source_target_pairs={{0,16},{1,17},{2,18},{3,19},{4,20},{5,21},{6,22},{7,23},{8,24},{9,... | collective-permute-start | bytes 786440 | tf_op jit(solution)/shard_map/ppermute | solution.py:61
  92.8 2.7 %collective-permute-start.19 = (bf16[1024,128]{1,0:T(8,128)(2,1)S(1)}, bf16[1024,128]{1,0:T(8,128)(2,1)S(1)}, u32[]{:S(2)}, u32[]{:S(2)}) collective-permute-start(bf16[1024,128]{1,0:T(8,128)(2,1)S(1)} %get-tuple-element.138), channel_id=1, source_target_pairs={{0,8},{1,25},{2,10},{3,27},{4,12},{5,29},{6,14},{7,31},{8,16},{9,1... | collective-permute-start | bytes 786440 | tf_op jit(solution)/shard_map/ppermute | solution.py:61
  96.6 3.0 %collective-permute-done.17 = bf16[1024,128]{1,0:T(8,128)(2,1)S(1)} collective-permute-done((bf16[1024,128]{1,0:T(8,128)(2,1)S(1)}, bf16[1024,128]{1,0:T(8,128)(2,1)S(1)}, u32[]{:S(2)}, u32[]{:S(2)}) %collective-permute-start.17) | collective-permute-done | bytes 262176 | tf_op jit(solution)/shard_map/ppermute | solution.py:61
  99.6 5.7 %collective-permute-done.18 = bf16[1024,128]{1,0:T(8,128)(2,1)S(1)} collective-permute-done((bf16[1024,128]{1,0:T(8,128)(2,1)S(1)}, bf16[1024,128]{1,0:T(8,128)(2,1)S(1)}, u32[]{:S(2)}, u32[]{:S(2)}) %collective-permute-start.18) | collective-permute-done | bytes 262176 | tf_op jit(solution)/shard_map/ppermute | solution.py:61
  109.4 1.9 %collective-permute-done.20.refs_5_ = bf16[512,256]{1,0:T(8,128)(2,1)} collective-permute-done((bf16[512,256]{1,0:T(8,128)(2,1)S(1)}, bf16[512,256]{1,0:T(8,128)(2,1)}, u32[]{:S(2)}, u32[]{:S(2)}) %collective-permute-start.20) | collective-permute-done | bytes 262176 | tf_op jit(solution)/shard_map/ppermute | solution.py:61
  111.3 2.3 %collective-permute-start.21 = (bf16[512,256]{1,0:T(8,128)(2,1)}, bf16[512,256]{1,0:T(8,128)(2,1)}, u32[]{:S(2)}, u32[]{:S(2)}) collective-permute-start(bf16[512,256]{1,0:T(8,128)(2,1)} %collective-permute-done.20.refs_5_), channel_id=1, source_target_pairs={{0,8},{1,25},{2,10},{3,27},{4,12},{5,29},{6,14},{7,31},{8,16},{9,1... | collective-permute-start | bytes 786440 | tf_op jit(solution)/shard_map/ppermute | solution.py:61
  113.6 4.1 %collective-permute-done.28.refs_6_ = bf16[1024,128]{1,0:T(8,128)(2,1)S(1)} collective-permute-done((bf16[1024,128]{1,0:T(8,128)(2,1)S(1)}, bf16[1024,128]{1,0:T(8,128)(2,1)S(1)}, u32[]{:S(2)}, u32[]{:S(2)}) %collective-permute-start.28) | collective-permute-done | bytes 262176 | tf_op jit(solution)/shard_map/ppermute | solution.py:61
  117.8 5.2 %collective-permute-done.29.refs_7_ = bf16[1024,128]{1,0:T(8,128)(2,1)S(1)} collective-permute-done((bf16[1024,128]{1,0:T(8,128)(2,1)S(1)}, bf16[1024,128]{1,0:T(8,128)(2,1)S(1)}, u32[]{:S(2)}, u32[]{:S(2)}) %collective-permute-start.29) | collective-permute-done | bytes 262176 | tf_op jit(solution)/shard_map/ppermute | solution.py:61
  123.0 2.9 %shard_map.110 = (f32[1024,128]{1,0:T(8,128)S(1)}, bf16[1024,128]{1,0:T(8,128)(2,1)S(1)}, bf16[1024,128]{1,0:T(8,128)(2,1)S(1)}, bf16[1024,128]{1,0:T(8,128)(2,1)S(1)}, bf16[4096,128]{1,0:T(8,128)(2,1)S(1)}) custom-call(s32[512]{0:T(512)S(1)} %maximum_convert_fusion.codes, bf16[4112,128]{1,0:T(8,128)(2,1)S(1)} %copy-done.3, ...), custom_call_target="tpu_custom_call" | custom-call | flops 6000000000 | bytes 1000000 | tf_op jit(solution)/shard_map/pallas_call | solution.py:361
  125.9 1.7 %collective-permute-start.30 = (bf16[4096,128]{1,0:T(8,128)(2,1)S(1)}, bf16[4096,128]{1,0:T(8,128)(2,1)}, u32[]{:S(2)}, u32[]{:S(2)}) collective-permute-start(bf16[4096,128]{1,0:T(8,128)(2,1)S(1)} %get-tuple-element.115), channel_id=1, source_target_pairs={{0,1},{1,0},{2,3},{3,2},{4,5},{5,4},{6,7},{7,6},{8,9},{9,8},{10,11... | collective-permute-start | bytes 3145736 | tf_op jit(solution)/shard_map/ppermute | solution.py:61
  131.6 1.7 %collective-permute-start.34 = (bf16[1024,128]{1,0:T(8,128)(2,1)S(1)}, bf16[1024,128]{1,0:T(8,128)(2,1)S(1)}, u32[]{:S(2)}, u32[]{:S(2)}) collective-permute-start(bf16[1024,128]{1,0:T(8,128)(2,1)S(1)} %get-tuple-element.132), channel_id=1, source_target_pairs={{0,16},{1,17},{2,18},{3,19},{4,20},{5,21},{6,22},{7,23},{8,24},{9,... | collective-permute-start | bytes 786440 | tf_op jit(solution)/shard_map/ppermute | solution.py:61
  133.4 2.7 %collective-permute-start.36 = (bf16[1024,128]{1,0:T(8,128)(2,1)S(1)}, bf16[1024,128]{1,0:T(8,128)(2,1)S(1)}, u32[]{:S(2)}, u32[]{:S(2)}) collective-permute-start(bf16[1024,128]{1,0:T(8,128)(2,1)S(1)} %get-tuple-element.134), channel_id=1, source_target_pairs={{0,8},{1,25},{2,10},{3,27},{4,12},{5,29},{6,14},{7,31},{8,16},{9,1... | collective-permute-start | bytes 786440 | tf_op jit(solution)/shard_map/ppermute | solution.py:61
  136.0 3.1 %shard_map.111 = (f32[512,256]{1,0:T(8,128)S(1)}, bf16[512,256]{1,0:T(8,128)(2,1)S(1)}, bf16[512,256]{1,0:T(8,128)(2,1)S(1)}, f32[512,256]{1,0:T(8,128)S(1)}) custom-call(s32[512]{0:T(512)S(1)} %maximum_convert_fusion.codes, bf16[4112,128]{1,0:T(8,128)(2,1)S(1)} %copy-done.4, bf16[4112,128]{1,0:T(8,128)(2,1)} %collective-permute-done.3.refs_1_, ...), custom_call_target="tpu_custom_call" | custom-call | flops 6000000000 | bytes 1000000 | tf_op jit(solution)/shard_map/pallas_call | solution.py:312
  140.8 6.3 %collective-permute-done.35 = bf16[1024,128]{1,0:T(8,128)(2,1)S(1)} collective-permute-done((bf16[1024,128]{1,0:T(8,128)(2,1)S(1)}, bf16[1024,128]{1,0:T(8,128)(2,1)S(1)}, u32[]{:S(2)}, u32[]{:S(2)}) %collective-permute-start.35) | collective-permute-done | bytes 262176 | tf_op jit(solution)/shard_map/ppermute | solution.py:61
  148.7 7.7 %all-to-all-start.1 = ((bf16[128,4,256]{2,1,0:T(4,128)(2,1)}), bf16[128,4,256]{2,1,0:T(4,128)(2,1)S(1)}, u32[]{:S(2)}, u32[]{:S(2)}) async-start(bf16[128,4,256]{2,1,0:T(4,128)(2,1)} %reshape.58), calls=%async_computation.1 | async-start | bytes 524288 | tf_op jit(solution)/shard_map/all_to_all | solution.py:67
  157.2 2.6 %collective-permute-start.33 = (bf16[512,256]{1,0:T(8,128)(2,1)}, bf16[512,256]{1,0:T(8,128)(2,1)S(1)}, u32[]{:S(2)}, u32[]{:S(2)}) collective-permute-start(bf16[512,256]{1,0:T(8,128)(2,1)} %add_convert_fusion), channel_id=1, source_target_pairs={{0,2},{1,7},{2,4},{3,1},{4,6},{5,3},{6,0},{7,5},{8,10},{9,15},{10,... | collective-permute-start | bytes 786440 | tf_op jit(solution)/shard_map/ppermute | solution.py:61
  160.0 7.5 %all-to-all-done.1 = bf16[128,4,256]{2,1,0:T(4,128)(2,1)S(1)} async-done(((bf16[128,4,256]{2,1,0:T(4,128)(2,1)}), bf16[128,4,256]{2,1,0:T(4,128)(2,1)S(1)}, u32[]{:S(2)}, u32[]{:S(2)}) %all-to-all-start.1) | async-done | bytes 262176 | tf_op jit(solution)/shard_map/all_to_all | solution.py:67
  (94 shorter events, 35.7 us)
Async XLA Ops:
  4.2 16.5 %collective-permute-start = (bf16[1280,128]{1,0:T(8,128)(2,1)}, bf16[1280,128]{1,0:T(8,128)(2,1)S(1)}, u32[]{:S(2)}, u32[]{:S(2)}) collective-permute-start(bf16[1280,128]{1,0:T(8,128)(2,1)} %get-tuple-element.68), channel_id=1, source_target_pairs={{0,2},{1,7},{2,4},{3,1},{4,6},{5,3},{6,0},{7,5},{8,10},{9,15},{10,... | collective-permute-start | bytes 983048 | tf_op jit(solution)/shard_map/ppermute | solution.py:61
  7.8 16.2 %collective-permute-start.1 = (bf16[1280,128]{1,0:T(8,128)(2,1)}, bf16[1280,128]{1,0:T(8,128)(2,1)S(1)}, u32[]{:S(2)}, u32[]{:S(2)}) collective-permute-start(bf16[1280,128]{1,0:T(8,128)(2,1)} %get-tuple-element.69), channel_id=1, source_target_pairs={{0,4},{1,5},{2,6},{3,7},{4,0},{5,1},{6,2},{7,3},{8,12},{9,13},{10,... | collective-permute-start | bytes 983048 | tf_op jit(solution)/shard_map/ppermute | solution.py:61
  8.1 15.9 %collective-permute-start.2 = (bf16[1280,128]{1,0:T(8,128)(2,1)}, bf16[1280,128]{1,0:T(8,128)(2,1)S(1)}, u32[]{:S(2)}, u32[]{:S(2)}) collective-permute-start(bf16[1280,128]{1,0:T(8,128)(2,1)} %get-tuple-element.70), channel_id=1, source_target_pairs={{0,6},{1,3},{2,0},{3,5},{4,2},{5,7},{6,4},{7,1},{8,14},{9,11},{10,... | collective-permute-start | bytes 983048 | tf_op jit(solution)/shard_map/ppermute | solution.py:61
  20.7 45.0 %collective-permute-start.3 = (bf16[4112,128]{1,0:T(8,128)(2,1)}, bf16[4112,128]{1,0:T(8,128)(2,1)}, u32[]{:S(2)}, u32[]{:S(2)}) collective-permute-start(bf16[4112,128]{1,0:T(8,128)(2,1)} %get-tuple-element.74), channel_id=1, source_target_pairs={{0,2},{1,7},{2,4},{3,1},{4,6},{5,3},{6,0},{7,5},{8,10},{9,15},{10,... | collective-permute-start | bytes 3158024 | tf_op jit(solution)/shard_map/ppermute | solution.py:61
  24.0 41.6 %collective-permute-start.4 = (bf16[4112,128]{1,0:T(8,128)(2,1)}, bf16[4112,128]{1,0:T(8,128)(2,1)}, u32[]{:S(2)}, u32[]{:S(2)}) collective-permute-start(bf16[4112,128]{1,0:T(8,128)(2,1)} %get-tuple-element.76), channel_id=1, source_target_pairs={{0,4},{1,5},{2,6},{3,7},{4,0},{5,1},{6,2},{7,3},{8,12},{9,13},{10,... | collective-permute-start | bytes 3158024 | tf_op jit(solution)/shard_map/ppermute | solution.py:61
  25.8 44.0 %collective-permute-start.5 = (bf16[4112,128]{1,0:T(8,128)(2,1)}, bf16[4112,128]{1,0:T(8,128)(2,1)}, u32[]{:S(2)}, u32[]{:S(2)}) collective-permute-start(bf16[4112,128]{1,0:T(8,128)(2,1)} %get-tuple-element.78), channel_id=1, source_target_pairs={{0,6},{1,3},{2,0},{3,5},{4,2},{5,7},{6,4},{7,1},{8,14},{9,11},{10,... | collective-permute-start | bytes 3158024 | tf_op jit(solution)/shard_map/ppermute | solution.py:61
  27.6 19.6 %all-to-all-start = ((bf16[32,16,256]{2,1,0:T(8,128)(2,1)}), bf16[32,16,256]{2,1,0:T(8,128)(2,1)S(1)}, u32[]{:S(2)}, u32[]{:S(2)}) async-start(bf16[32,16,256]{2,1,0:T(8,128)(2,1)} %bitcast.7), calls=%async_computation | async-start | bytes 524288 | tf_op jit(solution)/shard_map/all_to_all | solution.py:78
  48.0 7.2 %collective-permute-start.6 = (bf16[512,256]{1,0:T(8,128)(2,1)S(1)}, bf16[512,256]{1,0:T(8,128)(2,1)S(1)}, u32[]{:S(2)}, u32[]{:S(2)}) collective-permute-start(bf16[512,256]{1,0:T(8,128)(2,1)S(1)} %shard_map.106.refs_4_), channel_id=1, source_target_pairs={{0,8},{1,25},{2,10},{3,27},{4,12},{5,29},{6,14},{7,31},{8,16},{9,1... | collective-permute-start | bytes 786440 | tf_op jit(solution)/shard_map/ppermute | solution.py:61
  49.2 9.2 %collective-permute-start.8 = (bf16[512,256]{1,0:T(8,128)(2,1)S(1)}, bf16[512,256]{1,0:T(8,128)(2,1)S(1)}, u32[]{:S(2)}, u32[]{:S(2)}) collective-permute-start(bf16[512,256]{1,0:T(8,128)(2,1)S(1)} %shard_map.106.refs_4_), channel_id=1, source_target_pairs={{0,24},{1,9},{2,26},{3,11},{4,28},{5,13},{6,30},{7,15},{8,0},{9,17... | collective-permute-start | bytes 786440 | tf_op jit(solution)/shard_map/ppermute | solution.py:61
  55.2 5.6 %collective-permute-start.7 = (bf16[512,256]{1,0:T(8,128)(2,1)S(1)}, bf16[512,256]{1,0:T(8,128)(2,1)S(1)}, u32[]{:S(2)}, u32[]{:S(2)}) collective-permute-start(bf16[512,256]{1,0:T(8,128)(2,1)S(1)} %collective-permute-done.6.refs_5_), channel_id=1, source_target_pairs={{0,8},{1,25},{2,10},{3,27},{4,12},{5,29},{6,14},{7,31},{8,16},{9,1... | collective-permute-start | bytes 786440 | tf_op jit(solution)/shard_map/ppermute | solution.py:61
  76.0 8.2 %collective-permute-start.13 = (bf16[4096,128]{1,0:T(8,128)(2,1)S(1)}, bf16[4096,128]{1,0:T(8,128)(2,1)S(1)}, u32[]{:S(2)}, u32[]{:S(2)}) collective-permute-start(bf16[4096,128]{1,0:T(8,128)(2,1)S(1)} %get-tuple-element.100), channel_id=1, source_target_pairs={{0,1},{1,0},{2,3},{3,2},{4,5},{5,4},{6,7},{7,6},{8,9},{9,8},{10,11... | collective-permute-start | bytes 3145736 | tf_op jit(solution)/shard_map/ppermute | solution.py:61
  84.5 11.0 %collective-permute-start.14 = (bf16[512,256]{1,0:T(8,128)(2,1)S(1)}, bf16[512,256]{1,0:T(8,128)(2,1)S(1)}, u32[]{:S(2)}, u32[]{:S(2)}) collective-permute-start(bf16[512,256]{1,0:T(8,128)(2,1)S(1)} %get-tuple-element.105), channel_id=1, source_target_pairs={{0,6},{1,3},{2,0},{3,5},{4,2},{5,7},{6,4},{7,1},{8,14},{9,11},{10,... | collective-permute-start | bytes 786440 | tf_op jit(solution)/shard_map/ppermute | solution.py:61
  84.7 10.8 %collective-permute-start.15 = (bf16[512,256]{1,0:T(8,128)(2,1)S(1)}, bf16[512,256]{1,0:T(8,128)(2,1)S(1)}, u32[]{:S(2)}, u32[]{:S(2)}) collective-permute-start(bf16[512,256]{1,0:T(8,128)(2,1)S(1)} %get-tuple-element.107), channel_id=1, source_target_pairs={{0,2},{1,7},{2,4},{3,1},{4,6},{5,3},{6,0},{7,5},{8,10},{9,15},{10,... | collective-permute-start | bytes 786440 | tf_op jit(solution)/shard_map/ppermute | solution.py:61
  88.0 11.6 %collective-permute-start.17 = (bf16[1024,128]{1,0:T(8,128)(2,1)S(1)}, bf16[1024,128]{1,0:T(8,128)(2,1)S(1)}, u32[]{:S(2)}, u32[]{:S(2)}) collective-permute-start(bf16[1024,128]{1,0:T(8,128)(2,1)S(1)} %get-tuple-element.136), channel_id=1, source_target_pairs={{0,16},{1,17},{2,18},{3,19},{4,20},{5,21},{6,22},{7,23},{8,24},{9,... | collective-permute-start | bytes 786440 | tf_op jit(solution)/shard_map/ppermute | solution.py:61
  92.8 12.4 %collective-permute-start.18 = (bf16[1024,128]{1,0:T(8,128)(2,1)S(1)}, bf16[1024,128]{1,0:T(8,128)(2,1)S(1)}, u32[]{:S(2)}, u32[]{:S(2)}) collective-permute-start(bf16[1024,128]{1,0:T(8,128)(2,1)S(1)} %get-tuple-element.137), channel_id=1, source_target_pairs={{0,24},{1,9},{2,26},{3,11},{4,28},{5,13},{6,30},{7,15},{8,0},{9,17... | collective-permute-start | bytes 786440 | tf_op jit(solution)/shard_map/ppermute | solution.py:61
  92.8 12.4 %collective-permute-start.19 = (bf16[1024,128]{1,0:T(8,128)(2,1)S(1)}, bf16[1024,128]{1,0:T(8,128)(2,1)S(1)}, u32[]{:S(2)}, u32[]{:S(2)}) collective-permute-start(bf16[1024,128]{1,0:T(8,128)(2,1)S(1)} %get-tuple-element.138), channel_id=1, source_target_pairs={{0,8},{1,25},{2,10},{3,27},{4,12},{5,29},{6,14},{7,31},{8,16},{9,1... | collective-permute-start | bytes 786440 | tf_op jit(solution)/shard_map/ppermute | solution.py:61
  95.6 9.9 %collective-permute-start.16 = (bf16[512,256]{1,0:T(8,128)(2,1)S(1)}, bf16[512,256]{1,0:T(8,128)(2,1)S(1)}, u32[]{:S(2)}, u32[]{:S(2)}) collective-permute-start(bf16[512,256]{1,0:T(8,128)(2,1)S(1)} %add_convert_fusion.2), channel_id=1, source_target_pairs={{0,2},{1,7},{2,4},{3,1},{4,6},{5,3},{6,0},{7,5},{8,10},{9,15},{10,... | collective-permute-start | bytes 786440 | tf_op jit(solution)/shard_map/ppermute | solution.py:61
  105.6 5.7 %collective-permute-start.20 = (bf16[512,256]{1,0:T(8,128)(2,1)S(1)}, bf16[512,256]{1,0:T(8,128)(2,1)}, u32[]{:S(2)}, u32[]{:S(2)}) collective-permute-start(bf16[512,256]{1,0:T(8,128)(2,1)S(1)} %add_convert_fusion.1.refs_4_), channel_id=1, source_target_pairs={{0,8},{1,25},{2,10},{3,27},{4,12},{5,29},{6,14},{7,31},{8,16},{9,1... | collective-permute-start | bytes 786440 | tf_op jit(solution)/shard_map/ppermute | solution.py:61
  106.9 6.7 %collective-permute-start.27 = (bf16[1024,128]{1,0:T(8,128)(2,1)S(1)}, bf16[1024,128]{1,0:T(8,128)(2,1)S(1)}, u32[]{:S(2)}, u32[]{:S(2)}) collective-permute-start(bf16[1024,128]{1,0:T(8,128)(2,1)S(1)} %fusion.1.refs_4_), channel_id=1, source_target_pairs={{0,2},{1,7},{2,4},{3,1},{4,6},{5,3},{6,0},{7,5},{8,10},{9,15},{10,... | collective-permute-start | bytes 786440 | tf_op jit(solution)/shard_map/ppermute | solution.py:61
  108.0 9.7 %collective-permute-start.28 = (bf16[1024,128]{1,0:T(8,128)(2,1)S(1)}, bf16[1024,128]{1,0:T(8,128)(2,1)S(1)}, u32[]{:S(2)}, u32[]{:S(2)}) collective-permute-start(bf16[1024,128]{1,0:T(8,128)(2,1)S(1)} %fusion.1.refs_4_), channel_id=1, source_target_pairs={{0,4},{1,5},{2,6},{3,7},{4,0},{5,1},{6,2},{7,3},{8,12},{9,13},{10,... | collective-permute-start | bytes 786440 | tf_op jit(solution)/shard_map/ppermute | solution.py:61
  108.0 15.0 %collective-permute-start.29 = (bf16[1024,128]{1,0:T(8,128)(2,1)S(1)}, bf16[1024,128]{1,0:T(8,128)(2,1)S(1)}, u32[]{:S(2)}, u32[]{:S(2)}) collective-permute-start(bf16[1024,128]{1,0:T(8,128)(2,1)S(1)} %fusion.1.refs_4_), channel_id=1, source_target_pairs={{0,6},{1,3},{2,0},{3,5},{4,2},{5,7},{6,4},{7,1},{8,14},{9,11},{10,... | collective-permute-start | bytes 786440 | tf_op jit(solution)/shard_map/ppermute | solution.py:61
  108.8 14.2 %collective-permute-start.22 = (bf16[512,256]{1,0:T(8,128)(2,1)S(1)}, bf16[512,256]{1,0:T(8,128)(2,1)}, u32[]{:S(2)}, u32[]{:S(2)}) collective-permute-start(bf16[512,256]{1,0:T(8,128)(2,1)S(1)} %add_convert_fusion.1.refs_4_), channel_id=1, source_target_pairs={{0,24},{1,9},{2,26},{3,11},{4,28},{5,13},{6,30},{7,15},{8,0},{9,17... | collective-permute-start | bytes 786440 | tf_op jit(solution)/shard_map/ppermute | solution.py:61
  111.3 11.7 %collective-permute-start.21 = (bf16[512,256]{1,0:T(8,128)(2,1)}, bf16[512,256]{1,0:T(8,128)(2,1)}, u32[]{:S(2)}, u32[]{:S(2)}) collective-permute-start(bf16[512,256]{1,0:T(8,128)(2,1)} %collective-permute-done.20.refs_5_), channel_id=1, source_target_pairs={{0,8},{1,25},{2,10},{3,27},{4,12},{5,29},{6,14},{7,31},{8,16},{9,1... | collective-permute-start | bytes 786440 | tf_op jit(solution)/shard_map/ppermute | solution.py:61
  125.9 4.1 %collective-permute-start.30 = (bf16[4096,128]{1,0:T(8,128)(2,1)S(1)}, bf16[4096,128]{1,0:T(8,128)(2,1)}, u32[]{:S(2)}, u32[]{:S(2)}) collective-permute-start(bf16[4096,128]{1,0:T(8,128)(2,1)S(1)} %get-tuple-element.115), channel_id=1, source_target_pairs={{0,1},{1,0},{2,3},{3,2},{4,5},{5,4},{6,7},{7,6},{8,9},{9,8},{10,11... | collective-permute-start | bytes 3145736 | tf_op jit(solution)/shard_map/ppermute | solution.py:61
  127.8 3.8 %collective-permute-start.23 = (bf16[512,256]{1,0:T(8,128)(2,1)S(1)}, bf16[512,256]{1,0:T(8,128)(2,1)S(1)}, u32[]{:S(2)}, u32[]{:S(2)}) collective-permute-start(bf16[512,256]{1,0:T(8,128)(2,1)S(1)} %add_convert_fusion.1.refs_4_), channel_id=1, source_target_pairs={{0,1},{1,0},{2,3},{3,2},{4,5},{5,4},{6,7},{7,6},{8,9},{9,8},{10,11... | collective-permute-start | bytes 786440 | tf_op jit(solution)/shard_map/ppermute | solution.py:61
  131.6 9.1 %collective-permute-start.34 = (bf16[1024,128]{1,0:T(8,128)(2,1)S(1)}, bf16[1024,128]{1,0:T(8,128)(2,1)S(1)}, u32[]{:S(2)}, u32[]{:S(2)}) collective-permute-start(bf16[1024,128]{1,0:T(8,128)(2,1)S(1)} %get-tuple-element.132), channel_id=1, source_target_pairs={{0,16},{1,17},{2,18},{3,19},{4,20},{5,21},{6,22},{7,23},{8,24},{9,... | collective-permute-start | bytes 786440 | tf_op jit(solution)/shard_map/ppermute | solution.py:61
  133.4 13.7 %collective-permute-start.35 = (bf16[1024,128]{1,0:T(8,128)(2,1)S(1)}, bf16[1024,128]{1,0:T(8,128)(2,1)S(1)}, u32[]{:S(2)}, u32[]{:S(2)}) collective-permute-start(bf16[1024,128]{1,0:T(8,128)(2,1)S(1)} %get-tuple-element.133), channel_id=1, source_target_pairs={{0,24},{1,9},{2,26},{3,11},{4,28},{5,13},{6,30},{7,15},{8,0},{9,17... | collective-permute-start | bytes 786440 | tf_op jit(solution)/shard_map/ppermute | solution.py:61
  133.4 13.7 %collective-permute-start.36 = (bf16[1024,128]{1,0:T(8,128)(2,1)S(1)}, bf16[1024,128]{1,0:T(8,128)(2,1)S(1)}, u32[]{:S(2)}, u32[]{:S(2)}) collective-permute-start(bf16[1024,128]{1,0:T(8,128)(2,1)S(1)} %get-tuple-element.134), channel_id=1, source_target_pairs={{0,8},{1,25},{2,10},{3,27},{4,12},{5,29},{6,14},{7,31},{8,16},{9,1... | collective-permute-start | bytes 786440 | tf_op jit(solution)/shard_map/ppermute | solution.py:61
  139.2 17.2 %collective-permute-start.32 = (bf16[512,256]{1,0:T(8,128)(2,1)S(1)}, bf16[512,256]{1,0:T(8,128)(2,1)S(1)}, u32[]{:S(2)}, u32[]{:S(2)}) collective-permute-start(bf16[512,256]{1,0:T(8,128)(2,1)S(1)} %get-tuple-element.130), channel_id=1, source_target_pairs={{0,2},{1,7},{2,4},{3,1},{4,6},{5,3},{6,0},{7,5},{8,10},{9,15},{10,... | collective-permute-start | bytes 786440 | tf_op jit(solution)/shard_map/ppermute | solution.py:61
  139.4 29.6 %collective-permute-start.31 = (bf16[512,256]{1,0:T(8,128)(2,1)S(1)}, bf16[512,256]{1,0:T(8,128)(2,1)S(1)}, u32[]{:S(2)}, u32[]{:S(2)}) collective-permute-start(bf16[512,256]{1,0:T(8,128)(2,1)S(1)} %get-tuple-element.128), channel_id=1, source_target_pairs={{0,6},{1,3},{2,0},{3,5},{4,2},{5,7},{6,4},{7,1},{8,14},{9,11},{10,... | collective-permute-start | bytes 786440 | tf_op jit(solution)/shard_map/ppermute | solution.py:61
  148.7 18.8 %all-to-all-start.1 = ((bf16[128,4,256]{2,1,0:T(4,128)(2,1)}), bf16[128,4,256]{2,1,0:T(4,128)(2,1)S(1)}, u32[]{:S(2)}, u32[]{:S(2)}) async-start(bf16[128,4,256]{2,1,0:T(4,128)(2,1)} %reshape.58), calls=%async_computation.1 | async-start | bytes 524288 | tf_op jit(solution)/shard_map/all_to_all | solution.py:67
  157.2 11.8 %collective-permute-start.33 = (bf16[512,256]{1,0:T(8,128)(2,1)}, bf16[512,256]{1,0:T(8,128)(2,1)S(1)}, u32[]{:S(2)}, u32[]{:S(2)}) collective-permute-start(bf16[512,256]{1,0:T(8,128)(2,1)} %add_convert_fusion), channel_id=1, source_target_pairs={{0,2},{1,7},{2,4},{3,1},{4,6},{5,3},{6,0},{7,5},{8,10},{9,15},{10,... | collective-permute-start | bytes 786440 | tf_op jit(solution)/shard_map/ppermute | solution.py:61
  (15 other events, 77.9 us)
